TPU v7x, 32 devices: a whole 2x2x4 slice. The times are simulated.
32 devices in a mesh: tm: 4 (over y, core), vert: 8 (over z, x).
Axes of the slice: x: 2, y: 2, z: 4, core: 2. Of those that a mesh axis runs over, the one named last changes fastest.
Arguments:
- features: bfloat16 [4, 4096, 1024], P('tm', 'vert'), may hold values from -6 to 6
- graph_weight: bfloat16 [1024, 1024], P('vert'), may hold values from -0.1875 to 0.1875
- head_weight: bfloat16 [16, 192, 1024], P('tm'), may hold values from -16 to 16
- send_rows: int32 [4, 8, 8, 16], P('tm', 'vert'), may hold values from 0 to 511, as said below
- send_count: int32 [4, 8, 8], P('tm', 'vert'), may hold values from 0 to 16, as said below
- block_index: int32 [4, 32, 3], P('tm', 'vert'), may hold values from 0 to 4, as said below
- block_values: bfloat16 [4, 4096, 3, 128], P('tm', 'vert'), may hold values from -0.3125 to 0.3125
Outputs:
- combined: bfloat16 [4, 4096, 1024], P('tm', 'vert')
Inputs may be any that keep to these rules, and one draw needn't show every extreme that they name: send_rows[s, p, q] holds 16 distinct local rows of partition p; slots from send_count[s, p, q] on are ignored. send_count[s, p, p] is 0; in every snapshot some pairs reach 16. `block_index`: the 3 entries of a block row are distinct; column blocks below 4 are the partition's own rows, the others its boundary rows in the order of columns.
All inputs are finite; a program needn't handle non-finite values.
Results may differ from a plain program's by a relative error of at most 0.0075.
Values may be sent and summed in bfloat16 or wider, within the bound.
No kernel may reach another device: no remote copies, remote signals or barrier semaphores. Data moves between devices by JAX's collectives and lax.ppermute only.
A program may use at most 64 MiB of HBM per device.

v0:
```python
import jax
import jax.numpy as jnp
from jax import lax
from jax.sharding import PartitionSpec as P


def attend_heads(regrouped, head_piece):
    head_size = head_piece.shape[1] // 3
    count_heads = head_piece.shape[0]
    snapshots = regrouped.shape[0]
    packed = jnp.einsum("tvd,hcd->tvhc", regrouped, head_piece, preferred_element_type=jnp.float32)
    queries = packed[..., :head_size].astype(jnp.bfloat16)
    keys_part = packed[..., head_size : 2 * head_size].astype(jnp.bfloat16)
    values = packed[..., 2 * head_size :].astype(jnp.bfloat16)
    scores = jnp.einsum(
        "tvhc,svhc->vhts", queries, keys_part, preferred_element_type=jnp.float32
    ) * head_size ** (-0.5)
    causal = jnp.arange(snapshots)[:, None] >= jnp.arange(snapshots)[None, :]
    scores = jnp.where(causal, scores, -1e30)
    row_max = jnp.max(scores, axis=-1, keepdims=True)
    exponent = jnp.where(causal, jnp.exp(scores - row_max), 0.0)
    attention = (exponent / jnp.sum(exponent, axis=-1, keepdims=True)).astype(jnp.bfloat16)
    attended = jnp.einsum("vhts,svhc->tvhc", attention, values, preferred_element_type=jnp.float32)
    return attended.astype(jnp.bfloat16).reshape(
        snapshots, regrouped.shape[1], count_heads * head_size
    )


def fold_rows(left, piece):
    return jnp.dot(left, piece, preferred_element_type=jnp.float32)


def shards(features, graph_weight, head_weight, send_rows, send_count, block_index, block_values):
    inputs = features[0]
    feature_width = inputs.shape[1]
    own_count = inputs.shape[0]
    rows_list = send_rows[0, 0]
    sources = rows_list.shape[0]
    most_rows = rows_list.shape[1]
    live_slots = jnp.arange(most_rows)[None, :] < send_count[0, 0][:, None]
    picked = jnp.take(inputs, rows_list.reshape(-1), axis=0).reshape(
        sources, most_rows, feature_width
    )
    picked = jnp.where(live_slots[:, :, None], picked, jnp.zeros_like(picked))
    arrived = lax.all_to_all(picked, "vert", split_axis=0, concat_axis=0, tiled=True)
    stacked = jnp.concatenate([inputs, arrived.reshape(sources * most_rows, feature_width)], axis=0)
    whole = fold_rows(stacked, lax.all_gather(graph_weight, "vert", axis=0, tiled=True)).astype(
        jnp.bfloat16
    )
    projected = whole[:own_count]
    received = whole[own_count:]
    block_size = block_values.shape[-1]
    index_list = block_index[0]
    own_blocks = index_list.shape[0]
    chosen_count = index_list.shape[1]
    columns = jnp.concatenate([projected, received], axis=0)
    columns = columns.reshape(-1, block_size, feature_width)
    chosen = jnp.take(columns, index_list.reshape(-1), axis=0).reshape(
        own_blocks, chosen_count, block_size, feature_width
    )
    edge_weights = block_values[0].reshape(own_blocks, block_size, chosen_count, block_size)
    summed = jnp.einsum("rikj,rkjd->rid", edge_weights, chosen, preferred_element_type=jnp.float32)
    pre_act = projected.astype(jnp.float32) + summed.reshape(own_count, feature_width)
    hidden = jax.nn.relu(pre_act).astype(jnp.bfloat16)
    regrouped = lax.all_to_all(hidden[None], "tm", split_axis=1, concat_axis=0, tiled=True)
    attended = attend_heads(regrouped, lax.all_gather(head_weight, "tm", axis=0, tiled=True))
    returned = lax.all_to_all(attended, "tm", split_axis=0, concat_axis=1, tiled=True)
    combined = (hidden.astype(jnp.float32) + returned[0].astype(jnp.float32)).astype(jnp.bfloat16)
    return combined[None]


def solution(mesh):
    return jax.shard_map(
        shards,
        mesh=mesh,
        in_specs=(
            P("tm", "vert", None),
            P("vert", None),
            P("tm", None, None),
            P("tm", "vert", None, None),
            P("tm", "vert", None),
            P("tm", "vert", None),
            P("tm", "vert", None, None),
        ),
        out_specs=P("tm", "vert", None),
        check_vma=False,
    )
```

profile of v0, /device:TPU:0, one launch (start us, length us, event | category | flops | bytes accessed | tf_op | source)
XLA Modules:
  0.0 190.8 jit_solution(4202133148746718751)
XLA Ops:
  6.5 0.0 all-gather.3.cloned.1.call-start
  6.5 0.7 all-gather.3.cloned.1.call-update
  7.3 0.0 all-gather.5.cloned.1.call-start
  7.3 0.7 all-gather.5.cloned.1.call-update
  8.0 0.0 copy-start.3
  8.0 0.8 reshape_squeeze.14
  8.8 0.0 copy-done
  8.8 0.9 gather_fusion
  9.7 0.0 copy-done.2
  9.7 0.0 copy-done.4
  9.7 0.1 iota_compare_fusion
  9.8 0.8 select_select_fusion
  10.6 7.3 %all-to-all-start = ((bf16[8,16,1024]{2,1,0:T(8,128)(2,1)}), bf16[8,16,1024]{2,1,0:T(8,128)(2,1)S(1)}, u32[]{:S(2)}, u32[]{:S(2)}) async-start(bf16[8,16,1024]{2,1,0:T(8,128)(2,1)} %select_select_fusion), calls=%async_computation | async-start | bytes 524288 | tf_op jit(solution)/shard_map/all_to_all | solution.py:45
  17.8 0.1 copy.44
  17.9 0.1 reshape_squeeze.16
  18.1 12.8 %all-to-all-done = bf16[8,16,1024]{2,1,0:T(8,128)(2,1)S(1)} async-done(((bf16[8,16,1024]{2,1,0:T(8,128)(2,1)}), bf16[8,16,1024]{2,1,0:T(8,128)(2,1)S(1)}, u32[]{:S(2)}, u32[]{:S(2)}) %all-to-all-start) | async-done | bytes 262176 | tf_op jit(solution)/shard_map/all_to_all | solution.py:45
  30.9 33.0 %all-gather.3.cloned.1.call-done = bf16[1024,1024]{1,0:T(8,128)(2,1)} async-done(((bf16[128,1024]{1,0:T(8,128)(2,1)}), bf16[1024,1024]{1,0:T(8,128)(2,1)}) %all-gather.3.cloned.1.call-update) | async-done | bytes 2097168 | tf_op jit(solution)/shard_map/all_gather | solution.py:47
  63.9 3.1 %convolution_convert_fusion = bf16[640,1024]{1,0:T(8,128)(2,1)S(1)} fusion(bf16[1024,1024]{1,0:T(8,128)(2,1)} %all-gather.3.cloned.1.call-done, bf16[128,1024]{1,0:T(8,128)(2,1)S(1)} %bitcast.69, bf16[512,1024]{1,0:T(8,128)(2,1)S(1)} %bitcast.64), kind=kOutput, calls=%fused_computation.14 | convolution fusion | flops 1345454080 | bytes 4718592 | tf_op jit(solution)/shard_map/dot_general | solution.py:30
  67.0 0.0 copy-start.5
  67.0 2.6 %gather_fusion.1 = bf16[12,128,1024]{2,1,0:T(8,128)(2,1)} fusion(bf16[5,128,1024]{2,1,0:T(8,128)(2,1)S(1)} %bitcast.59, s32[1024]{0:T(1024)S(1)} %pad_clamp_fusion), kind=kCustom, calls=%fused_computation.1 | custom fusion | bytes 6291504 | tf_op jit(solution)/shard_map/jit(_take)/gather | solution.py:58
  69.6 0.0 copy-done.5
  69.6 3.1 %fusion.2 = f32[4,1024,128,1]{1,2,3,0:T(8,128)S(1)} fusion(bf16[4,3,128,1024]{3,2,1,0:T(8,128)(2,1)} %bitcast.66, pred[4,3]{1,0:T(4,128)(4,1)S(1)} %compare_and_fusion.1, bf16[4,128,3,128]{3,1,0,2:T(8,128)(2,1)S(1)} %bitcast.71), kind=kOutput, calls=%fused_computation.4 | convolution fusion | flops 404226048 | bytes 5636108 | tf_op jit(solution)/shard_map/rikj,rkjd->rid/dot_general | solution.py:62
  72.6 0.4 fusion.9
  73.1 1.6 copy.61
  74.7 0.5 broadcast.92
  75.2 7.7 %reduce = bf16[512,1024]{1,0:T(8,128)(2,1)} reduce(bf16[512,1,1024]{2,1,0:T(2,128)(2,1)S(1)} %bitcast.62, bf16[]{:T(256)} %broadcast.92), dimensions={1}, to_apply=%bitcast.58.reduce_sub_computation | reduce | bytes 2097154
  83.0 3.8 %reshape.151 = bf16[4,2,65536]{2,1,0:T(2,128)(2,1)} reshape(bf16[512,1024]{1,0:T(8,128)(2,1)} %reduce) | data formatting | bytes 2097152
  86.7 4.4 %all-to-all-start.1 = ((bf16[4,2,65536]{2,1,0:T(2,128)(2,1)}), bf16[4,2,65536]{2,1,0:T(2,128)(2,1)}, u32[]{:S(2)}, u32[]{:S(2)}) async-start(bf16[4,2,65536]{2,1,0:T(2,128)(2,1)} %reshape.151), calls=%async_computation.1 | async-start | bytes 2097152 | tf_op jit(solution)/shard_map/all_to_all | solution.py:65
  91.2 25.9 %all-to-all-done.1 = bf16[4,2,65536]{2,1,0:T(2,128)(2,1)} async-done(((bf16[4,2,65536]{2,1,0:T(2,128)(2,1)}), bf16[4,2,65536]{2,1,0:T(2,128)(2,1)}, u32[]{:S(2)}, u32[]{:S(2)}) %all-to-all-start.1) | async-done | bytes 1048608 | tf_op jit(solution)/shard_map/all_to_all | solution.py:65
  117.0 2.6 %reshape.152 = bf16[512,1,1024]{2,1,0:T(2,128)(2,1)S(1)} reshape(bf16[4,2,65536]{2,1,0:T(2,128)(2,1)} %all-to-all-done.1) | data formatting | bytes 2097152
  119.7 1.3 copy.57
  121.0 0.5 all-gather.5.cloned.1.call-done
  121.6 5.9 %fusion.5 = bf16[4,128,16,192]{1,3,2,0:T(8,128)(2,1)S(1)} fusion(bf16[4,128,1024,1]{2,1,3,0:T(8,128)(2,1)} %bitcast.67, bf16[16,192,1024]{2,1,0:T(8,128)(2,1)} %all-gather.5.cloned.1.call-done), kind=kOutput, calls=%fused_computation.7 | convolution fusion | flops 3222798336 | bytes 10485760 | tf_op jit(solution)/shard_map/tvd,hcd->tvhc/dot_general | solution.py:11
  127.5 1.7 fusion.22
  129.2 3.3 %copy.48 = bf16[4,128,16,64]{3,0,2,1:T(4,128)(2,1)S(1)} copy(bf16[4,128,16,64]{1,3,2,0:T(8,128)(2,1)} %get-tuple-element.6) | data formatting | bytes 2097152 | tf_op jit(solution)/shard_map/slice | solution.py:12
  132.5 4.4 %copy.49 = bf16[4,128,16,64]{3,0,2,1:T(4,128)(2,1)} copy(bf16[4,128,16,64]{1,3,2,0:T(8,128)(2,1)} %get-tuple-element.5) | data formatting | bytes 2097152 | tf_op jit(solution)/shard_map/slice | solution.py:13
  137.0 5.9 %fusion.23 = f32[128,16,4,4]{2,3,1,0:T(4,128)} fusion(bf16[4,128,16,64]{3,0,2,1:T(4,128)(2,1)S(1)} %copy.48, bf16[4,128,16,64]{3,0,2,1:T(4,128)(2,1)} %copy.49), kind=kOutput, calls=%fused_computation.42 | convolution fusion | flops 4194304 | bytes 2228224 | tf_op jit(solution)/shard_map/tvhc,svhc->vhts/dot_general | solution.py:15
  142.8 3.8 %copy.50 = f32[128,16,4,4]{0,1,3,2:T(8,128)S(1)} copy(f32[128,16,4,4]{2,3,1,0:T(4,128)} %fusion.23) | data formatting | bytes 262144 | tf_op jit(solution)/shard_map/tvhc,svhc->vhts/dot_general | solution.py:15
  146.6 0.1 fusion.16
  146.7 0.1 fusion.17
  146.8 0.1 divide_convert_fusion
  146.9 4.3 %copy.52 = bf16[128,16,4,4]{3,2,1,0:T(4,128)(2,1)} copy(bf16[128,16,4,4]{0,1,3,2:T(8,128)(2,1)S(1)} %divide_convert_fusion) | data formatting | bytes 131072 | tf_op jit(solution)/shard_map/convert_element_type | solution.py:22
  151.3 2.9 %copy.51 = bf16[4,128,16,64]{3,0,2,1:T(4,128)(2,1)} copy(bf16[4,128,16,64]{1,3,2,0:T(8,128)(2,1)S(1)} %copy-done.1) | data formatting | bytes 2097152 | tf_op jit(solution)/shard_map/slice | solution.py:14
  154.2 5.9 %convert_bitcast_fusion = bf16[4,128,16,64]{3,0,2,1:T(4,128)(2,1)} fusion(bf16[4,128,16,64]{3,0,2,1:T(4,128)(2,1)} %copy.51, bf16[128,16,4,4]{3,2,1,0:T(4,128)(2,1)} %copy.52), kind=kOutput, calls=%fused_computation.13 | convolution fusion | flops 4718592 | bytes 2162688 | tf_op jit(solution)/shard_map/vhts,svhc->tvhc/dot_general | solution.py:23
  160.0 3.5 %copy.53 = bf16[4,128,16,64]{1,3,2,0:T(8,128)(2,1)S(1)} copy(bf16[4,128,16,64]{3,0,2,1:T(4,128)(2,1)} %convert_bitcast_fusion) | data formatting | bytes 2097152 | tf_op jit(solution)/shard_map/convert_element_type | solution.py:24
  163.5 17.6 %all_to_all.26 = bf16[4,128,1024]{1,2,0:T(8,128)(2,1)} all-to-all(bf16[4,128,1024]{1,2,0:T(8,128)(2,1)S(1)} %bitcast.65), channel_id=1, replica_groups=mesh['tm'=4,'vert'=8] {'tm'}, dimensions={0} | all-to-all | bytes 2097152 | tf_op jit(solution)/shard_map/all_to_all | solution.py:67
  181.1 1.5 copy.54
  182.6 1.3 fusion.10
  (12 shorter events, 0.1 us)
Async XLA Ops:
  6.5 3.1 %copy-start.2 = (s32[1,1,8,16]{3,2,1,0:T(8,128)S(1)}, s32[1,1,8,16]{3,2,1,0:T(8,128)}, u32[]{:S(2)}) copy-start(s32[1,1,8,16]{3,2,1,0:T(8,128)} %param.10) | copy-start | bytes 1540
  6.5 2.3 %copy-start = (bf16[1,512,1024]{2,1,0:T(8,128)(2,1)S(1)}, bf16[1,512,1024]{2,1,0:T(8,128)(2,1)}, u32[]{:S(2)}) copy-start(bf16[1,512,1024]{2,1,0:T(8,128)(2,1)} %param.7) | copy-start | bytes 3145732
  6.5 3.2 %copy-start.4 = (s32[1,1,8]{2,1,0:T(1,128)S(1)}, s32[1,1,8]{2,1,0:T(1,128)}, u32[]{:S(2)}) copy-start(s32[1,1,8]{2,1,0:T(1,128)} %param.11) | copy-start | bytes 100
  6.5 57.3 %all-gather.3.cloned.1.call-start = ((), (), s32[]{:S(2)}) async-start(), calls=%async_computation.3 | async-start | bytes 2359296 | tf_op jit(solution)/shard_map/all_gather | solution.py:47
  7.3 114.3 %all-gather.5.cloned.1.call-start = ((), (), s32[]{:S(2)}) async-start(), calls=%async_computation.4 | async-start | bytes 7864320 | tf_op jit(solution)/shard_map/all_gather | solution.py:66
  8.0 9.8 %copy-start.3 = (s32[1,4,3]{1,0,2:T(1,128)S(1)}, s32[1,4,3]{1,0,2:T(1,128)}, u32[]{:S(2)}) copy-start(s32[1,4,3]{1,0,2:T(1,128)} %param.12) | copy-start | bytes 148
  10.6 20.3 %all-to-all-start = ((bf16[8,16,1024]{2,1,0:T(8,128)(2,1)}), bf16[8,16,1024]{2,1,0:T(8,128)(2,1)S(1)}, u32[]{:S(2)}, u32[]{:S(2)}) async-start(bf16[8,16,1024]{2,1,0:T(8,128)(2,1)} %select_select_fusion), calls=%async_computation | async-start | bytes 524288 | tf_op jit(solution)/shard_map/all_to_all | solution.py:45
  67.0 2.6 %copy-start.5 = (bf16[1,512,3,128]{3,1,2,0:T(8,128)(2,1)S(1)}, bf16[1,512,3,128]{3,1,2,0:T(8,128)(2,1)}, u32[]{:S(2)}) copy-start(bf16[1,512,3,128]{3,1,2,0:T(8,128)(2,1)} %param.13) | copy-start | bytes 1179652
  86.7 30.3 %all-to-all-start.1 = ((bf16[4,2,65536]{2,1,0:T(2,128)(2,1)}), bf16[4,2,65536]{2,1,0:T(2,128)(2,1)}, u32[]{:S(2)}, u32[]{:S(2)}) async-start(bf16[4,2,65536]{2,1,0:T(2,128)(2,1)} %reshape.151), calls=%async_computation.1 | async-start | bytes 2097152 | tf_op jit(solution)/shard_map/all_to_all | solution.py:65
  146.6 4.7 %copy-start.1 = (bf16[4,128,16,64]{1,3,2,0:T(8,128)(2,1)S(1)}, bf16[4,128,16,64]{1,3,2,0:T(8,128)(2,1)}, u32[]{:S(2)}) copy-start(bf16[4,128,16,64]{1,3,2,0:T(8,128)(2,1)} %get-tuple-element.7) | copy-start | bytes 3145732
Sparse Core Ops, SparseCore 0:
  9.5 54.3 all-gather.2
  65.4 56.0 all-gather.4
where the time goes:
time: 192 us; the launch traced here: 191 us
  waiting for transfers between devices  73.7 us (38%)
  local copies, waits for them, and re-layouts  39.7 us (21%)
  matrix products  23.8 us (12%)
  blocking collectives  17.6 us (9%)
  between operations  13.6 us (7%)
  starting transfers between devices  11.7 us (6%)
  other arithmetic  10.7 us (6%)
    all_gather x1, waiting for transfers between devices, shards(): lax.all_gather(graph_weight, 'vert', axis=0, tiled=True)  33 us
    all_to_all x1, waiting for transfers between devices, shards(): lax.all_to_all(hidden[None], 'tm', split_axis=1, concat_axis=0, tiled=True)  25.9 us
    all_to_all x1, blocking collectives, shards(): lax.all_to_all(attended, 'tm', split_axis=0, concat_axis=1, tiled=True)  17.6 us
    all_to_all x1, waiting for transfers between devices, shards(): lax.all_to_all(picked, 'vert', split_axis=0, concat_axis=0, tiled=True)  12.8 us
    unnamed x17, local copies, waits for them, and re-layouts  8.39 us
    unnamed x1, other arithmetic  7.74 us
    all_to_all x1, starting transfers between devices, shards(): lax.all_to_all(picked, 'vert', split_axis=0, concat_axis=0, tiled=True)  7.25 us
    slice x2, local copies, waits for them, and re-layouts, attend_heads(): keys_part = packed[..., head_size:2 * head_size].astype(jnp.bfloat16)  6.19 us
  transfers between devices with their start and end apart: 4, of which 4 were waited for; matrix products, arithmetic and copies ran while one was open for 15% of the time, Pallas kernels for 0%

commit v1 on v0

v1 whole, which is shorter than its diff:
```python
import functools

import jax
import jax.numpy as jnp
from jax import lax
from jax.experimental import pallas as pl
from jax.experimental.pallas import tpu as pltpu
from jax.sharding import PartitionSpec as P

CORES = 2
ROW_BLOCKS = 4
VMEM = pl.BlockSpec(memory_space=pltpu.VMEM)
SMEM = pl.BlockSpec(memory_space=pltpu.SMEM)
MASKED = -1e30


def call(kernel, outs, ins, flops=0, scratch=(), limit=24):
    moved = sum(a.size * a.dtype.itemsize for a in (*ins, *jax.tree.leaves(outs)))
    return pl.pallas_call(
        kernel,
        out_shape=outs,
        in_specs=[SMEM if a.dtype == jnp.int32 else VMEM for a in ins],
        out_specs=jax.tree.map(lambda _: VMEM, outs),
        scratch_shapes=scratch,
        compiler_params=pltpu.CompilerParams(vmem_limit_bytes=limit * 2**20),
        cost_estimate=pl.CostEstimate(flops=flops, bytes_accessed=moved, transcendentals=0),
    )(*ins)


def mix_kernel(index_ref, own_ref, arrived_ref, edge_ref, mixed_ref, columns_ref):
    own = own_ref.shape[0]
    block_rows, chosen = index_ref.shape
    size = own // block_rows
    columns_ref[:own, :] = own_ref[...]
    columns_ref[own:, :] = arrived_ref[...]
    for b in range(block_rows):
        rows = slice(b * size, (b + 1) * size)
        total = own_ref[rows, :].astype(jnp.float32)
        for k in range(chosen):
            start = pl.multiple_of(index_ref[b, k] * size, size)
            total += jnp.dot(
                edge_ref[rows, k * size : (k + 1) * size],
                columns_ref[pl.ds(start, size), :],
                preferred_element_type=jnp.float32,
            )
        mixed_ref[rows, :] = total.astype(mixed_ref.dtype)


def relu_dot(left, right):
    total = jnp.dot(left, right, preferred_element_type=jnp.float32)
    return jnp.maximum(total, 0.0).astype(jnp.bfloat16)


def assemble_kernel(place_ref, mine_ref, other_ref, mixed_ref, weight_ref, hidden_ref):
    pieces, depth, width = mine_ref.shape
    for half, ref in enumerate((mine_ref, other_ref)):
        column = pl.multiple_of(place_ref[pieces + half] * width, width)
        for i in range(pieces):
            row = pl.multiple_of(place_ref[i] * depth, depth)
            weight_ref[pl.ds(row, depth), pl.ds(column, width)] = ref[i]
    hidden_ref[...] = relu_dot(mixed_ref[...], weight_ref[...])


def hidden_kernel(mixed_ref, weight_ref, hidden_ref):
    hidden_ref[...] = relu_dot(mixed_ref[...], weight_ref[...])


def attend_kernel(slots, pieces, head_size, flag_ref, *refs):
    hidden_refs, weight_refs = refs[:slots], refs[slots : slots + pieces]
    mine_ref, other_ref, stacked_ref = refs[slots + pieces :]
    rows = hidden_refs[0].shape[0]
    for s in range(slots):
        stacked_ref[s * rows : (s + 1) * rows, :] = hidden_refs[s][...]
    width = weight_refs[0].shape[0] // 3
    contract = (((1,), (1,)), ((), ()))
    group = lambda axis: lax.broadcasted_iota(jnp.int32, (2 * width, width), axis) % width // head_size
    spread = (group(0) == group(1)).astype(jnp.bfloat16)
    for p in range(pieces):
        weight = weight_refs[p]
        queries = lax.dot_general(
            stacked_ref[: CORES * rows, :], weight[:width, :], contract,
            preferred_element_type=jnp.float32,
        ).astype(jnp.bfloat16).astype(jnp.float32)
        both = lax.dot_general(
            stacked_ref[...], weight[width:, :], contract, preferred_element_type=jnp.float32
        ).astype(jnp.bfloat16).astype(jnp.float32)
        for t, out_ref in enumerate((mine_ref, other_ref)):
            query = queries[t * rows : (t + 1) * rows]
            products = jnp.concatenate(
                [query * both[u * rows : (u + 1) * rows, :width] for u in range(slots)], axis=0
            )
            high = products.astype(jnp.bfloat16)
            low = (products - high.astype(jnp.float32)).astype(jnp.bfloat16)
            scores = jnp.dot(
                jnp.concatenate([high, low], axis=1), spread, preferred_element_type=jnp.float32
            ) * head_size ** (-0.5)
            parts = [
                jnp.where(flag_ref[t * slots + u] > 0, scores[u * rows : (u + 1) * rows], MASKED)
                for u in range(slots)
            ]
            top = functools.reduce(jnp.maximum, parts)
            parts = [jnp.exp(part - top) for part in parts]
            scale = 1.0 / functools.reduce(jnp.add, parts)
            total = jnp.zeros_like(top)
            for u in range(slots):
                share = (parts[u] * scale).astype(jnp.bfloat16).astype(jnp.float32)
                total += share * both[u * rows : (u + 1) * rows, width:]
            out_ref[:, p * width : (p + 1) * width] = total.astype(out_ref.dtype)


def combine_kernel(blocks, pieces, place_ref, hidden_ref, *refs):
    out_ref = refs[-1]
    width = refs[0].shape[1] // pieces
    lanes = width % 128 == 0
    for r in range(blocks):
        rows = refs[r].shape[0]
        here = slice(r * rows, (r + 1) * rows)
        whole = None if lanes else hidden_ref[here, :].astype(jnp.float32)
        for half in range(CORES):
            for p in range(pieces):
                start = place_ref[half * pieces + p] * width
                attended = refs[half * blocks + r][:, p * width : (p + 1) * width]
                if lanes:
                    column = pl.ds(pl.multiple_of(start, width), width)
                    total = hidden_ref[here, column].astype(jnp.float32) + attended.astype(jnp.float32)
                    out_ref[here, column] = total.astype(out_ref.dtype)
                else:
                    shape = (width, out_ref.shape[1])
                    spot = lax.broadcasted_iota(jnp.int32, shape, 0) + start
                    spot = (spot == lax.broadcasted_iota(jnp.int32, shape, 1)).astype(jnp.bfloat16)
                    whole += jnp.dot(attended, spot, preferred_element_type=jnp.float32)
        if not lanes:
            out_ref[here, :] = whole.astype(out_ref.dtype)


def shards(sizes, features, graph_weight, head_weight, send_rows, send_count, block_index, block_values):
    steps, parts = sizes["tm"], sizes["vert"]
    chips = steps // CORES
    step, part = lax.axis_index("tm"), lax.axis_index("vert")
    core, chip = step % CORES, step // CORES
    swap_core = lambda a: lax.ppermute(a, "tm", [(i, i ^ 1) for i in range(steps)])
    swap_part = lambda a: lax.ppermute(a, "vert", [(i, i ^ 1) for i in range(parts)])
    inputs = features[0]
    own, width = inputs.shape

    rows_list = send_rows[0, 0]
    sources, most_rows = rows_list.shape
    live = jnp.arange(most_rows)[None, :] < send_count[0, 0][:, None]
    chosen = (rows_list[:, :, None] == jnp.arange(own)) & live[:, :, None]
    picked = jnp.einsum(
        "qjv,vd->qjd", chosen.astype(jnp.bfloat16), inputs, preferred_element_type=jnp.float32
    ).astype(jnp.bfloat16)
    arrived = lax.all_to_all(picked, "vert", split_axis=0, concat_axis=0, tiled=True)

    heads, head_rows, _ = head_weight.shape
    head_size = head_rows // 3
    shares = 2 if heads % 2 == 0 and parts % 2 == 0 else 1
    ordered = head_weight.reshape(shares, heads // shares, 3, head_size, width)
    ordered = ordered.transpose(0, 2, 1, 3, 4).reshape(shares, -1, width)
    share = part % shares
    sent = lax.dynamic_index_in_dim(ordered, share, 0, keepdims=False)
    weights = [ordered[i] for i in range(shares)]
    spots = [(step, i) for i in range(shares)]
    for d in range(1, chips):
        fetched = lax.ppermute(sent, "tm", [(i, (i + CORES * d) % steps) for i in range(steps)])
        weights.append(fetched)
        spots.append(((step - CORES * d) % steps, share))
        if shares == 2:
            weights.append(swap_part(fetched))
            spots.append(((step - CORES * d) % steps, 1 - share))
    place = [s * shares + i for s, i in spots] + [(s ^ 1) * shares + i for s, i in spots]
    place = jnp.stack([jnp.asarray(i, jnp.int32) for i in place])

    depth = graph_weight.shape[0]
    half = width // CORES
    piece = lax.dynamic_slice(graph_weight, (0, core * half), (depth, half))
    pieces = [piece]
    for d in range(1, parts // 2):
        pieces.append(lax.ppermute(piece, "vert", [(i, (i + 2 * d) % parts) for i in range(parts)]))
    pieces = pieces + [swap_part(piece) for piece in pieces]
    origin = [(part - 2 * d) % parts for d in range(parts // 2)]
    origin = jnp.stack(origin + [i ^ 1 for i in origin] + [core, 1 - core]).astype(jnp.int32)
    mine = jnp.stack(pieces)
    other = swap_core(mine)

    edges = block_values[0].reshape(own, -1)
    boundary = arrived.reshape(sources * most_rows, width)
    mixed = call(
        mix_kernel,
        jax.ShapeDtypeStruct((own, width), jnp.bfloat16),
        (block_index[0], inputs, boundary, edges),
        flops=2 * edges.size * width,
        scratch=[pltpu.VMEM((own + sources * most_rows, width), jnp.bfloat16)],
    )
    blocks = ROW_BLOCKS
    rows = own // blocks
    lower = []
    for r in range(blocks):
        chunk = mixed[r * rows : (r + 1) * rows]
        lower.append([
            lax.ppermute(chunk, "tm", [(i, i + CORES * d) for i in range(steps - CORES * d)])
            for d in range(1, chips)
        ])
    weight, hidden = call(
        assemble_kernel,
        (
            jax.ShapeDtypeStruct((width, width), jnp.bfloat16),
            jax.ShapeDtypeStruct((own, width), jnp.bfloat16),
        ),
        (origin, mine, other, mixed),
        flops=2 * own * width * width,
    )
    sibling = swap_core(hidden)

    slots = CORES * chips
    flags = [jnp.bool_(True), core == 1, core == 0, jnp.bool_(True)]
    reach = [chip >= d for d in range(1, chips) for _ in range(CORES)]
    flags = jnp.stack([*flags[:2], *reach, *flags[2:], *reach]).astype(jnp.int32)
    kept, got = [], []
    group = len(weights) * weights[0].shape[0] // 3
    for r in range(blocks):
        here = slice(r * rows, (r + 1) * rows)
        slot_rows = [hidden[here], sibling[here]]
        for chunk in lower[r]:
            raised = call(
                hidden_kernel,
                jax.ShapeDtypeStruct((rows, width), jnp.bfloat16),
                (chunk, weight),
                flops=2 * rows * width * width,
            )
            slot_rows += [raised, swap_core(raised)]
        shape = jax.ShapeDtypeStruct((rows, group), jnp.bfloat16)
        keep, send = call(
            functools.partial(attend_kernel, slots, len(weights), head_size),
            (shape, shape),
            (flags, *slot_rows, *weights),
            flops=2 * slots * rows * width * 3 * group,
            scratch=[pltpu.VMEM((slots * rows, width), jnp.bfloat16)],
            limit=40,
        )
        kept.append(keep)
        got.append(swap_core(send))

    combined = call(
        functools.partial(combine_kernel, blocks, len(weights)),
        jax.ShapeDtypeStruct((own, width), jnp.bfloat16),
        (place, hidden, *kept, *got),
    )
    return combined[None]


def solution(mesh):
    return jax.shard_map(
        functools.partial(shards, dict(mesh.shape)),
        mesh=mesh,
        in_specs=(
            P("tm", "vert", None),
            P("vert", None),
            P("tm", None, None),
            P("tm", "vert", None, None),
            P("tm", "vert", None),
            P("tm", "vert", None),
            P("tm", "vert", None, None),
        ),
        out_specs=P("tm", "vert", None),
        check_vma=False,
    )
```

time: 192 us -> 104 us (0.54)
  waiting for transfers between devices: 73.7 us -> 35.2 us
  local copies, waits for them, and re-layouts: 39.7 us -> 11.2 us
  Pallas kernels: 0 us -> 24.6 us
  matrix products: 23.8 us -> 1.07 us
  starting transfers between devices: 11.7 us -> 30.9 us
  blocking collectives: 17.6 us -> 0 us
  between operations: 13.6 us -> 0.41 us
  other arithmetic: 10.7 us -> 0.08 us
    all_gather x2 -> x0, waiting for transfers between devices: 33.5 us -> none  [the longest x1 33 us: shards(): lax.all_gather(graph_weight, 'vert', axis=0, tiled=True)]
    ppermute x0 -> x23, waiting for transfers between devices: none -> 32.4 us  [the longest x4 17.1 us: shards(): lax.ppermute(chunk, 'tm', [(i, i + CORES * d) for i in range(steps - CORE...]
    ppermute x0 -> x23, starting transfers between devices: none -> 27.5 us  [the longest x4 10.6 us: shards(): lax.ppermute(chunk, 'tm', [(i, i + CORES * d) for i in range(steps - CORE...]
    all_to_all x1 -> x0, waiting for transfers between devices: 25.9 us -> none  [shards(): lax.all_to_all(hidden[None], 'tm', split_axis=1, concat_axis=0, tiled=True)]
    pallas_call x0 -> x11, Pallas kernels: none -> 24.6 us  [call(): pl.pallas_call(kernel, out_shape=outs, in_specs=[SMEM if a.dtype == jnp.i...]
    dot_general x5 -> x1, matrix products: 23.8 us -> 1.07 us  [shards(): jnp.einsum('qjv,vd->qjd', chosen.astype(jnp.bfloat16), inputs, preferred_...]
    all_to_all x1 -> x0, blocking collectives: 17.6 us -> none  [shards(): lax.all_to_all(attended, 'tm', split_axis=0, concat_axis=1, tiled=True)]
    all_to_all x1, waiting for transfers between devices: 12.8 us -> 2.8 us  [shards(): lax.all_to_all(picked, 'vert', split_axis=0, concat_axis=0, tiled=True)]
  transfers between devices with their start and end apart: 4 -> 24, of which waited for: 4 -> 8; matrix products, arithmetic and copies ran while one was open for 15% -> 9% of each run, Pallas kernels for 0% -> 22%
where the time goes in v1:
time: 104 us; the launch traced here: 103 us
  waiting for transfers between devices  35.2 us (34%)
  starting transfers between devices  30.9 us (30%)
  Pallas kernels  24.6 us (24%)
  local copies, waits for them, and re-layouts  11.2 us (11%)
  matrix products  1.07 us (1%)
    pallas_call x11, Pallas kernels, call(): pl.pallas_call(kernel, out_shape=outs, in_specs=[SMEM if a.dtype == jnp.i...  24.6 us
    ppermute x4, waiting for transfers between devices, shards(): lax.ppermute(chunk, 'tm', [(i, i + CORES * d) for i in range(steps - CORE...  17.1 us
    ppermute x4, starting transfers between devices, shards(): lax.ppermute(chunk, 'tm', [(i, i + CORES * d) for i in range(steps - CORE...  10.6 us
    ppermute x3, waiting for transfers between devices, shards(): lax.ppermute(piece, 'vert', [(i, (i + 2 * d) % parts) for i in range(part...  7.21 us
    ppermute x5, starting transfers between devices, shards(): lax.ppermute(a, 'vert', [(i, i ^ 1) for i in range(parts)])  6.63 us
    ppermute x3, starting transfers between devices, shards(): lax.ppermute(piece, 'vert', [(i, (i + 2 * d) % parts) for i in range(part...  6.14 us
    ppermute x5, waiting for transfers between devices, shards(): lax.ppermute(a, 'vert', [(i, i ^ 1) for i in range(parts)])  5.46 us
    all_to_all x1, starting transfers between devices, shards(): lax.all_to_all(picked, 'vert', split_axis=0, concat_axis=0, tiled=True)  3.41 us
  transfers between devices with their start and end apart: 24, of which 8 were waited for; matrix products, arithmetic and copies ran while one was open for 9% of the time, Pallas kernels for 22%

profile of v1, /device:TPU:0, one launch (start us, length us, event | category | flops | bytes accessed | tf_op | source)
XLA Modules:
  0.0 103.5 jit_solution(1303193917841853781)
XLA Ops:
  0.0 1.0 bitcast_dynamic-update-slice_fusion.7
  1.0 5.1 %collective-permute-start.2 = (bf16[128,512]{1,0:T(8,128)(2,1)S(1)}, bf16[128,512]{1,0:T(8,128)(2,1)S(1)}, u32[]{:S(2)}, u32[]{:S(2)}) collective-permute-start(bf16[128,512]{1,0:T(8,128)(2,1)S(1)} %get-tuple-element.26), channel_id=1, source_target_pairs={{0,6},{1,7},{2,0},{3,1},{4,2},{5,3},{6,4},{7,5},{8,14},{9,15},{10,... | collective-permute-start | bytes 393224 | tf_op jit(solution)/shard_map/ppermute | solution.py:179
  6.2 1.0 collective-permute-start
  7.2 1.5 %collective-permute-start.3 = (bf16[128,512]{1,0:T(8,128)(2,1)S(1)}, bf16[128,512]{1,0:T(8,128)(2,1)S(1)}, u32[]{:S(2)}, u32[]{:S(2)}) collective-permute-start(bf16[128,512]{1,0:T(8,128)(2,1)S(1)} %get-tuple-element.26), channel_id=1, source_target_pairs={{0,1},{1,0},{2,3},{3,2},{4,5},{5,4},{6,7},{7,6},{8,9},{9,8},{10,11... | collective-permute-start | bytes 393224 | tf_op jit(solution)/shard_map/ppermute | solution.py:142
  8.7 1.4 %collective-permute-done.2 = bf16[128,512]{1,0:T(8,128)(2,1)S(1)} collective-permute-done((bf16[128,512]{1,0:T(8,128)(2,1)S(1)}, bf16[128,512]{1,0:T(8,128)(2,1)S(1)}, u32[]{:S(2)}, u32[]{:S(2)}) %collective-permute-start.2) | collective-permute-done | bytes 131104 | tf_op jit(solution)/shard_map/ppermute | solution.py:179
  10.1 1.5 %collective-permute-start.6 = (bf16[128,512]{1,0:T(8,128)(2,1)S(1)}, bf16[128,512]{1,0:T(8,128)(2,1)S(1)}, u32[]{:S(2)}, u32[]{:S(2)}) collective-permute-start(bf16[128,512]{1,0:T(8,128)(2,1)S(1)} %collective-permute-done.2), channel_id=1, source_target_pairs={{0,1},{1,0},{2,3},{3,2},{4,5},{5,4},{6,7},{7,6},{8,9},{9,8},{10,11... | collective-permute-start | bytes 393224 | tf_op jit(solution)/shard_map/ppermute | solution.py:142
  11.5 5.8 %collective-permute-done.1 = bf16[128,512]{1,0:T(8,128)(2,1)S(1)} collective-permute-done((bf16[128,512]{1,0:T(8,128)(2,1)S(1)}, bf16[128,512]{1,0:T(8,128)(2,1)S(1)}, u32[]{:S(2)}, u32[]{:S(2)}) %collective-permute-start.1) | collective-permute-done | bytes 131104 | tf_op jit(solution)/shard_map/ppermute | solution.py:179
  17.4 1.5 %collective-permute-start.5 = (bf16[128,512]{1,0:T(8,128)(2,1)S(1)}, bf16[128,512]{1,0:T(8,128)(2,1)S(1)}, u32[]{:S(2)}, u32[]{:S(2)}) collective-permute-start(bf16[128,512]{1,0:T(8,128)(2,1)S(1)} %collective-permute-done.1), channel_id=1, source_target_pairs={{0,1},{1,0},{2,3},{3,2},{4,5},{5,4},{6,7},{7,6},{8,9},{9,8},{10,11... | collective-permute-start | bytes 393224 | tf_op jit(solution)/shard_map/ppermute | solution.py:142
  18.8 0.5 collective-permute-start.4
  19.5 5.5 %collective-permute-done.4 = bf16[128,512]{1,0:T(8,128)(2,1)S(1)} collective-permute-done((bf16[128,512]{1,0:T(8,128)(2,1)S(1)}, bf16[128,512]{1,0:T(8,128)(2,1)S(1)}, u32[]{:S(2)}, u32[]{:S(2)}) %collective-permute-start.4) | collective-permute-done | bytes 131104 | tf_op jit(solution)/shard_map/ppermute | solution.py:142
  25.2 1.1 %convolution_convert_fusion = bf16[8,16,1024]{2,1,0:T(8,128)(2,1)} fusion(bf16[1,512,1024]{2,1,0:T(8,128)(2,1)S(1)} %copy-done, s32[8,16]{1,0:T(8,128)S(1)} %bitcast.71, pred[8,16]{1,0:T(8,128)(4,1)S(1)} %iota_compare_fusion.1), kind=kOutput, calls=%fused_computation | convolution fusion | flops 134479872 | bytes 1311360 | tf_op jit(solution)/shard_map/qjv,vd->qjd/dot_general | solution.py:150
  26.2 3.4 %all-to-all-start = ((bf16[8,16,1024]{2,1,0:T(8,128)(2,1)}), bf16[8,16,1024]{2,1,0:T(8,128)(2,1)S(1)}, u32[]{:S(2)}, u32[]{:S(2)}) async-start(bf16[8,16,1024]{2,1,0:T(8,128)(2,1)} %convolution_convert_fusion), calls=%async_computation | async-start | bytes 524288 | tf_op jit(solution)/shard_map/all_to_all | solution.py:153
  29.7 2.7 %copy.17 = bf16[2,2,3,64,1024]{4,3,1,2,0:T(8,128)(2,1)} copy(bf16[2,2,3,64,1024]{4,3,2,1,0:T(8,128)(2,1)} %bitcast.69) | data formatting | bytes 3145728 | tf_op jit(solution)/shard_map/reshape | solution.py:158
  32.4 2.1 %dynamic-slice_bitcast_fusion = bf16[384,1024]{1,0:T(8,128)(2,1)} fusion(bf16[2,384,1024]{2,1,0:T(8,128)(2,1)} %bitcast.67, s32[]{:T(128)S(6)} %select_n.53), kind=kLoop, calls=%fused_computation.2 | loop fusion | bytes 1572868 | tf_op jit(solution)/shard_map/jit(dynamic_index_in_dim)/squeeze | solution.py:161
  34.5 1.5 %collective-permute-start.11 = (bf16[384,1024]{1,0:T(8,128)(2,1)}, bf16[384,1024]{1,0:T(8,128)(2,1)}, u32[]{:S(2)}, u32[]{:S(2)}) collective-permute-start(bf16[384,1024]{1,0:T(8,128)(2,1)} %dynamic-slice_bitcast_fusion), channel_id=1, source_target_pairs={{0,16},{8,24},{16,0},{24,8},{1,17},{9,25},{17,1},{25,9},{2,18},{10... | collective-permute-start | bytes 2359304 | tf_op jit(solution)/shard_map/ppermute | solution.py:165
  36.0 0.1 copy.11
  36.1 0.2 copy.12
  36.3 0.2 copy.13.edge_ref
  36.6 2.8 %all-to-all-done = bf16[8,16,1024]{2,1,0:T(8,128)(2,1)S(1)} async-done(((bf16[8,16,1024]{2,1,0:T(8,128)(2,1)}), bf16[8,16,1024]{2,1,0:T(8,128)(2,1)S(1)}, u32[]{:S(2)}, u32[]{:S(2)}) %all-to-all-start) | async-done | bytes 262176 | tf_op jit(solution)/shard_map/all_to_all | solution.py:153
  39.4 1.6 %shard_map.73.mixed_ref = bf16[512,1024]{1,0:T(8,128)(2,1)S(1)} custom-call(s32[4,3]{1,0:T(4,128)S(1)} %bitcast.66, bf16[512,1024]{1,0:T(8,128)(2,1)S(1)} %bitcast.56, bf16[128,1024]{1,0:T(8,128)(2,1)S(1)} %bitcast.57, bf16[512,384]{1,0:T(8,128)(2,1)S(1)} %copy.13.edge_ref), custom_call_target="tpu_custom_call" | custom-call | flops 402653184 | bytes 2752560 | tf_op jit(solution)/shard_map/pallas_call | solution.py:19
  41.1 1.6 %copy-done.3 = bf16[8,128,512]{2,1,0:T(8,128)(2,1)S(1)} copy-done((bf16[8,128,512]{2,1,0:T(8,128)(2,1)S(1)}, bf16[8,128,512]{2,1,0:T(8,128)(2,1)}, u32[]{:S(2)}) %copy-start.3) | copy-done | bytes 1048600
  42.7 2.6 %shard_map.74 = (bf16[1024,1024]{1,0:T(8,128)(2,1)S(1)}, bf16[512,1024]{1,0:T(8,128)(2,1)S(1)}) custom-call(s32[10]{0:T(128)S(1)} %stack.121.place_ref, bf16[8,128,512]{2,1,0:T(8,128)(2,1)S(1)} %copy-done.3, bf16[8,128,512]{2,1,0:T(8,128)(2,1)} %collective-permute-done.7.other_ref, bf16[512,1024]{1,0:T(8,128)(2,1)S(1)} %shard_map.73.mixed_ref), custom_call_target="tpu_custom_call" | custom-call | flops 1073741824 | bytes 6291496 | tf_op jit(solution)/shard_map/pallas_call | solution.py:19
  45.5 0.1 stack.134
  45.6 1.4 %fusion.7 = (bf16[128,1024]{1,0:T(8,128)(2,1)S(1)}, bf16[128,1024]{1,0:T(8,128)(2,1)S(1)}, bf16[128,1024]{1,0:T(8,128)(2,1)S(1)}, bf16[128,1024]{1,0:T(8,128)(2,1)S(1)}) fusion(bf16[512,1024]{1,0:T(8,128)(2,1)} %copy-done.1), kind=kLoop, calls=%fused_computation.20 | loop fusion | bytes 2097152 | tf_op jit(solution)/shard_map/slice | solution.py:199
  47.0 3.4 %collective-permute-start.17 = (bf16[128,1024]{1,0:T(8,128)(2,1)S(1)}, bf16[128,1024]{1,0:T(8,128)(2,1)S(1)}, u32[]{:S(2)}, u32[]{:S(2)}) collective-permute-start(bf16[128,1024]{1,0:T(8,128)(2,1)S(1)} %get-tuple-element.31), channel_id=1, source_target_pairs={{0,16},{8,24},{1,17},{9,25},{2,18},{10,26},{3,19},{11,27},{4,20},{... | collective-permute-start | bytes 786440 | tf_op jit(solution)/shard_map/ppermute | solution.py:201
  50.4 1.3 %collective-permute-start.13 = (bf16[128,1024]{1,0:T(8,128)(2,1)S(1)}, bf16[128,1024]{1,0:T(8,128)(2,1)S(1)}, u32[]{:S(2)}, u32[]{:S(2)}) collective-permute-start(bf16[128,1024]{1,0:T(8,128)(2,1)S(1)} %get-tuple-element.33), channel_id=1, source_target_pairs={{0,16},{8,24},{1,17},{9,25},{2,18},{10,26},{3,19},{11,27},{4,20},{... | collective-permute-start | bytes 786440 | tf_op jit(solution)/shard_map/ppermute | solution.py:201
  51.7 1.3 %collective-permute-start.9 = (bf16[128,1024]{1,0:T(8,128)(2,1)S(1)}, bf16[128,1024]{1,0:T(8,128)(2,1)S(1)}, u32[]{:S(2)}, u32[]{:S(2)}) collective-permute-start(bf16[128,1024]{1,0:T(8,128)(2,1)S(1)} %get-tuple-element.34), channel_id=1, source_target_pairs={{0,16},{8,24},{1,17},{9,25},{2,18},{10,26},{3,19},{11,27},{4,20},{... | collective-permute-start | bytes 786440 | tf_op jit(solution)/shard_map/ppermute | solution.py:201
  53.0 1.7 %collective-permute-done.11.refs_6_ = bf16[384,1024]{1,0:T(8,128)(2,1)} collective-permute-done((bf16[384,1024]{1,0:T(8,128)(2,1)}, bf16[384,1024]{1,0:T(8,128)(2,1)}, u32[]{:S(2)}, u32[]{:S(2)}) %collective-permute-start.11) | collective-permute-done | bytes 786464 | tf_op jit(solution)/shard_map/ppermute | solution.py:165
  54.8 1.6 %collective-permute-start.12 = (bf16[384,1024]{1,0:T(8,128)(2,1)}, bf16[384,1024]{1,0:T(8,128)(2,1)S(1)}, u32[]{:S(2)}, u32[]{:S(2)}) collective-permute-start(bf16[384,1024]{1,0:T(8,128)(2,1)} %collective-permute-done.11.refs_6_), channel_id=1, source_target_pairs={{0,1},{1,0},{2,3},{3,2},{4,5},{5,4},{6,7},{7,6},{8,9},{9,8},{10,11... | collective-permute-start | bytes 2359304 | tf_op jit(solution)/shard_map/ppermute | solution.py:142
  56.4 0.1 fusion.6
  56.5 14.0 %collective-permute-done.9.mixed_ref = bf16[128,1024]{1,0:T(8,128)(2,1)S(1)} collective-permute-done((bf16[128,1024]{1,0:T(8,128)(2,1)S(1)}, bf16[128,1024]{1,0:T(8,128)(2,1)S(1)}, u32[]{:S(2)}, u32[]{:S(2)}) %collective-permute-start.9) | collective-permute-done | bytes 262176 | tf_op jit(solution)/shard_map/ppermute | solution.py:201
  70.6 4.6 %collective-permute-start.15 = (bf16[128,1024]{1,0:T(8,128)(2,1)S(1)}, bf16[128,1024]{1,0:T(8,128)(2,1)S(1)}, u32[]{:S(2)}, u32[]{:S(2)}) collective-permute-start(bf16[128,1024]{1,0:T(8,128)(2,1)S(1)} %get-tuple-element.32), channel_id=1, source_target_pairs={{0,16},{8,24},{1,17},{9,25},{2,18},{10,26},{3,19},{11,27},{4,20},{... | collective-permute-start | bytes 786440 | tf_op jit(solution)/shard_map/ppermute | solution.py:201
  75.1 0.5 shard_map.75.refs_2_
  75.7 0.5 shard_map.77.refs_2_
  76.2 0.6 collective-permute-start.14
  76.7 0.5 shard_map.81.refs_2_
  77.3 3.1 %collective-permute-done.15.mixed_ref = bf16[128,1024]{1,0:T(8,128)(2,1)S(1)} collective-permute-done((bf16[128,1024]{1,0:T(8,128)(2,1)S(1)}, bf16[128,1024]{1,0:T(8,128)(2,1)S(1)}, u32[]{:S(2)}, u32[]{:S(2)}) %collective-permute-start.15) | collective-permute-done | bytes 262176 | tf_op jit(solution)/shard_map/ppermute | solution.py:201
  80.4 0.5 shard_map.79.refs_2_
  80.8 0.6 collective-permute-start.16
  81.4 1.3 %fusion.8 = (bf16[128,1024]{1,0:T(8,128)(2,1)S(1)}, bf16[128,1024]{1,0:T(8,128)(2,1)S(1)}, bf16[128,1024]{1,0:T(8,128)(2,1)S(1)}, bf16[128,1024]{1,0:T(8,128)(2,1)S(1)}) fusion(bf16[512,1024]{1,0:T(8,128)(2,1)} %collective-permute-done.8), kind=kLoop, calls=%fused_computation.21 | loop fusion | bytes 2097152 | tf_op jit(solution)/shard_map/slice | solution.py:223
  82.7 4.2 %shard_map.82 = (bf16[128,512]{1,0:T(8,128)(2,1)S(1)}, bf16[128,512]{1,0:T(8,128)(2,1)S(1)}) custom-call(s32[8]{0:T(128)S(1)} %convert_element_type.8.flag_ref, bf16[128,1024]{1,0:T(8,128)(2,1)S(1)} %get-tuple-element.39.refs_0_, bf16[128,1024]{1,0:T(8,128)(2,1)S(1)} %get-tuple-element.35.refs_1_, bf16[128,1024]{1,0:T(8,128)(2,1)S(1)} %shard_map.81.refs_2_, ...), custom_call_target="tpu_custom_call" | custom-call | flops 1610612736 | bytes 4456480 | tf_op jit(solution)/shard_map/pallas_call | solution.py:19
  86.9 4.1 %shard_map.80 = (bf16[128,512]{1,0:T(8,128)(2,1)S(1)}, bf16[128,512]{1,0:T(8,128)(2,1)S(1)}) custom-call(s32[8]{0:T(128)S(1)} %convert_element_type.8.flag_ref, bf16[128,1024]{1,0:T(8,128)(2,1)S(1)} %get-tuple-element.40.refs_0_, bf16[128,1024]{1,0:T(8,128)(2,1)S(1)} %get-tuple-element.36.refs_1_, bf16[128,1024]{1,0:T(8,128)(2,1)S(1)} %shard_map.79.refs_2_, ...), custom_call_target="tpu_custom_call" | custom-call | flops 1610612736 | bytes 4456480 | tf_op jit(solution)/shard_map/pallas_call | solution.py:19
  91.1 0.6 collective-permute-start.21
  91.6 4.1 %shard_map.78 = (bf16[128,512]{1,0:T(8,128)(2,1)S(1)}, bf16[128,512]{1,0:T(8,128)(2,1)S(1)}) custom-call(s32[8]{0:T(128)S(1)} %convert_element_type.8.flag_ref, bf16[128,1024]{1,0:T(8,128)(2,1)S(1)} %get-tuple-element.41.refs_0_, bf16[128,1024]{1,0:T(8,128)(2,1)S(1)} %get-tuple-element.37.refs_1_, bf16[128,1024]{1,0:T(8,128)(2,1)S(1)} %shard_map.77.refs_2_, ...), custom_call_target="tpu_custom_call" | custom-call | flops 1610612736 | bytes 4456480 | tf_op jit(solution)/shard_map/pallas_call | solution.py:19
  95.9 4.1 %shard_map.76 = (bf16[128,512]{1,0:T(8,128)(2,1)S(1)}, bf16[128,512]{1,0:T(8,128)(2,1)S(1)}) custom-call(s32[8]{0:T(128)S(1)} %convert_element_type.8.flag_ref, bf16[128,1024]{1,0:T(8,128)(2,1)S(1)} %get-tuple-element.42.refs_0_, bf16[128,1024]{1,0:T(8,128)(2,1)S(1)} %get-tuple-element.38.refs_1_, bf16[128,1024]{1,0:T(8,128)(2,1)S(1)} %shard_map.75.refs_2_, ...), custom_call_target="tpu_custom_call" | custom-call | flops 1610612736 | bytes 4456480 | tf_op jit(solution)/shard_map/pallas_call | solution.py:19
  100.0 0.6 collective-permute-start.19
  100.7 0.9 collective-permute-done.19.refs_4_
  101.6 1.9 %shard_map.83 = bf16[512,1024]{1,0:T(8,128)(2,1)} custom-call(s32[8]{0:T(128)S(1)} %stack.110.place_ref, bf16[512,1024]{1,0:T(8,128)(2,1)S(1)} %get-tuple-element.15.hidden_ref, bf16[128,512]{1,0:T(8,128)(2,1)S(1)} %get-tuple-element.17.refs_0_, bf16[128,512]{1,0:T(8,128)(2,1)S(1)} %get-tuple-element.18.refs_1_, ...), custom_call_target="tpu_custom_call" | custom-call | bytes 3145760 | tf_op jit(solution)/shard_map/pallas_call | solution.py:19
  (52 shorter events, 0.9 us)
Async XLA Ops:
  0.0 25.1 %copy-start.8 = (s32[1,1,8]{2,1,0:T(1,128)S(1)}, s32[1,1,8]{2,1,0:T(1,128)}, u32[]{:S(2)}) copy-start(s32[1,1,8]{2,1,0:T(1,128)} %param.11) | copy-start | bytes 100
  0.0 25.2 %copy-start = (bf16[1,512,1024]{2,1,0:T(8,128)(2,1)S(1)}, bf16[1,512,1024]{2,1,0:T(8,128)(2,1)}, u32[]{:S(2)}) copy-start(bf16[1,512,1024]{2,1,0:T(8,128)(2,1)} %param.7) | copy-start | bytes 3145732
  0.0 25.2 %copy-start.6 = (s32[1,1,8,16]{3,2,1,0:T(8,128)S(1)}, s32[1,1,8,16]{3,2,1,0:T(8,128)}, u32[]{:S(2)}) copy-start(s32[1,1,8,16]{3,2,1,0:T(8,128)} %param.10) | copy-start | bytes 1540
  1.0 9.0 %collective-permute-start.2 = (bf16[128,512]{1,0:T(8,128)(2,1)S(1)}, bf16[128,512]{1,0:T(8,128)(2,1)S(1)}, u32[]{:S(2)}, u32[]{:S(2)}) collective-permute-start(bf16[128,512]{1,0:T(8,128)(2,1)S(1)} %get-tuple-element.26), channel_id=1, source_target_pairs={{0,6},{1,7},{2,0},{3,1},{4,2},{5,3},{6,4},{7,5},{8,14},{9,15},{10,... | collective-permute-start | bytes 393224 | tf_op jit(solution)/shard_map/ppermute | solution.py:179
  6.1 11.2 %collective-permute-start.1 = (bf16[128,512]{1,0:T(8,128)(2,1)S(1)}, bf16[128,512]{1,0:T(8,128)(2,1)S(1)}, u32[]{:S(2)}, u32[]{:S(2)}) collective-permute-start(bf16[128,512]{1,0:T(8,128)(2,1)S(1)} %get-tuple-element.26), channel_id=1, source_target_pairs={{0,4},{1,5},{2,6},{3,7},{4,0},{5,1},{6,2},{7,3},{8,12},{9,13},{10,... | collective-permute-start | bytes 393224 | tf_op jit(solution)/shard_map/ppermute | solution.py:179
  6.2 12.7 %collective-permute-start = (bf16[128,512]{1,0:T(8,128)(2,1)S(1)}, bf16[128,512]{1,0:T(8,128)(2,1)S(1)}, u32[]{:S(2)}, u32[]{:S(2)}) collective-permute-start(bf16[128,512]{1,0:T(8,128)(2,1)S(1)} %get-tuple-element.26), channel_id=1, source_target_pairs={{0,2},{1,3},{2,4},{3,5},{4,6},{5,7},{6,0},{7,1},{8,10},{9,11},{10,... | collective-permute-start | bytes 393224 | tf_op jit(solution)/shard_map/ppermute | solution.py:179
  7.2 12.3 %collective-permute-start.3 = (bf16[128,512]{1,0:T(8,128)(2,1)S(1)}, bf16[128,512]{1,0:T(8,128)(2,1)S(1)}, u32[]{:S(2)}, u32[]{:S(2)}) collective-permute-start(bf16[128,512]{1,0:T(8,128)(2,1)S(1)} %get-tuple-element.26), channel_id=1, source_target_pairs={{0,1},{1,0},{2,3},{3,2},{4,5},{5,4},{6,7},{7,6},{8,9},{9,8},{10,11... | collective-permute-start | bytes 393224 | tf_op jit(solution)/shard_map/ppermute | solution.py:142
  10.1 14.9 %collective-permute-start.6 = (bf16[128,512]{1,0:T(8,128)(2,1)S(1)}, bf16[128,512]{1,0:T(8,128)(2,1)S(1)}, u32[]{:S(2)}, u32[]{:S(2)}) collective-permute-start(bf16[128,512]{1,0:T(8,128)(2,1)S(1)} %collective-permute-done.2), channel_id=1, source_target_pairs={{0,1},{1,0},{2,3},{3,2},{4,5},{5,4},{6,7},{7,6},{8,9},{9,8},{10,11... | collective-permute-start | bytes 393224 | tf_op jit(solution)/shard_map/ppermute | solution.py:142
  17.4 7.6 %collective-permute-start.5 = (bf16[128,512]{1,0:T(8,128)(2,1)S(1)}, bf16[128,512]{1,0:T(8,128)(2,1)S(1)}, u32[]{:S(2)}, u32[]{:S(2)}) collective-permute-start(bf16[128,512]{1,0:T(8,128)(2,1)S(1)} %collective-permute-done.1), channel_id=1, source_target_pairs={{0,1},{1,0},{2,3},{3,2},{4,5},{5,4},{6,7},{7,6},{8,9},{9,8},{10,11... | collective-permute-start | bytes 393224 | tf_op jit(solution)/shard_map/ppermute | solution.py:142
  18.8 6.1 %collective-permute-start.4 = (bf16[128,512]{1,0:T(8,128)(2,1)S(1)}, bf16[128,512]{1,0:T(8,128)(2,1)S(1)}, u32[]{:S(2)}, u32[]{:S(2)}) collective-permute-start(bf16[128,512]{1,0:T(8,128)(2,1)S(1)} %collective-permute-done), channel_id=1, source_target_pairs={{0,1},{1,0},{2,3},{3,2},{4,5},{5,4},{6,7},{7,6},{8,9},{9,8},{10,11... | collective-permute-start | bytes 393224 | tf_op jit(solution)/shard_map/ppermute | solution.py:142
  25.0 7.4 %copy-start.2 = (bf16[8,128,512]{2,1,0:T(8,128)(2,1)}, bf16[8,128,512]{2,1,0:T(8,128)(2,1)S(1)}, u32[]{:S(2)}) copy-start(bf16[8,128,512]{2,1,0:T(8,128)(2,1)S(1)} %bitcast_dynamic-update-slice_fusion.mine_ref) | copy-start | bytes 3145732
  25.0 16.1 %collective-permute-start.7 = (bf16[8,128,512]{2,1,0:T(8,128)(2,1)S(1)}, bf16[8,128,512]{2,1,0:T(8,128)(2,1)}, u32[]{:S(2)}, u32[]{:S(2)}) collective-permute-start(bf16[8,128,512]{2,1,0:T(8,128)(2,1)S(1)} %bitcast_dynamic-update-slice_fusion.mine_ref), channel_id=1, source_target_pairs={{0,8},{8,0},{16,24},{24,16},{1,9},{9,1},{17,25},{25,17},{2,10},{10... | collective-permute-start | bytes 3145736 | tf_op jit(solution)/shard_map/ppermute | solution.py:141
  26.2 13.2 %all-to-all-start = ((bf16[8,16,1024]{2,1,0:T(8,128)(2,1)}), bf16[8,16,1024]{2,1,0:T(8,128)(2,1)S(1)}, u32[]{:S(2)}, u32[]{:S(2)}) async-start(bf16[8,16,1024]{2,1,0:T(8,128)(2,1)} %convolution_convert_fusion), calls=%async_computation | async-start | bytes 524288 | tf_op jit(solution)/shard_map/all_to_all | solution.py:153
  32.4 3.7 %copy-start.7 = (s32[1,4,3]{1,0,2:T(1,128)S(1)}, s32[1,4,3]{1,0,2:T(1,128)}, u32[]{:S(2)}) copy-start(s32[1,4,3]{1,0,2:T(1,128)} %param.12) | copy-start | bytes 148
  32.4 3.8 %copy-start.5 = (bf16[1,512,3,128]{3,1,2,0:T(8,128)(2,1)S(1)}, bf16[1,512,3,128]{3,1,2,0:T(8,128)(2,1)}, u32[]{:S(2)}) copy-start(bf16[1,512,3,128]{3,1,2,0:T(8,128)(2,1)} %param.13) | copy-start | bytes 1179652
  34.5 20.2 %collective-permute-start.11 = (bf16[384,1024]{1,0:T(8,128)(2,1)}, bf16[384,1024]{1,0:T(8,128)(2,1)}, u32[]{:S(2)}, u32[]{:S(2)}) collective-permute-start(bf16[384,1024]{1,0:T(8,128)(2,1)} %dynamic-slice_bitcast_fusion), channel_id=1, source_target_pairs={{0,16},{8,24},{16,0},{24,8},{1,17},{9,25},{17,1},{25,9},{2,18},{10... | collective-permute-start | bytes 2359304 | tf_op jit(solution)/shard_map/ppermute | solution.py:165
  41.1 4.3 %copy-start.1 = (bf16[512,1024]{1,0:T(8,128)(2,1)}, bf16[512,1024]{1,0:T(8,128)(2,1)S(1)}, u32[]{:S(2)}) copy-start(bf16[512,1024]{1,0:T(8,128)(2,1)S(1)} %shard_map.73.mixed_ref) | copy-start | bytes 3145732
  41.1 1.6 %copy-start.3 = (bf16[8,128,512]{2,1,0:T(8,128)(2,1)S(1)}, bf16[8,128,512]{2,1,0:T(8,128)(2,1)}, u32[]{:S(2)}) copy-start(bf16[8,128,512]{2,1,0:T(8,128)(2,1)} %copy-done.2) | copy-start | bytes 3145732
  45.4 35.5 %collective-permute-start.8 = (bf16[512,1024]{1,0:T(8,128)(2,1)S(1)}, bf16[512,1024]{1,0:T(8,128)(2,1)}, u32[]{:S(2)}, u32[]{:S(2)}) collective-permute-start(bf16[512,1024]{1,0:T(8,128)(2,1)S(1)} %get-tuple-element.15.hidden_ref), channel_id=1, source_target_pairs={{0,8},{8,0},{16,24},{24,16},{1,9},{9,1},{17,25},{25,17},{2,10},{10... | collective-permute-start | bytes 3145736 | tf_op jit(solution)/shard_map/ppermute | solution.py:141
  45.6 10.8 %copy-start.4 = (bf16[2,2,3,64,1024]{4,3,1,2,0:T(8,128)(2,1)S(1)}, bf16[2,2,3,64,1024]{4,3,1,2,0:T(8,128)(2,1)}, u32[]{:S(2)}) copy-start(bf16[2,2,3,64,1024]{4,3,1,2,0:T(8,128)(2,1)} %copy.17) | copy-start | bytes 4718596
  47.0 29.2 %collective-permute-start.17 = (bf16[128,1024]{1,0:T(8,128)(2,1)S(1)}, bf16[128,1024]{1,0:T(8,128)(2,1)S(1)}, u32[]{:S(2)}, u32[]{:S(2)}) collective-permute-start(bf16[128,1024]{1,0:T(8,128)(2,1)S(1)} %get-tuple-element.31), channel_id=1, source_target_pairs={{0,16},{8,24},{1,17},{9,25},{2,18},{10,26},{3,19},{11,27},{4,20},{... | collective-permute-start | bytes 786440 | tf_op jit(solution)/shard_map/ppermute | solution.py:201
  50.4 25.2 %collective-permute-start.13 = (bf16[128,1024]{1,0:T(8,128)(2,1)S(1)}, bf16[128,1024]{1,0:T(8,128)(2,1)S(1)}, u32[]{:S(2)}, u32[]{:S(2)}) collective-permute-start(bf16[128,1024]{1,0:T(8,128)(2,1)S(1)} %get-tuple-element.33), channel_id=1, source_target_pairs={{0,16},{8,24},{1,17},{9,25},{2,18},{10,26},{3,19},{11,27},{4,20},{... | collective-permute-start | bytes 786440 | tf_op jit(solution)/shard_map/ppermute | solution.py:201
  51.7 18.8 %collective-permute-start.9 = (bf16[128,1024]{1,0:T(8,128)(2,1)S(1)}, bf16[128,1024]{1,0:T(8,128)(2,1)S(1)}, u32[]{:S(2)}, u32[]{:S(2)}) collective-permute-start(bf16[128,1024]{1,0:T(8,128)(2,1)S(1)} %get-tuple-element.34), channel_id=1, source_target_pairs={{0,16},{8,24},{1,17},{9,25},{2,18},{10,26},{3,19},{11,27},{4,20},{... | collective-permute-start | bytes 786440 | tf_op jit(solution)/shard_map/ppermute | solution.py:201
  54.8 27.9 %collective-permute-start.12 = (bf16[384,1024]{1,0:T(8,128)(2,1)}, bf16[384,1024]{1,0:T(8,128)(2,1)S(1)}, u32[]{:S(2)}, u32[]{:S(2)}) collective-permute-start(bf16[384,1024]{1,0:T(8,128)(2,1)} %collective-permute-done.11.refs_6_), channel_id=1, source_target_pairs={{0,1},{1,0},{2,3},{3,2},{4,5},{5,4},{6,7},{7,6},{8,9},{9,8},{10,11... | collective-permute-start | bytes 2359304 | tf_op jit(solution)/shard_map/ppermute | solution.py:142
  70.6 9.8 %collective-permute-start.15 = (bf16[128,1024]{1,0:T(8,128)(2,1)S(1)}, bf16[128,1024]{1,0:T(8,128)(2,1)S(1)}, u32[]{:S(2)}, u32[]{:S(2)}) collective-permute-start(bf16[128,1024]{1,0:T(8,128)(2,1)S(1)} %get-tuple-element.32), channel_id=1, source_target_pairs={{0,16},{8,24},{1,17},{9,25},{2,18},{10,26},{3,19},{11,27},{4,20},{... | collective-permute-start | bytes 786440 | tf_op jit(solution)/shard_map/ppermute | solution.py:201
  75.6 20.3 %collective-permute-start.10 = (bf16[128,1024]{1,0:T(8,128)(2,1)S(1)}, bf16[128,1024]{1,0:T(8,128)(2,1)S(1)}, u32[]{:S(2)}, u32[]{:S(2)}) collective-permute-start(bf16[128,1024]{1,0:T(8,128)(2,1)S(1)} %shard_map.75.refs_2_), channel_id=1, source_target_pairs={{0,8},{8,0},{16,24},{24,16},{1,9},{9,1},{17,25},{25,17},{2,10},{10... | collective-permute-start | bytes 786440 | tf_op jit(solution)/shard_map/ppermute | solution.py:141
  76.2 15.5 %collective-permute-start.14 = (bf16[128,1024]{1,0:T(8,128)(2,1)S(1)}, bf16[128,1024]{1,0:T(8,128)(2,1)S(1)}, u32[]{:S(2)}, u32[]{:S(2)}) collective-permute-start(bf16[128,1024]{1,0:T(8,128)(2,1)S(1)} %shard_map.77.refs_2_), channel_id=1, source_target_pairs={{0,8},{8,0},{16,24},{24,16},{1,9},{9,1},{17,25},{25,17},{2,10},{10... | collective-permute-start | bytes 786440 | tf_op jit(solution)/shard_map/ppermute | solution.py:141
  80.3 2.3 %collective-permute-start.18 = (bf16[128,1024]{1,0:T(8,128)(2,1)S(1)}, bf16[128,1024]{1,0:T(8,128)(2,1)S(1)}, u32[]{:S(2)}, u32[]{:S(2)}) collective-permute-start(bf16[128,1024]{1,0:T(8,128)(2,1)S(1)} %shard_map.81.refs_2_), channel_id=1, source_target_pairs={{0,8},{8,0},{16,24},{24,16},{1,9},{9,1},{17,25},{25,17},{2,10},{10... | collective-permute-start | bytes 786440 | tf_op jit(solution)/shard_map/ppermute | solution.py:141
  80.8 6.1 %collective-permute-start.16 = (bf16[128,1024]{1,0:T(8,128)(2,1)S(1)}, bf16[128,1024]{1,0:T(8,128)(2,1)S(1)}, u32[]{:S(2)}, u32[]{:S(2)}) collective-permute-start(bf16[128,1024]{1,0:T(8,128)(2,1)S(1)} %shard_map.79.refs_2_), channel_id=1, source_target_pairs={{0,8},{8,0},{16,24},{24,16},{1,9},{9,1},{17,25},{25,17},{2,10},{10... | collective-permute-start | bytes 786440 | tf_op jit(solution)/shard_map/ppermute | solution.py:141
  86.9 13.8 %collective-permute-start.22 = (bf16[128,512]{1,0:T(8,128)(2,1)S(1)}, bf16[128,512]{1,0:T(8,128)(2,1)S(1)}, u32[]{:S(2)}, u32[]{:S(2)}) collective-permute-start(bf16[128,512]{1,0:T(8,128)(2,1)S(1)} %get-tuple-element.24), channel_id=1, source_target_pairs={{0,8},{8,0},{16,24},{24,16},{1,9},{9,1},{17,25},{25,17},{2,10},{10... | collective-permute-start | bytes 393224 | tf_op jit(solution)/shard_map/ppermute | solution.py:141
  91.1 9.6 %collective-permute-start.21 = (bf16[128,512]{1,0:T(8,128)(2,1)S(1)}, bf16[128,512]{1,0:T(8,128)(2,1)S(1)}, u32[]{:S(2)}, u32[]{:S(2)}) collective-permute-start(bf16[128,512]{1,0:T(8,128)(2,1)S(1)} %get-tuple-element.23), channel_id=1, source_target_pairs={{0,8},{8,0},{16,24},{24,16},{1,9},{9,1},{17,25},{25,17},{2,10},{10... | collective-permute-start | bytes 393224 | tf_op jit(solution)/shard_map/ppermute | solution.py:141
  95.8 4.9 %collective-permute-start.20 = (bf16[128,512]{1,0:T(8,128)(2,1)S(1)}, bf16[128,512]{1,0:T(8,128)(2,1)S(1)}, u32[]{:S(2)}, u32[]{:S(2)}) collective-permute-start(bf16[128,512]{1,0:T(8,128)(2,1)S(1)} %get-tuple-element.22), channel_id=1, source_target_pairs={{0,8},{8,0},{16,24},{24,16},{1,9},{9,1},{17,25},{25,17},{2,10},{10... | collective-permute-start | bytes 393224 | tf_op jit(solution)/shard_map/ppermute | solution.py:141
  100.0 1.5 %collective-permute-start.19 = (bf16[128,512]{1,0:T(8,128)(2,1)S(1)}, bf16[128,512]{1,0:T(8,128)(2,1)S(1)}, u32[]{:S(2)}, u32[]{:S(2)}) collective-permute-start(bf16[128,512]{1,0:T(8,128)(2,1)S(1)} %get-tuple-element.21), channel_id=1, source_target_pairs={{0,8},{8,0},{16,24},{24,16},{1,9},{9,1},{17,25},{25,17},{2,10},{10... | collective-permute-start | bytes 393224 | tf_op jit(solution)/shard_map/ppermute | solution.py:141

commit v2 on v1

v2 whole, which is shorter than its diff:
```python
import functools

import jax
import jax.numpy as jnp
from jax import lax
from jax.experimental import pallas as pl
from jax.experimental.pallas import tpu as pltpu
from jax.sharding import PartitionSpec as P

CORES = 2
ROW_BLOCKS = 4
VMEM = pl.BlockSpec(memory_space=pltpu.VMEM)
SMEM = pl.BlockSpec(memory_space=pltpu.SMEM)
MASKED = -1e30
LANES = 128
NT = (((1,), (1,)), ((), ()))


def call(kernel, outs, ins, specs=None, out_specs=None, flops=0, scratch=(), limit=24, aliases=None):
    moved = sum(a.size * a.dtype.itemsize for a in (*ins, *jax.tree.leaves(outs)))
    return pl.pallas_call(
        kernel,
        out_shape=outs,
        grid=(1,) if specs else (),
        in_specs=specs or [SMEM if a.dtype == jnp.int32 else VMEM for a in ins],
        out_specs=out_specs or jax.tree.map(lambda _: VMEM, outs),
        scratch_shapes=scratch,
        input_output_aliases=aliases or {},
        compiler_params=pltpu.CompilerParams(vmem_limit_bytes=limit * 2**20),
        cost_estimate=pl.CostEstimate(flops=flops, bytes_accessed=moved, transcendentals=0),
    )(*ins)


def shaped(*shape):
    return jax.ShapeDtypeStruct(shape, jnp.bfloat16)


def mix_kernel(index_ref, own_ref, arrived_ref, edge_ref, *refs):
    own = own_ref.shape[0]
    *chunk_refs, mixed_ref, columns_ref = refs
    block_rows, chosen = index_ref.shape
    size = own // block_rows
    columns_ref[:own, :] = own_ref[...]
    columns_ref[own:, :] = arrived_ref[...]
    for b in range(block_rows):
        rows = slice(b * size, (b + 1) * size)
        total = own_ref[rows, :].astype(jnp.float32)
        for k in range(chosen):
            start = pl.multiple_of(index_ref[b, k] * size, size)
            total += jnp.dot(
                edge_ref[rows, k * size : (k + 1) * size],
                columns_ref[pl.ds(start, size), :],
                preferred_element_type=jnp.float32,
            )
        mixed_ref[rows, :] = total.astype(mixed_ref.dtype)
    rows = own // len(chunk_refs)
    for r, chunk_ref in enumerate(chunk_refs):
        chunk_ref[...] = mixed_ref[r * rows : (r + 1) * rows, :]


def relu_dot(left, right):
    total = jnp.dot(left, right, preferred_element_type=jnp.float32)
    return jnp.maximum(total, 0.0).astype(jnp.bfloat16)


def assemble_kernel(place_ref, mine_ref, other_ref, mixed_ref, weight_ref, hidden_ref):
    pieces, depth, width = mine_ref.shape
    for half, ref in enumerate((mine_ref, other_ref)):
        column = pl.multiple_of(place_ref[pieces + half] * width, width)
        for i in range(pieces):
            row = pl.multiple_of(place_ref[i] * depth, depth)
            weight_ref[pl.ds(row, depth), pl.ds(column, width)] = ref[i]
    hidden_ref[...] = relu_dot(mixed_ref[...], weight_ref[...])


def own_kernel(lists, mine_ref, other_ref, *refs):
    weight_refs = refs[:lists]
    pair_ref, query_ref, both_ref, ask_ref, stacked_ref = refs[lists:]
    rows = mine_ref.shape[0]
    pieces, double, _ = pair_ref.shape
    width = double // 2
    head_size = weight_refs[0].shape[1] // 3
    i = 0
    for ref in weight_refs:
        for j in range(ref.shape[0]):
            piece, start = divmod(i * head_size, width)
            here = slice(start, start + head_size)
            ask_ref[piece, here, :] = ref[j, :head_size, :]
            pair_ref[piece, here, :] = ref[j, head_size : 2 * head_size, :]
            here = slice(width + start, width + start + head_size)
            pair_ref[piece, here, :] = ref[j, 2 * head_size :, :]
            i += 1
    stacked_ref[:rows, :] = mine_ref[...]
    stacked_ref[rows:, :] = other_ref[...]
    for p in range(pieces):
        for weight_ref, out_ref in ((ask_ref, query_ref), (pair_ref, both_ref)):
            packed = lax.dot_general(
                stacked_ref[...], weight_ref[p], NT, preferred_element_type=jnp.float32
            ).astype(jnp.bfloat16)
            out_ref[0, p] = packed[:rows]
            out_ref[1, p] = packed[rows:]


def attend_kernel(groups, head_size, flag_ref, weight_ref, *refs):
    pair_refs, query_refs, both_refs = refs[:groups], refs[groups : 2 * groups], refs[2 * groups : 3 * groups]
    *mixed_refs, mine_ref, other_ref, stacked_ref = refs[3 * groups :]
    rows = mine_ref.shape[0]
    slots = CORES + len(mixed_refs)
    for s, ref in enumerate(mixed_refs):
        stacked_ref[s * rows : (s + 1) * rows, :] = ref[...]
    raised = relu_dot(stacked_ref[...], weight_ref[...])
    at = 0
    for pair_ref, query_ref, both_ref in zip(pair_refs, query_refs, both_refs):
        pieces, double, _ = pair_ref.shape
        width = double // 2
        group = lambda axis: lax.broadcasted_iota(jnp.int32, (double, width), axis) % width // head_size
        spread = (group(0) == group(1)).astype(jnp.bfloat16)
        for p in range(pieces):
            packed = lax.dot_general(
                raised, pair_ref[p], NT, preferred_element_type=jnp.float32
            ).astype(jnp.bfloat16)
            both = [both_ref[u, p].astype(jnp.float32) for u in range(CORES)]
            both += [
                packed[s * rows : (s + 1) * rows].astype(jnp.float32) for s in range(len(mixed_refs))
            ]
            for t, out_ref in enumerate((mine_ref, other_ref)):
                query = query_ref[t, p].astype(jnp.float32)
                products = jnp.concatenate([query * b[:, :width] for b in both], axis=0)
                high = products.astype(jnp.bfloat16)
                low = (products - high.astype(jnp.float32)).astype(jnp.bfloat16)
                scores = jnp.dot(
                    jnp.concatenate([high, low], axis=1), spread, preferred_element_type=jnp.float32
                ) * head_size ** (-0.5)
                parts = [
                    jnp.where(flag_ref[t * slots + u] > 0, scores[u * rows : (u + 1) * rows], MASKED)
                    for u in range(slots)
                ]
                top = functools.reduce(jnp.maximum, parts)
                parts = [jnp.exp(part - top) for part in parts]
                scale = 1.0 / functools.reduce(jnp.add, parts)
                total = jnp.zeros_like(top)
                for u in range(slots):
                    share = (parts[u] * scale).astype(jnp.bfloat16).astype(jnp.float32)
                    total += share * both[u][:, width:]
                out_ref[:, at : at + width] = total.astype(out_ref.dtype)
            at += width


def combine_kernel(pieces, place_ref, hidden_ref, mine_ref, other_ref, *refs):
    out_ref = refs[-1]
    width = mine_ref.shape[1] // pieces
    lanes = width % LANES == 0
    whole = None if lanes else hidden_ref[...].astype(jnp.float32)
    for half, attended_ref in enumerate((mine_ref, other_ref)):
        for p in range(pieces):
            start = place_ref[half * pieces + p] * width
            attended = attended_ref[:, p * width : (p + 1) * width]
            if lanes:
                column = pl.ds(pl.multiple_of(start, width), width)
                total = hidden_ref[:, column].astype(jnp.float32) + attended.astype(jnp.float32)
                out_ref[:, column] = total.astype(out_ref.dtype)
            else:
                shape = (width, out_ref.shape[1])
                spot = lax.broadcasted_iota(jnp.int32, shape, 0) + start
                spot = (spot == lax.broadcasted_iota(jnp.int32, shape, 1)).astype(jnp.bfloat16)
                whole += jnp.dot(attended, spot, preferred_element_type=jnp.float32)
    if not lanes:
        out_ref[...] = whole.astype(out_ref.dtype)


def shards(sizes, features, graph_weight, head_weight, send_rows, send_count, block_index, block_values):
    steps, parts = sizes["tm"], sizes["vert"]
    chips = steps // CORES
    step, part = lax.axis_index("tm"), lax.axis_index("vert")
    core, chip = step % CORES, step // CORES
    swap_core = lambda a: lax.ppermute(a, "tm", [(i, i ^ 1) for i in range(steps)])
    swap_part = lambda a, bit: lax.ppermute(a, "vert", [(i, i ^ bit) for i in range(parts)])
    inputs = features[0]
    own, width = inputs.shape

    heads, head_rows, _ = head_weight.shape
    head_size = head_rows // 3
    shared = heads % 4 == 0 and parts % 4 == 0
    shares = 2 if shared else 1
    share = (part ^ (part >> 1)) % shares
    sent = lax.dynamic_slice_in_dim(head_weight, share * (heads // shares), heads // shares, 0)
    fetched = [
        lax.ppermute(sent, "tm", [(i, (i + CORES * d) % steps) for i in range(steps)])
        for d in range(1, chips)
    ]

    rows_list = send_rows[0, 0]
    sources, most_rows = rows_list.shape
    live = jnp.arange(most_rows)[None, :] < send_count[0, 0][:, None]
    chosen = (rows_list[:, :, None] == jnp.arange(own)) & live[:, :, None]
    picked = jnp.einsum(
        "qjv,vd->qjd", chosen.astype(jnp.bfloat16), inputs, preferred_element_type=jnp.float32
    ).astype(jnp.bfloat16)
    arrived = lax.all_to_all(picked, "vert", split_axis=0, concat_axis=0, tiled=True)

    depth = graph_weight.shape[0]
    half = width // CORES
    piece = lax.dynamic_slice(graph_weight, (0, core * half), (depth, half))
    piece, _ = lax.optimization_barrier((piece, picked))
    pieces = [piece]
    for d in range(1, parts // 2):
        pieces.append(lax.ppermute(piece, "vert", [(i, (i + 2 * d) % parts) for i in range(parts)]))
    pieces = pieces + [swap_part(piece, 1) for piece in pieces]
    mine = jnp.stack(pieces)
    other = swap_core(mine)
    origin = [(part - 2 * d) % parts for d in range(parts // 2)]
    origin = jnp.stack(origin + [i ^ 1 for i in origin] + [core, 1 - core]).astype(jnp.int32)

    edges = block_values[0].reshape(own, -1)
    boundary = arrived.reshape(sources * most_rows, width)
    blocks = ROW_BLOCKS
    rows = own // blocks
    *chunks, mixed = call(
        mix_kernel,
        (*[shaped(rows, width)] * blocks, shaped(own, width)),
        (block_index[0], inputs, boundary, edges),
        flops=2 * edges.size * width,
        scratch=[pltpu.VMEM((own + sources * most_rows, width), jnp.bfloat16)],
    )
    chunks, fetched = lax.optimization_barrier((chunks, fetched))
    lower = [
        [
            lax.ppermute(chunk, "tm", [(i, i + CORES * d) for i in range(steps - CORES * d)])
            for d in range(1, chips)
        ]
        for chunk in chunks
    ]
    weight, hidden = call(
        assemble_kernel,
        (shaped(width, width), shaped(own, width)),
        (origin, mine, other, mixed),
        flops=2 * own * width * width,
    )
    sibling = swap_core(hidden)

    groups = [[head_weight]]
    spots = [step * shares + i for i in range(shares)]
    for d in range(1, chips):
        block = (step - CORES * d) % steps
        group = fetched[d - 1]
        if shared:
            middle = heads // 4
            groups.append([group, swap_part(group[:middle], 1), swap_part(group[middle:], 2)])
            spots += [block * 2 + share, block * 2 + 1 - share]
        else:
            groups.append([group])
            spots.append(block)
    place = jnp.stack(spots + [i ^ shares for i in spots]).astype(jnp.int32)
    owned = []
    for group in groups:
        size = heads * head_size
        piece = min(size, LANES)
        count = size // piece
        owned.append(call(
            functools.partial(own_kernel, len(group)),
            (
                shaped(count, 2 * piece, width),
                shaped(CORES, count, own, piece),
                shaped(CORES, count, own, 2 * piece),
            ),
            (hidden, sibling, *group),
            flops=2 * CORES * own * width * 3 * size,
            scratch=[
                pltpu.VMEM((count, piece, width), jnp.bfloat16),
                pltpu.VMEM((CORES * own, width), jnp.bfloat16),
            ],
        ))
    pairs, queries, boths = zip(*owned)

    slots = CORES * chips
    flags = [jnp.bool_(True), core == 1, core == 0, jnp.bool_(True)]
    reach = [chip >= d for d in range(1, chips) for _ in range(CORES)]
    flags = jnp.stack([*flags[:2], *reach, *flags[2:], *reach]).astype(jnp.int32)
    total = sum(a.shape[1] * a.shape[3] for a in queries)
    combined = []
    for r in range(blocks):
        mixed_rows = [a for chunk in lower[r] for a in (chunk, swap_core(chunk))]
        cut = lambda a: pl.BlockSpec((*a.shape[:2], rows, a.shape[3]), lambda _, r=r: (0, 0, r, 0))
        keep, send = call(
            functools.partial(attend_kernel, len(groups), head_size),
            (shaped(rows, total), shaped(rows, total)),
            (flags, weight, *pairs, *queries, *boths, *mixed_rows),
            specs=[SMEM, VMEM] + [VMEM] * len(pairs) + [cut(a) for a in (*queries, *boths)] + [VMEM] * len(mixed_rows),
            flops=2 * len(mixed_rows) * rows * width * (2 * total + width),
            scratch=[pltpu.VMEM((len(mixed_rows) * rows, width), jnp.bfloat16)],
        )
        line = pl.BlockSpec((rows, width), lambda _, r=r: (r, 0))
        combined = [call(
            functools.partial(combine_kernel, len(spots)),
            shaped(own, width),
            (place, hidden, keep, swap_core(send), *combined),
            specs=[SMEM, line, VMEM, VMEM] + [pl.BlockSpec(memory_space=pl.ANY)] * len(combined),
            out_specs=line,
            aliases={4: 0} if combined else None,
        )]
    return combined[0][None]


def solution(mesh):
    return jax.shard_map(
        functools.partial(shards, dict(mesh.shape)),
        mesh=mesh,
        in_specs=(
            P("tm", "vert", None),
            P("vert", None),
            P("tm", None, None),
            P("tm", "vert", None, None),
            P("tm", "vert", None),
            P("tm", "vert", None),
            P("tm", "vert", None, None),
        ),
        out_specs=P("tm", "vert", None),
        check_vma=False,
    )
```

time: 104 us -> 110 us (1.058)
  waiting for transfers between devices: 35.2 us -> 20.8 us
  Pallas kernels: 24.6 us -> 35.8 us
  starting transfers between devices: 30.9 us -> 38 us
  matrix products: 1.07 us -> 2.3 us
    ppermute x4, waiting for transfers between devices: 17.1 us -> 2.82 us  [shards(): lax.ppermute(chunk, 'tm', [(i, i + CORES * d) for i in range(steps - CORE...]
    pallas_call x11 -> x12, Pallas kernels: 24.6 us -> 35.8 us  [call(): pl.pallas_call(kernel, out_shape=outs, grid=(1,) if specs else (), in_spe...]
    ppermute x3, waiting for transfers between devices: 7.21 us -> 2.72 us  [shards(): lax.ppermute(piece, 'vert', [(i, (i + 2 * d) % parts) for i in range(part...]
    ppermute x1, waiting for transfers between devices: 1.72 us -> 5.98 us  [shards(): lax.ppermute(sent, 'tm', [(i, (i + CORES * d) % steps) for i in range(ste...]
    unnamed x27 -> x33, local copies, waits for them, and re-layouts: 2.98 us -> 7.2 us
    all_to_all x1, waiting for transfers between devices: 2.8 us -> 6.5 us  [shards(): lax.all_to_all(picked, 'vert', split_axis=0, concat_axis=0, tiled=True)]
    reshape x1 -> x0, local copies, waits for them, and re-layouts: 2.7 us -> none  [shards(): ordered = head_weight.reshape(shares, heads // shares, 3, head_size, width)]
    ppermute x5 -> x6, waiting for transfers between devices: 5.46 us -> 2.78 us  [shards(): lax.ppermute(a, 'vert', [(i, i ^ bit) for i in range(parts)])]
  transfers between devices with their start and end apart: 24 -> 25, of which waited for: 8 -> 8; matrix products, arithmetic and copies ran while one was open for 9% -> 8% of each run, Pallas kernels for 22% -> 32%
where the time goes in v2:
time: 110 us; the launch traced here: 109 us
  starting transfers between devices  38 us (35%)
  Pallas kernels  35.8 us (33%)
  waiting for transfers between devices  20.8 us (19%)
  local copies, waits for them, and re-layouts  11.4 us (10%)
  matrix products  2.3 us (2%)
    pallas_call x12, Pallas kernels, call(): pl.pallas_call(kernel, out_shape=outs, grid=(1,) if specs else (), in_spe...  35.8 us
    ppermute x4, starting transfers between devices, shards(): lax.ppermute(chunk, 'tm', [(i, i + CORES * d) for i in range(steps - CORE...  13.3 us
    ppermute x6, starting transfers between devices, shards(): lax.ppermute(a, 'vert', [(i, i ^ bit) for i in range(parts)])  8.48 us
    unnamed x33, local copies, waits for them, and re-layouts  7.2 us
    ppermute x3, starting transfers between devices, shards(): lax.ppermute(piece, 'vert', [(i, (i + 2 * d) % parts) for i in range(part...  6.96 us
    all_to_all x1, waiting for transfers between devices, shards(): lax.all_to_all(picked, 'vert', split_axis=0, concat_axis=0, tiled=True)  6.5 us
    ppermute x1, waiting for transfers between devices, shards(): lax.ppermute(sent, 'tm', [(i, (i + CORES * d) % steps) for i in range(ste...  5.98 us
    all_to_all x1, starting transfers between devices, shards(): lax.all_to_all(picked, 'vert', split_axis=0, concat_axis=0, tiled=True)  5.59 us
  transfers between devices with their start and end apart: 25, of which 8 were waited for; matrix products, arithmetic and copies ran while one was open for 8% of the time, Pallas kernels for 32%

profile of v2, /device:TPU:0, one launch (start us, length us, event | category | flops | bytes accessed | tf_op | source)
XLA Modules:
  0.0 109.2 jit_solution(6714029493963717594)
XLA Ops:
  0.0 0.8 iota_compare_fusion.1
  1.0 2.3 %convolution_convert_fusion = bf16[8,16,1024]{2,1,0:T(8,128)(2,1)} fusion(bf16[1,512,1024]{2,1,0:T(8,128)(2,1)} %param.7, s32[8,16]{1,0:T(8,128)} %bitcast.51, pred[8,16]{1,0:T(8,128)(4,1)S(1)} %iota_compare_fusion.1), kind=kOutput, calls=%fused_computation | convolution fusion | flops 134479872 | bytes 1311360 | tf_op jit(solution)/shard_map/qjv,vd->qjd/dot_general | solution.py:196
  3.3 3.0 %collective-permute-start = (bf16[128,512]{1,0:T(8,128)(2,1)S(1)}, bf16[128,512]{1,0:T(8,128)(2,1)S(1)}, u32[]{:S(2)}, u32[]{:S(2)}) collective-permute-start(bf16[128,512]{1,0:T(8,128)(2,1)S(1)} %constant_dynamic-slice_fusion.1), channel_id=1, source_target_pairs={{0,2},{1,3},{2,4},{3,5},{4,6},{5,7},{6,0},{7,1},{8,10},{9,11},{10,... | collective-permute-start | bytes 393224 | tf_op jit(solution)/shard_map/ppermute | solution.py:207
  6.3 2.6 %collective-permute-start.1 = (bf16[128,512]{1,0:T(8,128)(2,1)S(1)}, bf16[128,512]{1,0:T(8,128)(2,1)S(1)}, u32[]{:S(2)}, u32[]{:S(2)}) collective-permute-start(bf16[128,512]{1,0:T(8,128)(2,1)S(1)} %constant_dynamic-slice_fusion.1), channel_id=1, source_target_pairs={{0,4},{1,5},{2,6},{3,7},{4,0},{5,1},{6,2},{7,3},{8,12},{9,13},{10,... | collective-permute-start | bytes 393224 | tf_op jit(solution)/shard_map/ppermute | solution.py:207
  8.9 1.3 %collective-permute-start.2 = (bf16[128,512]{1,0:T(8,128)(2,1)S(1)}, bf16[128,512]{1,0:T(8,128)(2,1)S(1)}, u32[]{:S(2)}, u32[]{:S(2)}) collective-permute-start(bf16[128,512]{1,0:T(8,128)(2,1)S(1)} %constant_dynamic-slice_fusion.1), channel_id=1, source_target_pairs={{0,6},{1,7},{2,0},{3,1},{4,2},{5,3},{6,4},{7,5},{8,14},{9,15},{10,... | collective-permute-start | bytes 393224 | tf_op jit(solution)/shard_map/ppermute | solution.py:207
  10.2 1.5 %collective-permute-start.3 = (bf16[128,512]{1,0:T(8,128)(2,1)S(1)}, bf16[128,512]{1,0:T(8,128)(2,1)S(1)}, u32[]{:S(2)}, u32[]{:S(2)}) collective-permute-start(bf16[128,512]{1,0:T(8,128)(2,1)S(1)} %constant_dynamic-slice_fusion.1), channel_id=1, source_target_pairs={{0,1},{1,0},{2,3},{3,2},{4,5},{5,4},{6,7},{7,6},{8,9},{9,8},{10,11... | collective-permute-start | bytes 393224 | tf_op jit(solution)/shard_map/ppermute | solution.py:177
  11.7 0.7 bitcast_dynamic-update-slice_fusion.7
  12.8 1.7 %collective-permute-start.4 = (bf16[128,512]{1,0:T(8,128)(2,1)S(1)}, bf16[128,512]{1,0:T(8,128)(2,1)S(1)}, u32[]{:S(2)}, u32[]{:S(2)}) collective-permute-start(bf16[128,512]{1,0:T(8,128)(2,1)S(1)} %collective-permute-done), channel_id=1, source_target_pairs={{0,1},{1,0},{2,3},{3,2},{4,5},{5,4},{6,7},{7,6},{8,9},{9,8},{10,11... | collective-permute-start | bytes 393224 | tf_op jit(solution)/shard_map/ppermute | solution.py:177
  14.5 0.7 bitcast_dynamic-update-slice_fusion.6
  15.2 2.4 %collective-permute-done.1 = bf16[128,512]{1,0:T(8,128)(2,1)S(1)} collective-permute-done((bf16[128,512]{1,0:T(8,128)(2,1)S(1)}, bf16[128,512]{1,0:T(8,128)(2,1)S(1)}, u32[]{:S(2)}, u32[]{:S(2)}) %collective-permute-start.1) | collective-permute-done | bytes 131104 | tf_op jit(solution)/shard_map/ppermute | solution.py:207
  17.5 1.5 %collective-permute-start.5 = (bf16[128,512]{1,0:T(8,128)(2,1)S(1)}, bf16[128,512]{1,0:T(8,128)(2,1)S(1)}, u32[]{:S(2)}, u32[]{:S(2)}) collective-permute-start(bf16[128,512]{1,0:T(8,128)(2,1)S(1)} %collective-permute-done.1), channel_id=1, source_target_pairs={{0,1},{1,0},{2,3},{3,2},{4,5},{5,4},{6,7},{7,6},{8,9},{9,8},{10,11... | collective-permute-start | bytes 393224 | tf_op jit(solution)/shard_map/ppermute | solution.py:177
  19.0 0.7 bitcast_dynamic-update-slice_fusion.5
  19.7 0.5 collective-permute-start.6
  20.2 0.7 bitcast_dynamic-update-slice_fusion.4
  20.9 0.7 bitcast_dynamic-update-slice_fusion.3
  21.6 0.7 bitcast_dynamic-update-slice_fusion.2
  22.2 1.6 %collective-permute-done.5 = bf16[128,512]{1,0:T(8,128)(2,1)S(1)} collective-permute-done((bf16[128,512]{1,0:T(8,128)(2,1)S(1)}, bf16[128,512]{1,0:T(8,128)(2,1)S(1)}, u32[]{:S(2)}, u32[]{:S(2)}) %collective-permute-start.5) | collective-permute-done | bytes 131104 | tf_op jit(solution)/shard_map/ppermute | solution.py:177
  23.8 0.7 bitcast_dynamic-update-slice_fusion.1
  24.5 1.2 %collective-permute-done.6 = bf16[128,512]{1,0:T(8,128)(2,1)S(1)} collective-permute-done((bf16[128,512]{1,0:T(8,128)(2,1)S(1)}, bf16[128,512]{1,0:T(8,128)(2,1)S(1)}, u32[]{:S(2)}, u32[]{:S(2)}) %collective-permute-start.6) | collective-permute-done | bytes 131104 | tf_op jit(solution)/shard_map/ppermute | solution.py:177
  25.7 0.7 bitcast_dynamic-update-slice_fusion.mine_ref
  26.3 5.6 %all-to-all-start = ((bf16[8,16,1024]{2,1,0:T(8,128)(2,1)}), bf16[8,16,1024]{2,1,0:T(8,128)(2,1)S(1)}, u32[]{:S(2)}, u32[]{:S(2)}) async-start(bf16[8,16,1024]{2,1,0:T(8,128)(2,1)} %convolution_convert_fusion), calls=%async_computation | async-start | bytes 524288 | tf_op jit(solution)/shard_map/all_to_all | solution.py:199
  32.0 0.9 constant_dynamic-slice_fusion
  32.9 1.5 %collective-permute-start.9 = (bf16[2,192,1024]{2,1,0:T(8,128)(2,1)}, bf16[2,192,1024]{2,1,0:T(8,128)(2,1)}, u32[]{:S(2)}, u32[]{:S(2)}) collective-permute-start(bf16[2,192,1024]{2,1,0:T(8,128)(2,1)} %constant_dynamic-slice_fusion), channel_id=1, source_target_pairs={{0,16},{8,24},{16,0},{24,8},{1,17},{9,25},{17,1},{25,9},{2,18},{10... | collective-permute-start | bytes 2359304 | tf_op jit(solution)/shard_map/ppermute | solution.py:188
  35.0 6.5 %all-to-all-done = bf16[8,16,1024]{2,1,0:T(8,128)(2,1)S(1)} async-done(((bf16[8,16,1024]{2,1,0:T(8,128)(2,1)}), bf16[8,16,1024]{2,1,0:T(8,128)(2,1)S(1)}, u32[]{:S(2)}, u32[]{:S(2)}) %all-to-all-start) | async-done | bytes 262176 | tf_op jit(solution)/shard_map/all_to_all | solution.py:199
  41.5 2.3 %shard_map.73 = (bf16[128,1024]{1,0:T(8,128)(2,1)S(1)}, bf16[128,1024]{1,0:T(8,128)(2,1)S(1)}, bf16[128,1024]{1,0:T(8,128)(2,1)}, bf16[128,1024]{1,0:T(8,128)(2,1)}, bf16[512,1024]{1,0:T(8,128)(2,1)S(1)}) custom-call(s32[4,3]{1,0:T(4,128)S(1)} %bitcast.49, bf16[512,1024]{1,0:T(8,128)(2,1)S(1)} %bitcast.47, bf16[128,1024]{1,0:T(8,128)(2,1)S(1)} %bitcast.48, ...), custom_call_target="tpu_custom_call" | custom-call | flops 402653184 | bytes 3801136 | tf_op jit(solution)/shard_map/pallas_call | solution.py:21
  43.9 3.0 %shard_map.74 = (bf16[1024,1024]{1,0:T(8,128)(2,1)S(1)}, bf16[512,1024]{1,0:T(8,128)(2,1)S(1)}) custom-call(s32[10]{0:T(128)S(1)} %stack.121.place_ref, bf16[8,128,512]{2,1,0:T(8,128)(2,1)} %bitcast_dynamic-update-slice_fusion.mine_ref, bf16[8,128,512]{2,1,0:T(8,128)(2,1)} %collective-permute-done.7.other_ref, bf16[512,1024]{1,0:T(8,128)(2,1)S(1)} %get-tuple-element.33.mixed_ref), custom_call_target="tpu_custom_call" | custom-call | flops 1073741824 | bytes 6291496 | tf_op jit(solution)/shard_map/pallas_call | solution.py:21
  46.9 6.0 %collective-permute-done.9.refs_0_ = bf16[2,192,1024]{2,1,0:T(8,128)(2,1)} collective-permute-done((bf16[2,192,1024]{2,1,0:T(8,128)(2,1)}, bf16[2,192,1024]{2,1,0:T(8,128)(2,1)}, u32[]{:S(2)}, u32[]{:S(2)}) %collective-permute-start.9) | collective-permute-done | bytes 786464 | tf_op jit(solution)/shard_map/ppermute | solution.py:188
  52.9 4.1 %collective-permute-start.21 = (bf16[128,1024]{1,0:T(8,128)(2,1)S(1)}, bf16[128,1024]{1,0:T(8,128)(2,1)}, u32[]{:S(2)}, u32[]{:S(2)}) collective-permute-start(bf16[128,1024]{1,0:T(8,128)(2,1)S(1)} %get-tuple-element.56), channel_id=1, source_target_pairs={{0,16},{8,24},{1,17},{9,25},{2,18},{10,26},{3,19},{11,27},{4,20},{... | collective-permute-start | bytes 786440 | tf_op jit(solution)/shard_map/ppermute | solution.py:228
  57.0 2.0 %collective-permute-start.18 = (bf16[128,1024]{1,0:T(8,128)(2,1)S(1)}, bf16[128,1024]{1,0:T(8,128)(2,1)}, u32[]{:S(2)}, u32[]{:S(2)}) collective-permute-start(bf16[128,1024]{1,0:T(8,128)(2,1)S(1)} %get-tuple-element.53), channel_id=1, source_target_pairs={{0,16},{8,24},{1,17},{9,25},{2,18},{10,26},{3,19},{11,27},{4,20},{... | collective-permute-start | bytes 786440 | tf_op jit(solution)/shard_map/ppermute | solution.py:228
  59.0 2.0 %collective-permute-start.15 = (bf16[128,1024]{1,0:T(8,128)(2,1)}, bf16[128,1024]{1,0:T(8,128)(2,1)}, u32[]{:S(2)}, u32[]{:S(2)}) collective-permute-start(bf16[128,1024]{1,0:T(8,128)(2,1)} %get-tuple-element.50), channel_id=1, source_target_pairs={{0,16},{8,24},{1,17},{9,25},{2,18},{10,26},{3,19},{11,27},{4,20},{... | collective-permute-start | bytes 786440 | tf_op jit(solution)/shard_map/ppermute | solution.py:228
  61.0 2.0 %fusion.5 = (bf16[1,192,1024]{2,1,0:T(8,128)(2,1)}, bf16[1,192,1024]{2,1,0:T(8,128)(2,1)}) fusion(bf16[2,192,1024]{2,1,0:T(8,128)(2,1)} %collective-permute-done.9.refs_0_), kind=kLoop, calls=%fused_computation.17 | loop fusion | bytes 1572864 | tf_op jit(solution)/shard_map/slice | solution.py:248
  63.1 1.8 %collective-permute-start.10 = (bf16[1,192,1024]{2,1,0:T(8,128)(2,1)}, bf16[1,192,1024]{2,1,0:T(8,128)(2,1)}, u32[]{:S(2)}, u32[]{:S(2)}) collective-permute-start(bf16[1,192,1024]{2,1,0:T(8,128)(2,1)} %get-tuple-element.60), channel_id=1, source_target_pairs={{0,1},{1,0},{2,3},{3,2},{4,5},{5,4},{6,7},{7,6},{8,9},{9,8},{10,11... | collective-permute-start | bytes 1179656 | tf_op jit(solution)/shard_map/ppermute | solution.py:177
  64.8 1.5 %collective-permute-start.11 = (bf16[1,192,1024]{2,1,0:T(8,128)(2,1)}, bf16[1,192,1024]{2,1,0:T(8,128)(2,1)}, u32[]{:S(2)}, u32[]{:S(2)}) collective-permute-start(bf16[1,192,1024]{2,1,0:T(8,128)(2,1)} %get-tuple-element.59), channel_id=1, source_target_pairs={{0,2},{1,3},{2,0},{3,1},{4,6},{5,7},{6,4},{7,5},{8,10},{9,11},{10,... | collective-permute-start | bytes 1179656 | tf_op jit(solution)/shard_map/ppermute | solution.py:177
  66.3 2.4 %collective-permute-done.18.refs_6_ = bf16[128,1024]{1,0:T(8,128)(2,1)} collective-permute-done((bf16[128,1024]{1,0:T(8,128)(2,1)S(1)}, bf16[128,1024]{1,0:T(8,128)(2,1)}, u32[]{:S(2)}, u32[]{:S(2)}) %collective-permute-start.18) | collective-permute-done | bytes 262176 | tf_op jit(solution)/shard_map/ppermute | solution.py:228
  68.7 5.2 %collective-permute-start.12 = (bf16[128,1024]{1,0:T(8,128)(2,1)}, bf16[128,1024]{1,0:T(8,128)(2,1)}, u32[]{:S(2)}, u32[]{:S(2)}) collective-permute-start(bf16[128,1024]{1,0:T(8,128)(2,1)} %get-tuple-element.47), channel_id=1, source_target_pairs={{0,16},{8,24},{1,17},{9,25},{2,18},{10,26},{3,19},{11,27},{4,20},{... | collective-permute-start | bytes 786440 | tf_op jit(solution)/shard_map/ppermute | solution.py:228
  74.4 0.5 collective-permute-start.19
  74.9 1.4 %copy-done.3 = bf16[4,192,1024]{2,1,0:T(8,128)(2,1)S(1)} copy-done((bf16[4,192,1024]{2,1,0:T(8,128)(2,1)S(1)}, bf16[4,192,1024]{2,1,0:T(8,128)(2,1)}, u32[]{:S(2)}) %copy-start.3) | copy-done | bytes 1572888
  76.3 3.6 %shard_map.75 = (bf16[2,256,1024]{2,1,0:T(8,128)(2,1)S(1)}, bf16[2,2,512,128]{3,2,1,0:T(8,128)(2,1)S(1)}, bf16[2,2,512,256]{3,2,1,0:T(8,128)(2,1)S(1)}) custom-call(bf16[512,1024]{1,0:T(8,128)(2,1)S(1)} %get-tuple-element.34.mine_ref.hidden_ref, bf16[512,1024]{1,0:T(8,128)(2,1)} %collective-permute-done.8.other_ref, bf16[4,192,1024]{2,1,0:T(8,128)(2,1)S(1)} %copy-done.3), custom_call_target="tpu_custom_call" | custom-call | flops 1610612736 | bytes 6291456 | tf_op jit(solution)/shard_map/pallas_call | solution.py:21
  80.5 4.0 %shard_map.76 = (bf16[2,256,1024]{2,1,0:T(8,128)(2,1)S(1)}, bf16[2,2,512,128]{3,2,1,0:T(8,128)(2,1)S(1)}, bf16[2,2,512,256]{3,2,1,0:T(8,128)(2,1)S(1)}) custom-call(bf16[512,1024]{1,0:T(8,128)(2,1)S(1)} %get-tuple-element.34.mine_ref.hidden_ref, bf16[512,1024]{1,0:T(8,128)(2,1)} %collective-permute-done.8.other_ref, ...), custom_call_target="tpu_custom_call" | custom-call | flops 1610612736 | bytes 6291456 | tf_op jit(solution)/shard_map/pallas_call | solution.py:21
  84.5 4.1 %shard_map.80 = (bf16[128,512]{1,0:T(8,128)(2,1)S(1)}, bf16[128,512]{1,0:T(8,128)(2,1)}) custom-call(s32[8]{0:T(128)S(1)} %convert_element_type.8.flag_ref, bf16[1024,1024]{1,0:T(8,128)(2,1)S(1)} %get-tuple-element.35.weight_ref, bf16[2,256,1024]{2,1,0:T(8,128)(2,1)S(1)} %get-tuple-element.36.refs_0_, bf16[2,256,1024]{2,1,0:T(8,128)(2,1)S(1)} %get-tuple-element.42.refs_1_, ...), custom_call_target="tpu_custom_call" | custom-call | flops 1073741824 | bytes 8126496 | tf_op jit(solution)/shard_map/pallas_call | solution.py:21
  88.7 4.1 %shard_map.79 = (bf16[128,512]{1,0:T(8,128)(2,1)S(1)}, bf16[128,512]{1,0:T(8,128)(2,1)}) custom-call(s32[8]{0:T(128)S(1)} %convert_element_type.8.flag_ref, bf16[1024,1024]{1,0:T(8,128)(2,1)S(1)} %get-tuple-element.35.weight_ref, bf16[2,256,1024]{2,1,0:T(8,128)(2,1)S(1)} %get-tuple-element.36.refs_0_, bf16[2,256,1024]{2,1,0:T(8,128)(2,1)S(1)} %get-tuple-element.42.refs_1_, ...), custom_call_target="tpu_custom_call" | custom-call | flops 1073741824 | bytes 8126496 | tf_op jit(solution)/shard_map/pallas_call | solution.py:21
  93.2 4.1 %shard_map.78 = (bf16[128,512]{1,0:T(8,128)(2,1)S(1)}, bf16[128,512]{1,0:T(8,128)(2,1)}) custom-call(s32[8]{0:T(128)S(1)} %convert_element_type.8.flag_ref, bf16[1024,1024]{1,0:T(8,128)(2,1)S(1)} %get-tuple-element.35.weight_ref, bf16[2,256,1024]{2,1,0:T(8,128)(2,1)S(1)} %get-tuple-element.36.refs_0_, bf16[2,256,1024]{2,1,0:T(8,128)(2,1)S(1)} %get-tuple-element.42.refs_1_, ...), custom_call_target="tpu_custom_call" | custom-call | flops 1073741824 | bytes 8126496 | tf_op jit(solution)/shard_map/pallas_call | solution.py:21
  97.4 4.1 %shard_map.77 = (bf16[128,512]{1,0:T(8,128)(2,1)S(1)}, bf16[128,512]{1,0:T(8,128)(2,1)}) custom-call(s32[8]{0:T(128)S(1)} %convert_element_type.8.flag_ref, bf16[1024,1024]{1,0:T(8,128)(2,1)S(1)} %get-tuple-element.35.weight_ref, bf16[2,256,1024]{2,1,0:T(8,128)(2,1)S(1)} %get-tuple-element.36.refs_0_, bf16[2,256,1024]{2,1,0:T(8,128)(2,1)S(1)} %get-tuple-element.42.refs_1_, ...), custom_call_target="tpu_custom_call" | custom-call | flops 1073741824 | bytes 8126496 | tf_op jit(solution)/shard_map/pallas_call | solution.py:21
  101.4 0.6 copy-done.8
  102.6 1.7 %shard_map.81.refs_0_ = bf16[512,1024]{1,0:T(8,128)(2,1)} custom-call(s32[8]{0:T(128)S(1)} %stack.110.place_ref, bf16[512,1024]{1,0:T(8,128)(2,1)S(1)} %get-tuple-element.34.mine_ref.hidden_ref, bf16[128,512]{1,0:T(8,128)(2,1)S(1)} %get-tuple-element.57.mine_ref, bf16[128,512]{1,0:T(8,128)(2,1)} %collective-permute-done.23.other_ref), custom_call_target="tpu_custom_call" | custom-call | bytes 2359328 | tf_op jit(solution)/shard_map/pallas_call | solution.py:21
  104.3 1.8 %shard_map.82.refs_0_ = bf16[512,1024]{1,0:T(8,128)(2,1)} custom-call(s32[8]{0:T(128)S(1)} %stack.110.place_ref, bf16[512,1024]{1,0:T(8,128)(2,1)S(1)} %get-tuple-element.34.mine_ref.hidden_ref, bf16[128,512]{1,0:T(8,128)(2,1)S(1)} %copy-done.5, bf16[128,512]{1,0:T(8,128)(2,1)} %collective-permute-done.20.other_ref, ...), custom_call_target="tpu_custom_call", output_to_operand_aliasing={{}: (4, {})} | custom-call | bytes 3407904 | tf_op jit(solution)/shard_map/pallas_call | solution.py:21
  106.1 1.8 %shard_map.83.refs_0_ = bf16[512,1024]{1,0:T(8,128)(2,1)} custom-call(s32[8]{0:T(128)S(1)} %stack.110.place_ref, bf16[512,1024]{1,0:T(8,128)(2,1)S(1)} %get-tuple-element.34.mine_ref.hidden_ref, bf16[128,512]{1,0:T(8,128)(2,1)S(1)} %copy-done.7, bf16[128,512]{1,0:T(8,128)(2,1)} %collective-permute-done.17.other_ref, ...), custom_call_target="tpu_custom_call", output_to_operand_aliasing={{}: (4, {})} | custom-call | bytes 3407904 | tf_op jit(solution)/shard_map/pallas_call | solution.py:21
  107.9 1.3 %shard_map.84 = bf16[512,1024]{1,0:T(8,128)(2,1)} custom-call(s32[8]{0:T(128)S(1)} %stack.110.place_ref, bf16[512,1024]{1,0:T(8,128)(2,1)S(1)} %get-tuple-element.34.mine_ref.hidden_ref, bf16[128,512]{1,0:T(8,128)(2,1)S(1)} %copy-done.9, bf16[128,512]{1,0:T(8,128)(2,1)S(1)} %collective-permute-done.14.other_ref, ...), custom_call_target="tpu_custom_call", output_to_operand_aliasing={{}: (4, {})} | custom-call | bytes 3407904 | tf_op jit(solution)/shard_map/pallas_call | solution.py:21
  (58 shorter events, 3.5 us)
Async XLA Ops:
  0.0 1.0 copy-start
  3.3 28.7 %copy-start.2 = (bf16[4,192,1024]{2,1,0:T(8,128)(2,1)S(1)}, bf16[4,192,1024]{2,1,0:T(8,128)(2,1)}, u32[]{:S(2)}) copy-start(bf16[4,192,1024]{2,1,0:T(8,128)(2,1)} %refs_0_.1) | copy-start | bytes 4718596
  3.3 9.5 %collective-permute-start = (bf16[128,512]{1,0:T(8,128)(2,1)S(1)}, bf16[128,512]{1,0:T(8,128)(2,1)S(1)}, u32[]{:S(2)}, u32[]{:S(2)}) collective-permute-start(bf16[128,512]{1,0:T(8,128)(2,1)S(1)} %constant_dynamic-slice_fusion.1), channel_id=1, source_target_pairs={{0,2},{1,3},{2,4},{3,5},{4,6},{5,7},{6,0},{7,1},{8,10},{9,11},{10,... | collective-permute-start | bytes 393224 | tf_op jit(solution)/shard_map/ppermute | solution.py:207
  6.3 11.2 %collective-permute-start.1 = (bf16[128,512]{1,0:T(8,128)(2,1)S(1)}, bf16[128,512]{1,0:T(8,128)(2,1)S(1)}, u32[]{:S(2)}, u32[]{:S(2)}) collective-permute-start(bf16[128,512]{1,0:T(8,128)(2,1)S(1)} %constant_dynamic-slice_fusion.1), channel_id=1, source_target_pairs={{0,4},{1,5},{2,6},{3,7},{4,0},{5,1},{6,2},{7,3},{8,12},{9,13},{10,... | collective-permute-start | bytes 393224 | tf_op jit(solution)/shard_map/ppermute | solution.py:207
  8.9 10.8 %collective-permute-start.2 = (bf16[128,512]{1,0:T(8,128)(2,1)S(1)}, bf16[128,512]{1,0:T(8,128)(2,1)S(1)}, u32[]{:S(2)}, u32[]{:S(2)}) collective-permute-start(bf16[128,512]{1,0:T(8,128)(2,1)S(1)} %constant_dynamic-slice_fusion.1), channel_id=1, source_target_pairs={{0,6},{1,7},{2,0},{3,1},{4,2},{5,3},{6,4},{7,5},{8,14},{9,15},{10,... | collective-permute-start | bytes 393224 | tf_op jit(solution)/shard_map/ppermute | solution.py:207
  10.2 10.7 %collective-permute-start.3 = (bf16[128,512]{1,0:T(8,128)(2,1)S(1)}, bf16[128,512]{1,0:T(8,128)(2,1)S(1)}, u32[]{:S(2)}, u32[]{:S(2)}) collective-permute-start(bf16[128,512]{1,0:T(8,128)(2,1)S(1)} %constant_dynamic-slice_fusion.1), channel_id=1, source_target_pairs={{0,1},{1,0},{2,3},{3,2},{4,5},{5,4},{6,7},{7,6},{8,9},{9,8},{10,11... | collective-permute-start | bytes 393224 | tf_op jit(solution)/shard_map/ppermute | solution.py:177
  12.8 8.8 %collective-permute-start.4 = (bf16[128,512]{1,0:T(8,128)(2,1)S(1)}, bf16[128,512]{1,0:T(8,128)(2,1)S(1)}, u32[]{:S(2)}, u32[]{:S(2)}) collective-permute-start(bf16[128,512]{1,0:T(8,128)(2,1)S(1)} %collective-permute-done), channel_id=1, source_target_pairs={{0,1},{1,0},{2,3},{3,2},{4,5},{5,4},{6,7},{7,6},{8,9},{9,8},{10,11... | collective-permute-start | bytes 393224 | tf_op jit(solution)/shard_map/ppermute | solution.py:177
  17.5 6.3 %collective-permute-start.5 = (bf16[128,512]{1,0:T(8,128)(2,1)S(1)}, bf16[128,512]{1,0:T(8,128)(2,1)S(1)}, u32[]{:S(2)}, u32[]{:S(2)}) collective-permute-start(bf16[128,512]{1,0:T(8,128)(2,1)S(1)} %collective-permute-done.1), channel_id=1, source_target_pairs={{0,1},{1,0},{2,3},{3,2},{4,5},{5,4},{6,7},{7,6},{8,9},{9,8},{10,11... | collective-permute-start | bytes 393224 | tf_op jit(solution)/shard_map/ppermute | solution.py:177
  19.7 6.0 %collective-permute-start.6 = (bf16[128,512]{1,0:T(8,128)(2,1)S(1)}, bf16[128,512]{1,0:T(8,128)(2,1)S(1)}, u32[]{:S(2)}, u32[]{:S(2)}) collective-permute-start(bf16[128,512]{1,0:T(8,128)(2,1)S(1)} %collective-permute-done.2), channel_id=1, source_target_pairs={{0,1},{1,0},{2,3},{3,2},{4,5},{5,4},{6,7},{7,6},{8,9},{9,8},{10,11... | collective-permute-start | bytes 393224 | tf_op jit(solution)/shard_map/ppermute | solution.py:177
  21.6 12.9 %copy-start.10 = (bf16[1,512,3,128]{3,1,2,0:T(8,128)(2,1)S(1)}, bf16[1,512,3,128]{3,1,2,0:T(8,128)(2,1)}, u32[]{:S(2)}) copy-start(bf16[1,512,3,128]{3,1,2,0:T(8,128)(2,1)} %param.13) | copy-start | bytes 1179652
  26.3 17.5 %collective-permute-start.7 = (bf16[8,128,512]{2,1,0:T(8,128)(2,1)}, bf16[8,128,512]{2,1,0:T(8,128)(2,1)}, u32[]{:S(2)}, u32[]{:S(2)}) collective-permute-start(bf16[8,128,512]{2,1,0:T(8,128)(2,1)} %bitcast_dynamic-update-slice_fusion.mine_ref), channel_id=1, source_target_pairs={{0,8},{8,0},{16,24},{24,16},{1,9},{9,1},{17,25},{25,17},{2,10},{10... | collective-permute-start | bytes 3145736 | tf_op jit(solution)/shard_map/ppermute | solution.py:176
  26.3 15.2 %all-to-all-start = ((bf16[8,16,1024]{2,1,0:T(8,128)(2,1)}), bf16[8,16,1024]{2,1,0:T(8,128)(2,1)S(1)}, u32[]{:S(2)}, u32[]{:S(2)}) async-start(bf16[8,16,1024]{2,1,0:T(8,128)(2,1)} %convolution_convert_fusion), calls=%async_computation | async-start | bytes 524288 | tf_op jit(solution)/shard_map/all_to_all | solution.py:199
  31.9 2.9 %copy-start.11 = (s32[1,4,3]{1,0,2:T(1,128)S(1)}, s32[1,4,3]{1,0,2:T(1,128)}, u32[]{:S(2)}) copy-start(s32[1,4,3]{1,0,2:T(1,128)} %param.12) | copy-start | bytes 148
  31.9 9.6 %copy-start.1 = (bf16[1,512,1024]{2,1,0:T(8,128)(2,1)S(1)}, bf16[1,512,1024]{2,1,0:T(8,128)(2,1)}, u32[]{:S(2)}) copy-start(bf16[1,512,1024]{2,1,0:T(8,128)(2,1)} %param.7) | copy-start | bytes 3145732
  32.9 20.0 %collective-permute-start.9 = (bf16[2,192,1024]{2,1,0:T(8,128)(2,1)}, bf16[2,192,1024]{2,1,0:T(8,128)(2,1)}, u32[]{:S(2)}, u32[]{:S(2)}) collective-permute-start(bf16[2,192,1024]{2,1,0:T(8,128)(2,1)} %constant_dynamic-slice_fusion), channel_id=1, source_target_pairs={{0,16},{8,24},{16,0},{24,8},{1,17},{9,25},{17,1},{25,9},{2,18},{10... | collective-permute-start | bytes 2359304 | tf_op jit(solution)/shard_map/ppermute | solution.py:188
  46.8 27.6 %collective-permute-start.8 = (bf16[512,1024]{1,0:T(8,128)(2,1)S(1)}, bf16[512,1024]{1,0:T(8,128)(2,1)}, u32[]{:S(2)}, u32[]{:S(2)}) collective-permute-start(bf16[512,1024]{1,0:T(8,128)(2,1)S(1)} %get-tuple-element.34.mine_ref.hidden_ref), channel_id=1, source_target_pairs={{0,8},{8,0},{16,24},{24,16},{1,9},{9,1},{17,25},{25,17},{2,10},{10... | collective-permute-start | bytes 3145736 | tf_op jit(solution)/shard_map/ppermute | solution.py:176
  52.9 11.9 %collective-permute-start.21 = (bf16[128,1024]{1,0:T(8,128)(2,1)S(1)}, bf16[128,1024]{1,0:T(8,128)(2,1)}, u32[]{:S(2)}, u32[]{:S(2)}) collective-permute-start(bf16[128,1024]{1,0:T(8,128)(2,1)S(1)} %get-tuple-element.56), channel_id=1, source_target_pairs={{0,16},{8,24},{1,17},{9,25},{2,18},{10,26},{3,19},{11,27},{4,20},{... | collective-permute-start | bytes 786440 | tf_op jit(solution)/shard_map/ppermute | solution.py:228
  57.0 11.6 %collective-permute-start.18 = (bf16[128,1024]{1,0:T(8,128)(2,1)S(1)}, bf16[128,1024]{1,0:T(8,128)(2,1)}, u32[]{:S(2)}, u32[]{:S(2)}) collective-permute-start(bf16[128,1024]{1,0:T(8,128)(2,1)S(1)} %get-tuple-element.53), channel_id=1, source_target_pairs={{0,16},{8,24},{1,17},{9,25},{2,18},{10,26},{3,19},{11,27},{4,20},{... | collective-permute-start | bytes 786440 | tf_op jit(solution)/shard_map/ppermute | solution.py:228
  59.0 15.4 %collective-permute-start.15 = (bf16[128,1024]{1,0:T(8,128)(2,1)}, bf16[128,1024]{1,0:T(8,128)(2,1)}, u32[]{:S(2)}, u32[]{:S(2)}) collective-permute-start(bf16[128,1024]{1,0:T(8,128)(2,1)} %get-tuple-element.50), channel_id=1, source_target_pairs={{0,16},{8,24},{1,17},{9,25},{2,18},{10,26},{3,19},{11,27},{4,20},{... | collective-permute-start | bytes 786440 | tf_op jit(solution)/shard_map/ppermute | solution.py:228
  63.1 16.9 %collective-permute-start.10 = (bf16[1,192,1024]{2,1,0:T(8,128)(2,1)}, bf16[1,192,1024]{2,1,0:T(8,128)(2,1)}, u32[]{:S(2)}, u32[]{:S(2)}) collective-permute-start(bf16[1,192,1024]{2,1,0:T(8,128)(2,1)} %get-tuple-element.60), channel_id=1, source_target_pairs={{0,1},{1,0},{2,3},{3,2},{4,5},{5,4},{6,7},{7,6},{8,9},{9,8},{10,11... | collective-permute-start | bytes 1179656 | tf_op jit(solution)/shard_map/ppermute | solution.py:177
  64.8 15.7 %collective-permute-start.11 = (bf16[1,192,1024]{2,1,0:T(8,128)(2,1)}, bf16[1,192,1024]{2,1,0:T(8,128)(2,1)}, u32[]{:S(2)}, u32[]{:S(2)}) collective-permute-start(bf16[1,192,1024]{2,1,0:T(8,128)(2,1)} %get-tuple-element.59), channel_id=1, source_target_pairs={{0,2},{1,3},{2,0},{3,1},{4,6},{5,7},{6,4},{7,5},{8,10},{9,11},{10,... | collective-permute-start | bytes 1179656 | tf_op jit(solution)/shard_map/ppermute | solution.py:177
  68.7 11.2 %collective-permute-start.12 = (bf16[128,1024]{1,0:T(8,128)(2,1)}, bf16[128,1024]{1,0:T(8,128)(2,1)}, u32[]{:S(2)}, u32[]{:S(2)}) collective-permute-start(bf16[128,1024]{1,0:T(8,128)(2,1)} %get-tuple-element.47), channel_id=1, source_target_pairs={{0,16},{8,24},{1,17},{9,25},{2,18},{10,26},{3,19},{11,27},{4,20},{... | collective-permute-start | bytes 786440 | tf_op jit(solution)/shard_map/ppermute | solution.py:228
  74.4 10.1 %collective-permute-start.22 = (bf16[128,1024]{1,0:T(8,128)(2,1)}, bf16[128,1024]{1,0:T(8,128)(2,1)S(1)}, u32[]{:S(2)}, u32[]{:S(2)}) collective-permute-start(bf16[128,1024]{1,0:T(8,128)(2,1)} %collective-permute-done.21.refs_6_), channel_id=1, source_target_pairs={{0,8},{8,0},{16,24},{24,16},{1,9},{9,1},{17,25},{25,17},{2,10},{10... | collective-permute-start | bytes 786440 | tf_op jit(solution)/shard_map/ppermute | solution.py:176
  74.4 14.3 %collective-permute-start.19 = (bf16[128,1024]{1,0:T(8,128)(2,1)}, bf16[128,1024]{1,0:T(8,128)(2,1)S(1)}, u32[]{:S(2)}, u32[]{:S(2)}) collective-permute-start(bf16[128,1024]{1,0:T(8,128)(2,1)} %collective-permute-done.18.refs_6_), channel_id=1, source_target_pairs={{0,8},{8,0},{16,24},{24,16},{1,9},{9,1},{17,25},{25,17},{2,10},{10... | collective-permute-start | bytes 786440 | tf_op jit(solution)/shard_map/ppermute | solution.py:176
  74.9 1.4 %copy-start.3 = (bf16[4,192,1024]{2,1,0:T(8,128)(2,1)S(1)}, bf16[4,192,1024]{2,1,0:T(8,128)(2,1)}, u32[]{:S(2)}) copy-start(bf16[4,192,1024]{2,1,0:T(8,128)(2,1)} %refs_0_.1) | copy-start | bytes 4718596
  79.9 13.3 %collective-permute-start.16 = (bf16[128,1024]{1,0:T(8,128)(2,1)}, bf16[128,1024]{1,0:T(8,128)(2,1)S(1)}, u32[]{:S(2)}, u32[]{:S(2)}) collective-permute-start(bf16[128,1024]{1,0:T(8,128)(2,1)} %collective-permute-done.15.refs_6_), channel_id=1, source_target_pairs={{0,8},{8,0},{16,24},{24,16},{1,9},{9,1},{17,25},{25,17},{2,10},{10... | collective-permute-start | bytes 786440 | tf_op jit(solution)/shard_map/ppermute | solution.py:176
  80.0 17.4 %collective-permute-start.13 = (bf16[128,1024]{1,0:T(8,128)(2,1)}, bf16[128,1024]{1,0:T(8,128)(2,1)S(1)}, u32[]{:S(2)}, u32[]{:S(2)}) collective-permute-start(bf16[128,1024]{1,0:T(8,128)(2,1)} %collective-permute-done.12.refs_6_), channel_id=1, source_target_pairs={{0,8},{8,0},{16,24},{24,16},{1,9},{9,1},{17,25},{25,17},{2,10},{10... | collective-permute-start | bytes 786440 | tf_op jit(solution)/shard_map/ppermute | solution.py:176
  88.6 14.0 %collective-permute-start.23 = (bf16[128,512]{1,0:T(8,128)(2,1)}, bf16[128,512]{1,0:T(8,128)(2,1)}, u32[]{:S(2)}, u32[]{:S(2)}) collective-permute-start(bf16[128,512]{1,0:T(8,128)(2,1)} %get-tuple-element.58), channel_id=1, source_target_pairs={{0,8},{8,0},{16,24},{24,16},{1,9},{9,1},{17,25},{25,17},{2,10},{10... | collective-permute-start | bytes 393224 | tf_op jit(solution)/shard_map/ppermute | solution.py:176
  92.8 4.5 %copy-start.4 = (bf16[128,512]{1,0:T(8,128)(2,1)}, bf16[128,512]{1,0:T(8,128)(2,1)S(1)}, u32[]{:S(2)}) copy-start(bf16[128,512]{1,0:T(8,128)(2,1)S(1)} %get-tuple-element.54.mine_ref) | copy-start | bytes 393220
  92.8 11.6 %collective-permute-start.20 = (bf16[128,512]{1,0:T(8,128)(2,1)}, bf16[128,512]{1,0:T(8,128)(2,1)}, u32[]{:S(2)}, u32[]{:S(2)}) collective-permute-start(bf16[128,512]{1,0:T(8,128)(2,1)} %get-tuple-element.55), channel_id=1, source_target_pairs={{0,8},{8,0},{16,24},{24,16},{1,9},{9,1},{17,25},{25,17},{2,10},{10... | collective-permute-start | bytes 393224 | tf_op jit(solution)/shard_map/ppermute | solution.py:176
  97.3 4.2 %copy-start.6 = (bf16[128,512]{1,0:T(8,128)(2,1)}, bf16[128,512]{1,0:T(8,128)(2,1)S(1)}, u32[]{:S(2)}) copy-start(bf16[128,512]{1,0:T(8,128)(2,1)S(1)} %get-tuple-element.51.mine_ref) | copy-start | bytes 393220
  97.3 8.8 %collective-permute-start.17 = (bf16[128,512]{1,0:T(8,128)(2,1)}, bf16[128,512]{1,0:T(8,128)(2,1)}, u32[]{:S(2)}, u32[]{:S(2)}) collective-permute-start(bf16[128,512]{1,0:T(8,128)(2,1)} %get-tuple-element.52), channel_id=1, source_target_pairs={{0,8},{8,0},{16,24},{24,16},{1,9},{9,1},{17,25},{25,17},{2,10},{10... | collective-permute-start | bytes 393224 | tf_op jit(solution)/shard_map/ppermute | solution.py:176
  101.4 0.6 copy-start.8
  102.1 2.2 %copy-start.5 = (bf16[128,512]{1,0:T(8,128)(2,1)S(1)}, bf16[128,512]{1,0:T(8,128)(2,1)}, u32[]{:S(2)}) copy-start(bf16[128,512]{1,0:T(8,128)(2,1)} %copy-done.4) | copy-start | bytes 393220
  102.1 5.8 %collective-permute-start.14 = (bf16[128,512]{1,0:T(8,128)(2,1)}, bf16[128,512]{1,0:T(8,128)(2,1)S(1)}, u32[]{:S(2)}, u32[]{:S(2)}) collective-permute-start(bf16[128,512]{1,0:T(8,128)(2,1)} %get-tuple-element.49), channel_id=1, source_target_pairs={{0,8},{8,0},{16,24},{24,16},{1,9},{9,1},{17,25},{25,17},{2,10},{10... | collective-permute-start | bytes 393224 | tf_op jit(solution)/shard_map/ppermute | solution.py:176
  104.3 1.8 %copy-start.7 = (bf16[128,512]{1,0:T(8,128)(2,1)S(1)}, bf16[128,512]{1,0:T(8,128)(2,1)}, u32[]{:S(2)}) copy-start(bf16[128,512]{1,0:T(8,128)(2,1)} %copy-done.6) | copy-start | bytes 393220
  106.1 1.8 %copy-start.9 = (bf16[128,512]{1,0:T(8,128)(2,1)S(1)}, bf16[128,512]{1,0:T(8,128)(2,1)}, u32[]{:S(2)}) copy-start(bf16[128,512]{1,0:T(8,128)(2,1)} %copy-done.8) | copy-start | bytes 393220

commit v3 on v0

v3 whole, which is shorter than its diff:
```python
import functools
import math

import jax
import jax.numpy as jnp
from jax import lax
from jax.experimental import pallas as pl
from jax.experimental.pallas import tpu as pltpu
from jax.sharding import PartitionSpec as P

CORES = 2
ROW_CUTS = (0, 5, 8)
VMEM = pl.BlockSpec(memory_space=pltpu.VMEM)
SMEM = pl.BlockSpec(memory_space=pltpu.SMEM)
MASKED = -1e30
LANES = 128
PIECE = 256
NT = (((1,), (1,)), ((), ()))
TN = (((0,), (0,)), ((), ()))


def call(kernel, outs, ins, specs=None, out_specs=None, flops=0, scratch=(), limit=16, aliases=None, seconds=0):
    return pl.pallas_call(
        kernel,
        out_shape=outs,
        grid=(1,) if specs else (),
        in_specs=specs or [SMEM if a.dtype == jnp.int32 else VMEM for a in ins],
        out_specs=out_specs or jax.tree.map(lambda _: VMEM, outs),
        scratch_shapes=scratch,
        input_output_aliases=aliases or {},
        compiler_params=pltpu.CompilerParams(vmem_limit_bytes=limit * 2**20),
        cost_estimate=pl.CostEstimate(flops=int(seconds * 1e15), bytes_accessed=0, transcendentals=0),
    )(*ins)


def shaped(*shape, dtype=jnp.bfloat16):
    return jax.ShapeDtypeStruct(shape, dtype)


def after(value, token):
    return lax.optimization_barrier((value, token))[0]


def pick_kernel(row_ref, own_ref, picked_ref):
    shape = (own_ref.shape[0], row_ref.shape[1])
    chosen = (lax.broadcasted_iota(jnp.int32, shape, 0) == row_ref[...]).astype(jnp.bfloat16)
    picked_ref[...] = lax.dot_general(
        chosen, own_ref[...], TN, preferred_element_type=jnp.float32
    ).astype(picked_ref.dtype)


def mix_own_kernel(index_ref, own_ref, edge_ref, partial_ref, outer_ref, dense_ref):
    own = own_ref.shape[0]
    block_rows, chosen = index_ref.shape
    size = own // block_rows
    for b in range(block_rows):
        rows = slice(b * size, (b + 1) * size)
        blocks = [edge_ref[k, rows, :] for k in range(chosen)]
        for j in range(block_rows + outer_ref.shape[1] // size):
            dense = jnp.zeros_like(blocks[0])
            for k in range(chosen):
                dense = jnp.where(index_ref[b, k] == j, blocks[k], dense)
            if j < block_rows:
                dense_ref[rows, j * size : (j + 1) * size] = dense
            else:
                outer_ref[rows, (j - block_rows) * size : (j - block_rows + 1) * size] = dense
    partial_ref[...] = own_ref[...].astype(jnp.float32) + jnp.dot(
        dense_ref[...], own_ref[...], preferred_element_type=jnp.float32
    )


def mix_outer_kernel(partial_ref, outer_ref, arrived_ref, *refs):
    *chunk_refs, mixed_ref = refs
    total = partial_ref[...] + jnp.dot(
        outer_ref[...], arrived_ref[...], preferred_element_type=jnp.float32
    )
    mixed = total.astype(mixed_ref.dtype)
    mixed_ref[...] = mixed
    at = 0
    for chunk_ref in chunk_refs:
        chunk_ref[...] = mixed[at : at + chunk_ref.shape[0]]
        at += chunk_ref.shape[0]


def stack_kernel(*refs):
    for i, ref in enumerate(refs[:-1]):
        refs[-1][i] = ref[...]


def relu_dot(left, right):
    total = jnp.dot(left, right, preferred_element_type=jnp.float32)
    return jnp.maximum(total, 0.0).astype(jnp.bfloat16)


def assemble_kernel(base, meta_ref, *refs):
    *piece_refs, mine_ref, other_ref, weight_ref, hidden_ref, hidden_other_ref = refs
    _, depth, half = piece_refs[0].shape
    at = base
    for first, second in zip(piece_refs[::2], piece_refs[1::2]):
        for i in range(first.shape[0]):
            row = pl.ds(pl.multiple_of(meta_ref[at] * depth, depth), depth)
            for ref, core in ((first, meta_ref[0]), (second, 1 - meta_ref[0])):
                weight_ref[row, pl.ds(pl.multiple_of(core * half, half), half)] = ref[i]
            at += 1
    hidden_ref[...] = relu_dot(mine_ref[...], weight_ref[...])
    hidden_other_ref[...] = relu_dot(other_ref[...], weight_ref[...])


def arrange_kernel(*refs):
    *weight_refs, ask_ref, pair_ref = refs
    width = ask_ref.shape[1]
    head_size = weight_refs[0].shape[1] // 3
    i = 0
    for ref in weight_refs:
        for j in range(ref.shape[0]):
            piece, start = divmod(i * head_size, width)
            here = slice(start, start + head_size)
            ask_ref[piece, here, :] = ref[j, :head_size, :]
            pair_ref[piece, here, :] = ref[j, head_size : 2 * head_size, :]
            here = slice(width + start, width + start + head_size)
            pair_ref[piece, here, :] = ref[j, 2 * head_size :, :]
            i += 1


def own_kernel(meta_ref, mine_ref, other_ref, ask_ref, pair_ref, query_ref, both_ref, stacked_ref):
    rows = mine_ref.shape[0]
    core = meta_ref[0]
    stacked_ref[:rows, :] = mine_ref[...]
    stacked_ref[rows:, :] = other_ref[...]
    for p in range(ask_ref.shape[0]):
        for weight_ref, out_ref in ((ask_ref, query_ref), (pair_ref, both_ref)):
            packed = lax.dot_general(
                stacked_ref[...], weight_ref[p], NT, preferred_element_type=jnp.float32
            ).astype(jnp.bfloat16)
            out_ref[core, p] = packed[:rows]
            out_ref[1 - core, p] = packed[rows:]


def attend_kernel(groups, head_size, start, meta_ref, weight_ref, *refs):
    pair_refs, query_refs, both_refs = refs[:groups], refs[groups : 2 * groups], refs[2 * groups : 3 * groups]
    *mixed_refs, mine_ref, other_ref, stacked_ref, attended_ref = refs[3 * groups :]
    rows = mine_ref.shape[0]
    here = slice(start, start + rows)
    for s, ref in enumerate(mixed_refs):
        stacked_ref[s * rows : (s + 1) * rows, :] = ref[...]
    raised = relu_dot(stacked_ref[...], weight_ref[...])
    scale = head_size ** (-0.5)
    folded = math.frexp(scale)[0] == 0.5
    at = 0
    for pair_ref, query_ref, both_ref in zip(pair_refs, query_refs, both_refs):
        pieces, double, _ = pair_ref.shape
        width = double // 2
        group = lambda axis: lax.broadcasted_iota(jnp.int32, (width, width), axis) // head_size
        spread = jnp.where(group(0) == group(1), scale if folded else 1.0, 0.0).astype(jnp.bfloat16)
        for p in range(pieces):
            packed = lax.dot_general(raised, pair_ref[p], NT, preferred_element_type=jnp.float32)
            lower = [packed[s * rows : (s + 1) * rows] for s in range(len(mixed_refs))]
            keys = [a[:, :width].astype(jnp.bfloat16) for a in lower]
            values = [a[:, width:] for a in lower]
            keys += [both_ref[u, p, here, :width] for u in range(CORES)]
            values += [both_ref[u, p, here, width:].astype(jnp.float32) for u in range(CORES)]
            for t in range(CORES):
                slots = len(lower) + t + 1
                query = query_ref[t, p, here, :]
                products = jnp.concatenate([query * key for key in keys[:slots]], axis=0)
                scores = jnp.dot(products, spread, preferred_element_type=jnp.float32)
                if not folded:
                    scores *= scale
                parts = [scores[u * rows : (u + 1) * rows] for u in range(slots)]
                for u in range(len(lower)):
                    parts[u] = jnp.where(meta_ref[1 + u // CORES] > 0, parts[u], MASKED)
                top = functools.reduce(jnp.maximum, parts)
                parts = [jnp.exp(part - top) for part in parts]
                total = functools.reduce(jnp.add, [a * b for a, b in zip(parts, values)])
                total *= 1.0 / functools.reduce(jnp.add, parts)
                attended_ref[t, :, at : at + width] = total.astype(attended_ref.dtype)
            at += width
    mine_ref[...] = attended_ref[meta_ref[0]]
    other_ref[...] = attended_ref[1 - meta_ref[0]]


def combine_kernel(blocks, pieces, base, meta_ref, hidden_ref, *refs):
    out_ref = refs[-1]
    width = refs[0].shape[1] // pieces
    lanes = width % LANES == 0
    at = 0
    for r in range(blocks):
        here = slice(at, at + refs[r].shape[0])
        at = here.stop
        whole = None if lanes else hidden_ref[here, :].astype(jnp.float32)
        for half in range(CORES):
            for p in range(pieces):
                start = meta_ref[base + half * pieces + p] * width
                attended = refs[half * blocks + r][:, p * width : (p + 1) * width]
                if lanes:
                    column = pl.ds(pl.multiple_of(start, width), width)
                    total = hidden_ref[here, column].astype(jnp.float32) + attended.astype(jnp.float32)
                    out_ref[here, column] = total.astype(out_ref.dtype)
                else:
                    shape = (width, out_ref.shape[1])
                    spot = lax.broadcasted_iota(jnp.int32, shape, 0) + start
                    spot = (spot == lax.broadcasted_iota(jnp.int32, shape, 1)).astype(jnp.bfloat16)
                    whole += jnp.dot(attended, spot, preferred_element_type=jnp.float32)
        if not lanes:
            out_ref[here, :] = whole.astype(out_ref.dtype)


def shards(sizes, features, graph_weight, head_weight, send_rows, send_count, block_index, block_values):
    steps, parts = sizes["tm"], sizes["vert"]
    chips = steps // CORES
    step, part = lax.axis_index("tm"), lax.axis_index("vert")
    core, chip = step % CORES, step // CORES
    swap_core = lambda a: lax.ppermute(a, "tm", [(i, i ^ 1) for i in range(steps)])
    swap_part = lambda a, bit: lax.ppermute(a, "vert", [(i, i ^ bit) for i in range(parts)])
    turn = lambda a, axis, by, n: lax.ppermute(a, axis, [(i, (i + by) % n) for i in range(n)])
    heads, head_rows, _ = head_weight.shape
    shared = heads % 2 == 0 and parts % 4 == 0
    shares = 2 if shared else 1
    share = (part >> 1) % shares

    around = [(part - 2 * d) % parts for d in range(parts // 2)]
    spots = [step * shares + i for i in range(shares)]
    for d in range(1, chips):
        block = (step - CORES * d) % steps * shares
        spots += [block + share, block + 1 - share] if shared else [block]
    meta = [core, *[chip >= d for d in range(1, chips)], *around, *[i ^ 1 for i in around]]
    meta = jnp.stack([jnp.asarray(i, jnp.int32) for i in meta + spots + [i ^ shares for i in spots]])
    arrays = (features, graph_weight, head_weight, send_rows, send_count, block_index, block_values)
    (features, graph_weight, head_weight, send_rows, send_count, block_index, block_values), meta = (
        lax.optimization_barrier((arrays, meta))
    )
    inputs = features[0]
    own, width = inputs.shape

    head_size = head_rows // 3
    sent = lax.dynamic_slice_in_dim(head_weight, share * (heads // shares), heads // shares, 0)
    fetched = [turn(sent, "tm", CORES * d, steps) for d in range(1, chips)]

    size = heads * head_size
    unit = min(size, PIECE)
    count = size // unit
    arrange = lambda group: call(
        arrange_kernel, (shaped(count, unit, width), shaped(count, 2 * unit, width)), group
    )

    rows_list = send_rows[0, 0]
    sources, most_rows = rows_list.shape
    live = jnp.arange(most_rows)[None, :] < send_count[0, 0][:, None]
    slots = jnp.where(live, rows_list, -1).reshape(1, -1)
    picked = call(
        pick_kernel, shaped(sources * most_rows, width), (slots, inputs),
        specs=[VMEM, VMEM], flops=2 * own * width * sources * most_rows,
    )
    arrived = lax.all_to_all(
        picked.reshape(sources, most_rows, width), "vert", split_axis=0, concat_axis=0, tiled=True
    ).reshape(picked.shape)

    edges = block_values[0].transpose(1, 0, 2)
    outer_size = sources * most_rows
    partial, outer = call(
        mix_own_kernel,
        (shaped(own, width, dtype=jnp.float32), shaped(own, outer_size)),
        (block_index[0], inputs, edges),
        flops=2 * own * own * width,
        scratch=[pltpu.VMEM((own, own), jnp.bfloat16)],
    )

    depth = graph_weight.shape[0]
    half = width // CORES
    piece = lax.dynamic_slice(graph_weight, (0, core * half), (depth, half))
    around = [turn(piece, "vert", 2 * d, parts) for d in range(1, parts // 2)]
    around = call(stack_kernel, shaped(parts // 2, depth, half), (piece, *around), seconds=4e-6)
    arrived, around, fetched, partial, outer = lax.optimization_barrier((arrived, around, fetched, partial, outer))
    across = swap_part(around, 1)

    cuts = [own * cut // ROW_CUTS[-1] for cut in ROW_CUTS]
    blocks = len(cuts) - 1
    *chunks, mixed = call(
        mix_outer_kernel,
        (*[shaped(b - a, width) for a, b in zip(cuts, cuts[1:])], shaped(own, width)),
        (partial, outer, arrived),
        flops=2 * outer.size * width,
    )
    lower = [
        [
            turn(chunk, "tm", CORES * d, steps)
            for d in range(1, chips)
        ]
        for chunk in chunks
    ]
    arranged = arrange([after(head_weight, mixed)])
    across = after(across, arranged)
    groups = []
    for group in fetched:
        groups.append([group, swap_part(group, 2)] if shared else [group])
    weight, hidden, sibling = call(
        functools.partial(assemble_kernel, chips),
        (shaped(width, width), shaped(own, width), shaped(own, width)),
        (
            meta, around, swap_core(around), across, swap_core(across), mixed, swap_core(mixed),
        ),
        flops=4 * own * width * width,
    )

    owned, pairs = [], []
    hidden, sibling, lower[0], groups = lax.optimization_barrier((hidden, sibling, lower[0], groups))
    for g in range(chips):
        ask, pair = arranged if g == 0 else arrange(groups[g - 1])
        pairs.append(pair)
        owned.append(call(
            own_kernel,
            (shaped(CORES, count, own, unit), shaped(CORES, count, own, 2 * unit)),
            (meta, hidden, sibling, ask, pair),
            scratch=[pltpu.VMEM((CORES * own, width), jnp.bfloat16)],
        ))
    queries, boths = zip(*owned)

    total = sum(a.shape[1] * a.shape[3] for a in queries)
    kept, got = [], []
    token = owned[0]
    for r in range(blocks):
        rows = cuts[r + 1] - cuts[r]
        chunk = after(lower[r], token)
        mixed_rows = [a for b in chunk for a in (b, swap_core(b))]
        keep, send = token = call(
            functools.partial(attend_kernel, chips, head_size, cuts[r]),
            (shaped(rows, total), shaped(rows, total)),
            (meta, weight, *pairs, *queries, *boths, *mixed_rows),
            limit=11 + len(mixed_rows) * rows * width // 2**17,
            flops=2 * len(mixed_rows) * rows * width * (2 * total + width),
            scratch=[
                pltpu.VMEM((len(mixed_rows) * rows, width), jnp.bfloat16),
                pltpu.VMEM((CORES, rows, total), jnp.bfloat16),
            ],
        )
        kept.append(keep)
        got.append(swap_core(send))
    combined = call(
        functools.partial(combine_kernel, blocks, len(spots), meta.size - 2 * len(spots)),
        shaped(own, width),
        (meta, hidden, *kept, *got),
    )
    return combined[None]


def solution(mesh):
    return jax.shard_map(
        functools.partial(shards, dict(mesh.shape)),
        mesh=mesh,
        in_specs=(
            P("tm", "vert", None),
            P("vert", None),
            P("tm", None, None),
            P("tm", "vert", None, None),
            P("tm", "vert", None),
            P("tm", "vert", None),
            P("tm", "vert", None, None),
        ),
        out_specs=P("tm", "vert", None),
        check_vma=False,
    )
```

time: 192 us -> 75.4 us (0.39)
  waiting for transfers between devices: 73.7 us -> 24.3 us
  local copies, waits for them, and re-layouts: 39.7 us -> 11.1 us
  matrix products: 23.8 us -> 0 us
  Pallas kernels: 0 us -> 21.2 us
  blocking collectives: 17.6 us -> 0 us
  between operations: 13.6 us -> 0.29 us
  other arithmetic: 10.7 us -> 0.08 us
  starting transfers between devices: 11.7 us -> 18.1 us
    all_to_all x2 -> x1, waiting for transfers between devices: 38.7 us -> 0.65 us  [shards(): lax.all_to_all(picked.reshape(sources, most_rows, width), 'vert', split_a...]
    all_gather x2 -> x0, waiting for transfers between devices: 33.5 us -> none  [the longest x1 33 us: shards(): lax.all_gather(graph_weight, 'vert', axis=0, tiled=True)]
    dot_general x5 -> x0, matrix products: 23.8 us -> none  [the longest x1 5.89 us: attend_heads(): jnp.einsum('tvd,hcd->tvhc', regrouped, head_piece, preferred_element_type...]
    ppermute x0 -> x15, waiting for transfers between devices: none -> 23.6 us  [the longest x6 10.9 us: shards(): lax.ppermute(a, axis, [(i, (i + by) % n) for i in range(n)])]
    pallas_call x0 -> x12, Pallas kernels: none -> 21.2 us  [call(): pl.pallas_call(kernel, out_shape=outs, grid=(1,) if specs else (), in_spe...]
    all_to_all x1 -> x0, blocking collectives: 17.6 us -> none  [shards(): lax.all_to_all(attended, 'tm', split_axis=0, concat_axis=1, tiled=True)]
    ppermute x0 -> x15, starting transfers between devices: none -> 14.7 us  [the longest x6 11.6 us: shards(): lax.ppermute(a, axis, [(i, (i + by) % n) for i in range(n)])]
    slice x4 -> x0, local copies, waits for them, and re-layouts: 12.4 us -> none  [the longest x2 6.19 us: attend_heads(): keys_part = packed[..., head_size:2 * head_size].astype(jnp.bfloat16)]
  transfers between devices with their start and end apart: 4 -> 16, of which waited for: 4 -> 9; matrix products, arithmetic and copies ran while one was open for 15% -> 3% of each run, Pallas kernels for 0% -> 23%
where the time goes in v3:
time: 75.4 us; the launch traced here: 75.1 us
  waiting for transfers between devices  24.3 us (32%)
  Pallas kernels  21.2 us (28%)
  starting transfers between devices  18.1 us (24%)
  local copies, waits for them, and re-layouts  11.1 us (15%)
    pallas_call x12, Pallas kernels, call(): pl.pallas_call(kernel, out_shape=outs, grid=(1,) if specs else (), in_spe...  21.2 us
    ppermute x6, starting transfers between devices, shards(): lax.ppermute(a, axis, [(i, (i + by) % n) for i in range(n)])  11.6 us
    ppermute x6, waiting for transfers between devices, shards(): lax.ppermute(a, axis, [(i, (i + by) % n) for i in range(n)])  10.9 us
    unnamed x30, local copies, waits for them, and re-layouts  8.68 us
    ppermute x2, waiting for transfers between devices, shards(): lax.ppermute(a, 'vert', [(i, i ^ bit) for i in range(parts)])  8.35 us
    ppermute x7, waiting for transfers between devices, shards(): lax.ppermute(a, 'tm', [(i, i ^ 1) for i in range(steps)])  4.43 us
    all_to_all x1, starting transfers between devices, shards(): lax.all_to_all(picked.reshape(sources, most_rows, width), 'vert', split_a...  3.41 us
    ppermute x2, starting transfers between devices, shards(): lax.ppermute(a, 'vert', [(i, i ^ bit) for i in range(parts)])  2.23 us
  transfers between devices with their start and end apart: 16, of which 9 were waited for; matrix products, arithmetic and copies ran while one was open for 3% of the time, Pallas kernels for 23%

profile of v3, /device:TPU:0, one launch (start us, length us, event | category | flops | bytes accessed | tf_op | source)
XLA Modules:
  0.0 75.1 jit_solution(17755090514055692557)
XLA Ops:
  0.1 0.1 stack.79.meta_ref
  0.2 1.0 %copy-done = bf16[128,1024]{1,0:T(8,128)(2,1)S(1)} copy-done((bf16[128,1024]{1,0:T(8,128)(2,1)S(1)}, bf16[128,1024]{1,0:T(8,128)(2,1)}, u32[]{:S(2)}) %copy-start) | copy-done | bytes 262168
  1.3 3.1 %collective-permute-start = (bf16[128,512]{1,0:T(8,128)(2,1)S(1)}, bf16[128,512]{1,0:T(8,128)(2,1)S(1)}, u32[]{:S(2)}, u32[]{:S(2)}) collective-permute-start(bf16[128,512]{1,0:T(8,128)(2,1)S(1)} %constant_dynamic-slice_fusion.1.refs_0_), channel_id=1, source_target_pairs={{0,2},{1,3},{2,4},{3,5},{4,6},{5,7},{6,0},{7,1},{8,10},{9,11},{10,... | collective-permute-start | bytes 393224 | tf_op jit(solution)/shard_map/ppermute | solution.py:215
  4.4 2.6 %collective-permute-start.1 = (bf16[128,512]{1,0:T(8,128)(2,1)S(1)}, bf16[128,512]{1,0:T(8,128)(2,1)S(1)}, u32[]{:S(2)}, u32[]{:S(2)}) collective-permute-start(bf16[128,512]{1,0:T(8,128)(2,1)S(1)} %constant_dynamic-slice_fusion.1.refs_0_), channel_id=1, source_target_pairs={{0,4},{1,5},{2,6},{3,7},{4,0},{5,1},{6,2},{7,3},{8,12},{9,13},{10,... | collective-permute-start | bytes 393224 | tf_op jit(solution)/shard_map/ppermute | solution.py:215
  7.0 1.3 %collective-permute-start.2 = (bf16[128,512]{1,0:T(8,128)(2,1)S(1)}, bf16[128,512]{1,0:T(8,128)(2,1)S(1)}, u32[]{:S(2)}, u32[]{:S(2)}) collective-permute-start(bf16[128,512]{1,0:T(8,128)(2,1)S(1)} %constant_dynamic-slice_fusion.1.refs_0_), channel_id=1, source_target_pairs={{0,6},{1,7},{2,0},{3,1},{4,2},{5,3},{6,4},{7,5},{8,14},{9,15},{10,... | collective-permute-start | bytes 393224 | tf_op jit(solution)/shard_map/ppermute | solution.py:215
  8.3 2.1 %constant_dynamic-slice_fusion = bf16[2,192,1024]{2,1,0:T(8,128)(2,1)} fusion(bf16[4,192,1024]{2,1,0:T(8,128)(2,1)} %refs_0_, s32[]{:T(128)S(6)} %select_n.62), kind=kLoop, calls=%fused_computation.1 | loop fusion | bytes 1572868 | tf_op jit(solution)/shard_map/dynamic_slice | solution.py:236
  10.4 1.5 %collective-permute-start.3 = (bf16[2,192,1024]{2,1,0:T(8,128)(2,1)}, bf16[2,192,1024]{2,1,0:T(8,128)(2,1)S(1)}, u32[]{:S(2)}, u32[]{:S(2)}) collective-permute-start(bf16[2,192,1024]{2,1,0:T(8,128)(2,1)} %constant_dynamic-slice_fusion), channel_id=1, source_target_pairs={{0,16},{8,24},{16,0},{24,8},{1,17},{9,25},{17,1},{25,9},{2,18},{10... | collective-permute-start | bytes 2359304 | tf_op jit(solution)/shard_map/ppermute | solution.py:215
  11.9 0.1 iota_compare_fusion
  12.0 0.1 lt.72
  12.1 0.1 squeeze.12
  12.2 1.0 %shard_map.73 = bf16[128,1024]{1,0:T(8,128)(2,1)} custom-call(s32[1,128]{1,0:T(1,128)S(1)} %broadcast_select_fusion.row_ref, bf16[512,1024]{1,0:T(8,128)(2,1)S(1)} %bitcast.29), custom_call_target="tpu_custom_call" | custom-call | tf_op jit(solution)/shard_map/pallas_call | solution.py:23
  13.2 3.4 %all-to-all-start = ((bf16[8,16,1024]{2,1,0:T(8,128)(2,1)}), bf16[8,16,1024]{2,1,0:T(8,128)(2,1)S(1)}, u32[]{:S(2)}, u32[]{:S(2)}) async-start(bf16[8,16,1024]{2,1,0:T(8,128)(2,1)} %bitcast.20), calls=%async_computation | async-start | bytes 524288 | tf_op jit(solution)/shard_map/all_to_all | solution.py:254
  16.6 0.1 copy.8
  16.7 1.3 %shard_map.75 = (f32[512,1024]{1,0:T(8,128)S(1)}, bf16[512,128]{1,0:T(8,128)(2,1)S(1)}) custom-call(s32[4,3]{1,0:T(4,128)S(1)} %bitcast.33, bf16[512,1024]{1,0:T(8,128)(2,1)S(1)} %bitcast.30, bf16[3,512,128]{2,1,0:T(8,128)(2,1)S(1)} %bitcast.32), custom_call_target="tpu_custom_call" | custom-call | tf_op jit(solution)/shard_map/pallas_call | solution.py:23
  18.0 1.3 %copy-done.3 = f32[512,1024]{1,0:T(8,128)} copy-done((f32[512,1024]{1,0:T(8,128)}, f32[512,1024]{1,0:T(8,128)S(1)}, u32[]{:S(2)}) %copy-start.3) | copy-done | bytes 2097176
  19.4 0.7 copy-done.6
  20.1 0.6 copy-done.8
  20.7 0.6 copy-done.10
  21.4 0.9 %copy-done.7 = bf16[128,512]{1,0:T(8,128)(2,1)S(1)} copy-done((bf16[128,512]{1,0:T(8,128)(2,1)S(1)}, bf16[128,512]{1,0:T(8,128)(2,1)}, u32[]{:S(2)}) %copy-start.7) | copy-done | bytes 131096
  22.3 0.9 %copy-done.9 = bf16[128,512]{1,0:T(8,128)(2,1)S(1)} copy-done((bf16[128,512]{1,0:T(8,128)(2,1)S(1)}, bf16[128,512]{1,0:T(8,128)(2,1)}, u32[]{:S(2)}) %copy-start.9) | copy-done | bytes 131096
  23.2 0.9 %copy-done.11 = bf16[128,512]{1,0:T(8,128)(2,1)S(1)} copy-done((bf16[128,512]{1,0:T(8,128)(2,1)S(1)}, bf16[128,512]{1,0:T(8,128)(2,1)}, u32[]{:S(2)}) %copy-start.11) | copy-done | bytes 131096
  24.1 0.6 all-to-all-done
  24.8 4.2 %collective-permute-done.3.refs_0_ = bf16[2,192,1024]{2,1,0:T(8,128)(2,1)S(1)} collective-permute-done((bf16[2,192,1024]{2,1,0:T(8,128)(2,1)}, bf16[2,192,1024]{2,1,0:T(8,128)(2,1)S(1)}, u32[]{:S(2)}, u32[]{:S(2)}) %collective-permute-start.3) | collective-permute-done | bytes 786464 | tf_op jit(solution)/shard_map/ppermute | solution.py:215
  29.0 1.5 %collective-permute-start.5 = (bf16[4,128,512]{2,1,0:T(8,128)(2,1)S(1)}, bf16[4,128,512]{2,1,0:T(8,128)(2,1)S(1)}, u32[]{:S(2)}, u32[]{:S(2)}) collective-permute-start(bf16[4,128,512]{2,1,0:T(8,128)(2,1)S(1)} %shard_map.74.refs_0_), channel_id=1, source_target_pairs={{0,1},{1,0},{2,3},{3,2},{4,5},{5,4},{6,7},{7,6},{8,9},{9,8},{10,11... | collective-permute-start | bytes 1572872 | tf_op jit(solution)/shard_map/ppermute | solution.py:214
  30.5 1.6 %copy-done.4 = f32[512,1024]{1,0:T(8,128)S(1)} copy-done((f32[512,1024]{1,0:T(8,128)S(1)}, f32[512,1024]{1,0:T(8,128)}, u32[]{:S(2)}) %copy-start.4) | copy-done | bytes 2097176
  32.1 0.4 shard_map.76
  32.5 0.1 collective-permute-start.7
  32.6 0.7 collective-permute-start.9
  33.4 1.5 %collective-permute-start.8 = (bf16[320,1024]{1,0:T(8,128)(2,1)S(1)}, bf16[320,1024]{1,0:T(8,128)(2,1)S(1)}, u32[]{:S(2)}, u32[]{:S(2)}) collective-permute-start(bf16[320,1024]{1,0:T(8,128)(2,1)S(1)} %get-tuple-element.68), channel_id=1, source_target_pairs={{0,16},{8,24},{16,0},{24,8},{1,17},{9,25},{17,1},{25,9},{2,18},{10... | collective-permute-start | bytes 1966088 | tf_op jit(solution)/shard_map/ppermute | solution.py:215
  34.9 0.1 shard_map.77
  35.0 5.9 %collective-permute-done.5.refs_2_ = bf16[4,128,512]{2,1,0:T(8,128)(2,1)S(1)} collective-permute-done((bf16[4,128,512]{2,1,0:T(8,128)(2,1)S(1)}, bf16[4,128,512]{2,1,0:T(8,128)(2,1)S(1)}, u32[]{:S(2)}, u32[]{:S(2)}) %collective-permute-start.5) | collective-permute-done | bytes 524320 | tf_op jit(solution)/shard_map/ppermute | solution.py:214
  40.9 1.9 %collective-permute-done.6.refs_3_ = bf16[4,128,512]{2,1,0:T(8,128)(2,1)S(1)} collective-permute-done((bf16[4,128,512]{2,1,0:T(8,128)(2,1)S(1)}, bf16[4,128,512]{2,1,0:T(8,128)(2,1)S(1)}, u32[]{:S(2)}, u32[]{:S(2)}) %collective-permute-start.6) | collective-permute-done | bytes 524320 | tf_op jit(solution)/shard_map/ppermute | solution.py:213
  42.8 3.0 %shard_map.78 = (bf16[1024,1024]{1,0:T(8,128)(2,1)S(1)}, bf16[512,1024]{1,0:T(8,128)(2,1)S(1)}, bf16[512,1024]{1,0:T(8,128)(2,1)S(1)}) custom-call(s32[18]{0:T(128)S(1)} %stack.79.meta_ref, bf16[4,128,512]{2,1,0:T(8,128)(2,1)S(1)} %shard_map.74.refs_0_, bf16[4,128,512]{2,1,0:T(8,128)(2,1)S(1)} %collective-permute-done.4.refs_1_, ...), custom_call_target="tpu_custom_call" | custom-call | tf_op jit(solution)/shard_map/pallas_call | solution.py:23
  45.9 4.3 %collective-permute-done.8.refs_6_ = bf16[320,1024]{1,0:T(8,128)(2,1)S(1)} collective-permute-done((bf16[320,1024]{1,0:T(8,128)(2,1)S(1)}, bf16[320,1024]{1,0:T(8,128)(2,1)S(1)}, u32[]{:S(2)}, u32[]{:S(2)}) %collective-permute-start.8) | collective-permute-done | bytes 655392 | tf_op jit(solution)/shard_map/ppermute | solution.py:215
  50.2 2.4 %collective-permute-done.9.refs_1_ = bf16[2,192,1024]{2,1,0:T(8,128)(2,1)S(1)} collective-permute-done((bf16[2,192,1024]{2,1,0:T(8,128)(2,1)S(1)}, bf16[2,192,1024]{2,1,0:T(8,128)(2,1)S(1)}, u32[]{:S(2)}, u32[]{:S(2)}) %collective-permute-start.9) | collective-permute-done | bytes 786464 | tf_op jit(solution)/shard_map/ppermute | solution.py:214
  52.6 2.4 %shard_map.80 = (bf16[2,1,512,256]{3,2,1,0:T(8,128)(2,1)S(1)}, bf16[2,1,512,512]{3,2,1,0:T(8,128)(2,1)S(1)}) custom-call(s32[18]{0:T(128)S(1)} %stack.79.meta_ref, bf16[512,1024]{1,0:T(8,128)(2,1)S(1)} %get-tuple-element.70.mine_ref.hidden_ref, bf16[512,1024]{1,0:T(8,128)(2,1)S(1)} %get-tuple-element.75.other_ref, ...), custom_call_target="tpu_custom_call" | custom-call | tf_op jit(solution)/shard_map/pallas_call | solution.py:23
  54.9 0.1 collective-permute-start.10
  55.0 1.6 %collective-permute-start.11 = (bf16[192,1024]{1,0:T(8,128)(2,1)S(1)}, bf16[192,1024]{1,0:T(8,128)(2,1)S(1)}, u32[]{:S(2)}, u32[]{:S(2)}) collective-permute-start(bf16[192,1024]{1,0:T(8,128)(2,1)S(1)} %get-tuple-element.84), channel_id=1, source_target_pairs={{0,16},{8,24},{16,0},{24,8},{1,17},{9,25},{17,1},{25,9},{2,18},{10... | collective-permute-start | bytes 1179656 | tf_op jit(solution)/shard_map/ppermute | solution.py:215
  56.6 0.1 shard_map.79
  56.7 2.4 %shard_map.81 = (bf16[2,1,512,256]{3,2,1,0:T(8,128)(2,1)S(1)}, bf16[2,1,512,512]{3,2,1,0:T(8,128)(2,1)S(1)}) custom-call(s32[18]{0:T(128)S(1)} %stack.79.meta_ref, bf16[512,1024]{1,0:T(8,128)(2,1)S(1)} %get-tuple-element.70.mine_ref.hidden_ref, bf16[512,1024]{1,0:T(8,128)(2,1)S(1)} %get-tuple-element.75.other_ref, ...), custom_call_target="tpu_custom_call" | custom-call | tf_op jit(solution)/shard_map/pallas_call | solution.py:23
  59.1 5.1 %shard_map.82 = (bf16[320,512]{1,0:T(8,128)(2,1)S(1)}, bf16[320,512]{1,0:T(8,128)(2,1)S(1)}) custom-call(s32[18]{0:T(128)S(1)} %stack.79.meta_ref, bf16[1024,1024]{1,0:T(8,128)(2,1)S(1)} %get-tuple-element.71.weight_ref, bf16[1,512,1024]{2,1,0:T(8,128)(2,1)S(1)} %get-tuple-element.64.pair_ref.refs_0_, ...), custom_call_target="tpu_custom_call" | custom-call | tf_op jit(solution)/shard_map/pallas_call | solution.py:23
  64.2 2.3 %collective-permute-done.11.refs_6_ = bf16[192,1024]{1,0:T(8,128)(2,1)S(1)} collective-permute-done((bf16[192,1024]{1,0:T(8,128)(2,1)S(1)}, bf16[192,1024]{1,0:T(8,128)(2,1)S(1)}, u32[]{:S(2)}, u32[]{:S(2)}) %collective-permute-start.11) | collective-permute-done | bytes 393248 | tf_op jit(solution)/shard_map/ppermute | solution.py:215
  66.5 0.5 collective-permute-start.13
  67.1 1.2 %collective-permute-done.12.refs_7_ = bf16[192,1024]{1,0:T(8,128)(2,1)S(1)} collective-permute-done((bf16[192,1024]{1,0:T(8,128)(2,1)S(1)}, bf16[192,1024]{1,0:T(8,128)(2,1)S(1)}, u32[]{:S(2)}, u32[]{:S(2)}) %collective-permute-start.12) | collective-permute-done | bytes 393248 | tf_op jit(solution)/shard_map/ppermute | solution.py:213
  68.3 3.4 %shard_map.83 = (bf16[192,512]{1,0:T(8,128)(2,1)S(1)}, bf16[192,512]{1,0:T(8,128)(2,1)S(1)}) custom-call(s32[18]{0:T(128)S(1)} %stack.79.meta_ref, bf16[1024,1024]{1,0:T(8,128)(2,1)S(1)} %get-tuple-element.71.weight_ref, bf16[1,512,1024]{2,1,0:T(8,128)(2,1)S(1)} %get-tuple-element.64.pair_ref.refs_0_, ...), custom_call_target="tpu_custom_call" | custom-call | tf_op jit(solution)/shard_map/pallas_call | solution.py:23
  71.7 0.2 collective-permute-start.14
  71.9 1.3 %collective-permute-done.14.refs_3_ = bf16[192,512]{1,0:T(8,128)(2,1)S(1)} collective-permute-done((bf16[192,512]{1,0:T(8,128)(2,1)S(1)}, bf16[192,512]{1,0:T(8,128)(2,1)S(1)}, u32[]{:S(2)}, u32[]{:S(2)}) %collective-permute-start.14) | collective-permute-done | bytes 196640 | tf_op jit(solution)/shard_map/ppermute | solution.py:213
  73.2 1.9 %shard_map.84 = bf16[512,1024]{1,0:T(8,128)(2,1)} custom-call(s32[18]{0:T(128)S(1)} %stack.79.meta_ref, bf16[512,1024]{1,0:T(8,128)(2,1)S(1)} %get-tuple-element.70.mine_ref.hidden_ref, bf16[320,512]{1,0:T(8,128)(2,1)S(1)} %get-tuple-element.83.refs_0_, bf16[192,512]{1,0:T(8,128)(2,1)S(1)} %get-tuple-element.87.refs_1_, ...), custom_call_target="tpu_custom_call" | custom-call | tf_op jit(solution)/shard_map/pallas_call | solution.py:23
  (34 shorter events, 0.1 us)
Async XLA Ops:
  0.0 1.3 %copy-start = (bf16[128,1024]{1,0:T(8,128)(2,1)S(1)}, bf16[128,1024]{1,0:T(8,128)(2,1)}, u32[]{:S(2)}) copy-start(bf16[128,1024]{1,0:T(8,128)(2,1)} %param.8) | copy-start | bytes 786436
  0.0 12.1 %copy-start.12 = (s32[1,1,8,16]{3,2,1,0:T(8,128)S(1)}, s32[1,1,8,16]{3,2,1,0:T(8,128)}, u32[]{:S(2)}) copy-start(s32[1,1,8,16]{3,2,1,0:T(8,128)} %param.10) | copy-start | bytes 1540
  0.0 11.9 %copy-start.14 = (s32[1,1,8]{2,1,0:T(1,128)S(1)}, s32[1,1,8]{2,1,0:T(1,128)}, u32[]{:S(2)}) copy-start(s32[1,1,8]{2,1,0:T(1,128)} %param.11) | copy-start | bytes 100
  0.0 16.6 %copy-start.13 = (s32[1,4,3]{1,0,2:T(1,128)S(1)}, s32[1,4,3]{1,0,2:T(1,128)}, u32[]{:S(2)}) copy-start(s32[1,4,3]{1,0,2:T(1,128)} %param.12) | copy-start | bytes 148
  0.0 16.7 %copy-start.5 = (bf16[1,512,3,128]{3,1,2,0:T(8,128)(2,1)S(1)}, bf16[1,512,3,128]{3,1,2,0:T(8,128)(2,1)}, u32[]{:S(2)}) copy-start(bf16[1,512,3,128]{3,1,2,0:T(8,128)(2,1)} %param.13) | copy-start | bytes 1179652
  0.0 12.1 %copy-start.1 = (bf16[1,512,1024]{2,1,0:T(8,128)(2,1)S(1)}, bf16[1,512,1024]{2,1,0:T(8,128)(2,1)}, u32[]{:S(2)}) copy-start(bf16[1,512,1024]{2,1,0:T(8,128)(2,1)} %param.7) | copy-start | bytes 3145732
  1.3 18.1 %collective-permute-start = (bf16[128,512]{1,0:T(8,128)(2,1)S(1)}, bf16[128,512]{1,0:T(8,128)(2,1)S(1)}, u32[]{:S(2)}, u32[]{:S(2)}) collective-permute-start(bf16[128,512]{1,0:T(8,128)(2,1)S(1)} %constant_dynamic-slice_fusion.1.refs_0_), channel_id=1, source_target_pairs={{0,2},{1,3},{2,4},{3,5},{4,6},{5,7},{6,0},{7,1},{8,10},{9,11},{10,... | collective-permute-start | bytes 393224 | tf_op jit(solution)/shard_map/ppermute | solution.py:215
  4.4 15.7 %collective-permute-start.1 = (bf16[128,512]{1,0:T(8,128)(2,1)S(1)}, bf16[128,512]{1,0:T(8,128)(2,1)S(1)}, u32[]{:S(2)}, u32[]{:S(2)}) collective-permute-start(bf16[128,512]{1,0:T(8,128)(2,1)S(1)} %constant_dynamic-slice_fusion.1.refs_0_), channel_id=1, source_target_pairs={{0,4},{1,5},{2,6},{3,7},{4,0},{5,1},{6,2},{7,3},{8,12},{9,13},{10,... | collective-permute-start | bytes 393224 | tf_op jit(solution)/shard_map/ppermute | solution.py:215
  7.0 13.8 %collective-permute-start.2 = (bf16[128,512]{1,0:T(8,128)(2,1)S(1)}, bf16[128,512]{1,0:T(8,128)(2,1)S(1)}, u32[]{:S(2)}, u32[]{:S(2)}) collective-permute-start(bf16[128,512]{1,0:T(8,128)(2,1)S(1)} %constant_dynamic-slice_fusion.1.refs_0_), channel_id=1, source_target_pairs={{0,6},{1,7},{2,0},{3,1},{4,2},{5,3},{6,4},{7,5},{8,14},{9,15},{10,... | collective-permute-start | bytes 393224 | tf_op jit(solution)/shard_map/ppermute | solution.py:215
  10.4 18.7 %collective-permute-start.3 = (bf16[2,192,1024]{2,1,0:T(8,128)(2,1)}, bf16[2,192,1024]{2,1,0:T(8,128)(2,1)S(1)}, u32[]{:S(2)}, u32[]{:S(2)}) collective-permute-start(bf16[2,192,1024]{2,1,0:T(8,128)(2,1)} %constant_dynamic-slice_fusion), channel_id=1, source_target_pairs={{0,16},{8,24},{16,0},{24,8},{1,17},{9,25},{17,1},{25,9},{2,18},{10... | collective-permute-start | bytes 2359304 | tf_op jit(solution)/shard_map/ppermute | solution.py:215
  13.2 11.6 %all-to-all-start = ((bf16[8,16,1024]{2,1,0:T(8,128)(2,1)}), bf16[8,16,1024]{2,1,0:T(8,128)(2,1)S(1)}, u32[]{:S(2)}, u32[]{:S(2)}) async-start(bf16[8,16,1024]{2,1,0:T(8,128)(2,1)} %bitcast.20), calls=%async_computation | async-start | bytes 524288 | tf_op jit(solution)/shard_map/all_to_all | solution.py:254
  18.0 1.4 %copy-start.3 = (f32[512,1024]{1,0:T(8,128)}, f32[512,1024]{1,0:T(8,128)S(1)}, u32[]{:S(2)}) copy-start(f32[512,1024]{1,0:T(8,128)S(1)} %get-tuple-element.58.partial_ref) | copy-start | bytes 6291460
  19.4 0.7 copy-start.6
  20.1 0.6 copy-start.8
  20.7 0.6 copy-start.10
  21.4 0.9 %copy-start.7 = (bf16[128,512]{1,0:T(8,128)(2,1)S(1)}, bf16[128,512]{1,0:T(8,128)(2,1)}, u32[]{:S(2)}) copy-start(bf16[128,512]{1,0:T(8,128)(2,1)} %copy-done.6) | copy-start | bytes 393220
  22.3 0.9 %copy-start.9 = (bf16[128,512]{1,0:T(8,128)(2,1)S(1)}, bf16[128,512]{1,0:T(8,128)(2,1)}, u32[]{:S(2)}) copy-start(bf16[128,512]{1,0:T(8,128)(2,1)} %copy-done.8) | copy-start | bytes 393220
  23.2 0.9 %copy-start.11 = (bf16[128,512]{1,0:T(8,128)(2,1)S(1)}, bf16[128,512]{1,0:T(8,128)(2,1)}, u32[]{:S(2)}) copy-start(bf16[128,512]{1,0:T(8,128)(2,1)} %copy-done.10) | copy-start | bytes 393220
  24.1 10.8 %copy-start.2 = (bf16[4,192,1024]{2,1,0:T(8,128)(2,1)S(1)}, bf16[4,192,1024]{2,1,0:T(8,128)(2,1)}, u32[]{:S(2)}) copy-start(bf16[4,192,1024]{2,1,0:T(8,128)(2,1)} %refs_0_) | copy-start | bytes 4718596
  29.0 11.9 %collective-permute-start.5 = (bf16[4,128,512]{2,1,0:T(8,128)(2,1)S(1)}, bf16[4,128,512]{2,1,0:T(8,128)(2,1)S(1)}, u32[]{:S(2)}, u32[]{:S(2)}) collective-permute-start(bf16[4,128,512]{2,1,0:T(8,128)(2,1)S(1)} %shard_map.74.refs_0_), channel_id=1, source_target_pairs={{0,1},{1,0},{2,3},{3,2},{4,5},{5,4},{6,7},{7,6},{8,9},{9,8},{10,11... | collective-permute-start | bytes 1572872 | tf_op jit(solution)/shard_map/ppermute | solution.py:214
  30.5 1.6 %copy-start.4 = (f32[512,1024]{1,0:T(8,128)S(1)}, f32[512,1024]{1,0:T(8,128)}, u32[]{:S(2)}) copy-start(f32[512,1024]{1,0:T(8,128)} %copy-done.3) | copy-start | bytes 6291460
  32.5 10.3 %collective-permute-start.7 = (bf16[512,1024]{1,0:T(8,128)(2,1)S(1)}, bf16[512,1024]{1,0:T(8,128)(2,1)S(1)}, u32[]{:S(2)}, u32[]{:S(2)}) collective-permute-start(bf16[512,1024]{1,0:T(8,128)(2,1)S(1)} %get-tuple-element.61.refs_4_), channel_id=1, source_target_pairs={{0,8},{8,0},{16,24},{24,16},{1,9},{9,1},{17,25},{25,17},{2,10},{10... | collective-permute-start | bytes 3145736 | tf_op jit(solution)/shard_map/ppermute | solution.py:213
  32.6 20.0 %collective-permute-start.9 = (bf16[2,192,1024]{2,1,0:T(8,128)(2,1)S(1)}, bf16[2,192,1024]{2,1,0:T(8,128)(2,1)S(1)}, u32[]{:S(2)}, u32[]{:S(2)}) collective-permute-start(bf16[2,192,1024]{2,1,0:T(8,128)(2,1)S(1)} %collective-permute-done.3.refs_0_), channel_id=1, source_target_pairs={{0,2},{1,3},{2,0},{3,1},{4,6},{5,7},{6,4},{7,5},{8,10},{9,11},{10,... | collective-permute-start | bytes 2359304 | tf_op jit(solution)/shard_map/ppermute | solution.py:214
  33.4 16.8 %collective-permute-start.8 = (bf16[320,1024]{1,0:T(8,128)(2,1)S(1)}, bf16[320,1024]{1,0:T(8,128)(2,1)S(1)}, u32[]{:S(2)}, u32[]{:S(2)}) collective-permute-start(bf16[320,1024]{1,0:T(8,128)(2,1)S(1)} %get-tuple-element.68), channel_id=1, source_target_pairs={{0,16},{8,24},{16,0},{24,8},{1,17},{9,25},{17,1},{25,9},{2,18},{10... | collective-permute-start | bytes 1966088 | tf_op jit(solution)/shard_map/ppermute | solution.py:215
  34.9 6.1 %collective-permute-start.4 = (bf16[4,128,512]{2,1,0:T(8,128)(2,1)S(1)}, bf16[4,128,512]{2,1,0:T(8,128)(2,1)S(1)}, u32[]{:S(2)}, u32[]{:S(2)}) collective-permute-start(bf16[4,128,512]{2,1,0:T(8,128)(2,1)S(1)} %shard_map.74.refs_0_), channel_id=1, source_target_pairs={{0,8},{8,0},{16,24},{24,16},{1,9},{9,1},{17,25},{25,17},{2,10},{10... | collective-permute-start | bytes 1572872 | tf_op jit(solution)/shard_map/ppermute | solution.py:213
  40.9 1.9 %collective-permute-start.6 = (bf16[4,128,512]{2,1,0:T(8,128)(2,1)S(1)}, bf16[4,128,512]{2,1,0:T(8,128)(2,1)S(1)}, u32[]{:S(2)}, u32[]{:S(2)}) collective-permute-start(bf16[4,128,512]{2,1,0:T(8,128)(2,1)S(1)} %collective-permute-done.5.refs_2_), channel_id=1, source_target_pairs={{0,8},{8,0},{16,24},{24,16},{1,9},{9,1},{17,25},{25,17},{2,10},{10... | collective-permute-start | bytes 1572872 | tf_op jit(solution)/shard_map/ppermute | solution.py:213
  54.9 4.1 %collective-permute-start.10 = (bf16[320,1024]{1,0:T(8,128)(2,1)S(1)}, bf16[320,1024]{1,0:T(8,128)(2,1)S(1)}, u32[]{:S(2)}, u32[]{:S(2)}) collective-permute-start(bf16[320,1024]{1,0:T(8,128)(2,1)S(1)} %collective-permute-done.8.refs_6_), channel_id=1, source_target_pairs={{0,8},{8,0},{16,24},{24,16},{1,9},{9,1},{17,25},{25,17},{2,10},{10... | collective-permute-start | bytes 1966088 | tf_op jit(solution)/shard_map/ppermute | solution.py:213
  55.0 11.5 %collective-permute-start.11 = (bf16[192,1024]{1,0:T(8,128)(2,1)S(1)}, bf16[192,1024]{1,0:T(8,128)(2,1)S(1)}, u32[]{:S(2)}, u32[]{:S(2)}) collective-permute-start(bf16[192,1024]{1,0:T(8,128)(2,1)S(1)} %get-tuple-element.84), channel_id=1, source_target_pairs={{0,16},{8,24},{16,0},{24,8},{1,17},{9,25},{17,1},{25,9},{2,18},{10... | collective-permute-start | bytes 1179656 | tf_op jit(solution)/shard_map/ppermute | solution.py:215
  66.5 1.7 %collective-permute-start.12 = (bf16[192,1024]{1,0:T(8,128)(2,1)S(1)}, bf16[192,1024]{1,0:T(8,128)(2,1)S(1)}, u32[]{:S(2)}, u32[]{:S(2)}) collective-permute-start(bf16[192,1024]{1,0:T(8,128)(2,1)S(1)} %collective-permute-done.11.refs_6_), channel_id=1, source_target_pairs={{0,8},{8,0},{16,24},{24,16},{1,9},{9,1},{17,25},{25,17},{2,10},{10... | collective-permute-start | bytes 1179656 | tf_op jit(solution)/shard_map/ppermute | solution.py:213
  66.5 5.3 %collective-permute-start.13 = (bf16[320,512]{1,0:T(8,128)(2,1)S(1)}, bf16[320,512]{1,0:T(8,128)(2,1)S(1)}, u32[]{:S(2)}, u32[]{:S(2)}) collective-permute-start(bf16[320,512]{1,0:T(8,128)(2,1)S(1)} %get-tuple-element.85), channel_id=1, source_target_pairs={{0,8},{8,0},{16,24},{24,16},{1,9},{9,1},{17,25},{25,17},{2,10},{10... | collective-permute-start | bytes 983048 | tf_op jit(solution)/shard_map/ppermute | solution.py:213
  71.7 1.5 %collective-permute-start.14 = (bf16[192,512]{1,0:T(8,128)(2,1)S(1)}, bf16[192,512]{1,0:T(8,128)(2,1)S(1)}, u32[]{:S(2)}, u32[]{:S(2)}) collective-permute-start(bf16[192,512]{1,0:T(8,128)(2,1)S(1)} %get-tuple-element.88), channel_id=1, source_target_pairs={{0,8},{8,0},{16,24},{24,16},{1,9},{9,1},{17,25},{25,17},{2,10},{10... | collective-permute-start | bytes 589832 | tf_op jit(solution)/shard_map/ppermute | solution.py:213

commit v4 on v3

--- a/solution.py
+++ b/solution.py
@@ -9,9 +9,10 @@
 from jax.sharding import PartitionSpec as P
 
 CORES = 2
-ROW_CUTS = (0, 5, 8)
+ROW_CUTS = (0, 6, 8)
 VMEM = pl.BlockSpec(memory_space=pltpu.VMEM)
 SMEM = pl.BlockSpec(memory_space=pltpu.SMEM)
+ANY = pl.BlockSpec(memory_space=pl.ANY)
 MASKED = -1e30
 LANES = 128
 PIECE = 256
@@ -19,11 +20,11 @@
 TN = (((0,), (0,)), ((), ()))
 
 
-def call(kernel, outs, ins, specs=None, out_specs=None, flops=0, scratch=(), limit=16, aliases=None, seconds=0):
+def call(kernel, outs, ins, specs=None, out_specs=None, flops=0, scratch=(), limit=16, aliases=None, seconds=0, grid=None):
     return pl.pallas_call(
         kernel,
         out_shape=outs,
-        grid=(1,) if specs else (),
+        grid=(1,) if specs and grid is None else (),
         in_specs=specs or [SMEM if a.dtype == jnp.int32 else VMEM for a in ins],
         out_specs=out_specs or jax.tree.map(lambda _: VMEM, outs),
         scratch_shapes=scratch,
@@ -49,7 +50,8 @@
     ).astype(picked_ref.dtype)
 
 
-def mix_own_kernel(index_ref, own_ref, edge_ref, partial_ref, outer_ref, dense_ref):
+def mix_kernel(index_ref, own_ref, edge_ref, arrived_ref, *refs):
+    *chunk_refs, mixed_ref, dense_ref, outer_ref = refs
     own = own_ref.shape[0]
     block_rows, chosen = index_ref.shape
     size = own // block_rows
@@ -64,16 +66,9 @@
                 dense_ref[rows, j * size : (j + 1) * size] = dense
             else:
                 outer_ref[rows, (j - block_rows) * size : (j - block_rows + 1) * size] = dense
-    partial_ref[...] = own_ref[...].astype(jnp.float32) + jnp.dot(
-        dense_ref[...], own_ref[...], preferred_element_type=jnp.float32
-    )
-
-
-def mix_outer_kernel(partial_ref, outer_ref, arrived_ref, *refs):
-    *chunk_refs, mixed_ref = refs
-    total = partial_ref[...] + jnp.dot(
-        outer_ref[...], arrived_ref[...], preferred_element_type=jnp.float32
-    )
+    total = own_ref[...].astype(jnp.float32)
+    total += jnp.dot(dense_ref[...], own_ref[...], preferred_element_type=jnp.float32)
+    total += jnp.dot(outer_ref[...], arrived_ref[...], preferred_element_type=jnp.float32)
     mixed = total.astype(mixed_ref.dtype)
     mixed_ref[...] = mixed
     at = 0
@@ -83,8 +78,12 @@
 
 
 def stack_kernel(*refs):
-    for i, ref in enumerate(refs[:-1]):
-        refs[-1][i] = ref[...]
+    *piece_refs, out_ref, sems = refs
+    copies = [pltpu.make_async_copy(ref, out_ref.at[i], sems.at[i]) for i, ref in enumerate(piece_refs)]
+    for copy in copies:
+        copy.start()
+    for copy in copies:
+        copy.wait()
 
 
 def relu_dot(left, right):
@@ -239,8 +238,8 @@
     size = heads * head_size
     unit = min(size, PIECE)
     count = size // unit
-    arrange = lambda group: call(
-        arrange_kernel, (shaped(count, unit, width), shaped(count, 2 * unit, width)), group
+    arrange = lambda group, seconds=0: call(
+        arrange_kernel, (shaped(count, unit, width), shaped(count, 2 * unit, width)), group, seconds=seconds
     )
 
     rows_list = send_rows[0, 0]
@@ -255,31 +254,25 @@
         picked.reshape(sources, most_rows, width), "vert", split_axis=0, concat_axis=0, tiled=True
     ).reshape(picked.shape)
 
-    edges = block_values[0].transpose(1, 0, 2)
-    outer_size = sources * most_rows
-    partial, outer = call(
-        mix_own_kernel,
-        (shaped(own, width, dtype=jnp.float32), shaped(own, outer_size)),
-        (block_index[0], inputs, edges),
-        flops=2 * own * own * width,
-        scratch=[pltpu.VMEM((own, own), jnp.bfloat16)],
-    )
-
     depth = graph_weight.shape[0]
     half = width // CORES
     piece = lax.dynamic_slice(graph_weight, (0, core * half), (depth, half))
     around = [turn(piece, "vert", 2 * d, parts) for d in range(1, parts // 2)]
-    around = call(stack_kernel, shaped(parts // 2, depth, half), (piece, *around), seconds=4e-6)
-    arrived, around, fetched, partial, outer = lax.optimization_barrier((arrived, around, fetched, partial, outer))
+    around = call(
+        stack_kernel, shaped(parts // 2, depth, half), (piece, *around),
+        specs=[ANY] * (parts // 2), grid=(), limit=16, seconds=4e-6,
+        scratch=[pltpu.SemaphoreType.DMA((parts // 2,))],
+    )
     across = swap_part(around, 1)
 
     cuts = [own * cut // ROW_CUTS[-1] for cut in ROW_CUTS]
     blocks = len(cuts) - 1
+    outer_size = sources * most_rows
     *chunks, mixed = call(
-        mix_outer_kernel,
+        mix_kernel,
         (*[shaped(b - a, width) for a, b in zip(cuts, cuts[1:])], shaped(own, width)),
-        (partial, outer, arrived),
-        flops=2 * outer.size * width,
+        (block_index[0], inputs, block_values[0].transpose(1, 0, 2), arrived),
+        scratch=[pltpu.VMEM((own, own), jnp.bfloat16), pltpu.VMEM((own, outer_size), jnp.bfloat16)],
     )
     lower = [
         [
@@ -303,9 +296,10 @@
     )
 
     owned, pairs = [], []
-    hidden, sibling, lower[0], groups = lax.optimization_barrier((hidden, sibling, lower[0], groups))
     for g in range(chips):
-        ask, pair = arranged if g == 0 else arrange(groups[g - 1])
+        if g == 1:
+            owned, lower[0], groups = lax.optimization_barrier((owned, lower[0], groups))
+        ask, pair = arranged if g == 0 else arrange(groups[g - 1], 12e-6)
         pairs.append(pair)
         owned.append(call(
             own_kernel,

time: 75.4 us -> 64.3 us (0.85)
  local copies, waits for them, and re-layouts: 11.1 us -> 3.19 us
  waiting for transfers between devices: 24.3 us -> 18.7 us
  Pallas kernels: 21.2 us -> 24.4 us
  starting transfers between devices: 18.1 us -> 17.3 us
    unnamed x30 -> x14, local copies, waits for them, and re-layouts: 8.68 us -> 0.75 us
    ppermute x2, waiting for transfers between devices: 8.35 us -> 3.42 us  [shards(): lax.ppermute(a, 'vert', [(i, i ^ bit) for i in range(parts)])]
    all_to_all x1, waiting for transfers between devices: 0.65 us -> 4.6 us  [shards(): lax.all_to_all(picked.reshape(sources, most_rows, width), 'vert', split_a...]
    ppermute x6, waiting for transfers between devices: 10.9 us -> 7.41 us  [shards(): lax.ppermute(a, axis, [(i, (i + by) % n) for i in range(n)])]
    pallas_call x12 -> x11, Pallas kernels: 21.2 us -> 24.4 us  [call(): pl.pallas_call(kernel, out_shape=outs, grid=(1,) if specs and grid is Non...]
    ppermute x6, starting transfers between devices: 11.6 us -> 10 us  [shards(): lax.ppermute(a, axis, [(i, (i + by) % n) for i in range(n)])]
    ppermute x7, waiting for transfers between devices: 4.43 us -> 3.3 us  [shards(): lax.ppermute(a, 'tm', [(i, i ^ 1) for i in range(steps)])]
  transfers between devices with their start and end apart: 16 -> 16, of which waited for: 9 -> 7; matrix products, arithmetic and copies ran while one was open for 3% -> 4% of each run, Pallas kernels for 23% -> 35%
where the time goes in v4:
time: 64.3 us; the launch traced here: 64 us
  Pallas kernels  24.4 us (38%)
  waiting for transfers between devices  18.7 us (29%)
  starting transfers between devices  17.3 us (27%)
  local copies, waits for them, and re-layouts  3.19 us (5%)
    pallas_call x11, Pallas kernels, call(): pl.pallas_call(kernel, out_shape=outs, grid=(1,) if specs and grid is Non...  24.4 us
    ppermute x6, starting transfers between devices, shards(): lax.ppermute(a, axis, [(i, (i + by) % n) for i in range(n)])  10 us
    ppermute x6, waiting for transfers between devices, shards(): lax.ppermute(a, axis, [(i, (i + by) % n) for i in range(n)])  7.41 us
    all_to_all x1, waiting for transfers between devices, shards(): lax.all_to_all(picked.reshape(sources, most_rows, width), 'vert', split_a...  4.6 us
    ppermute x2, waiting for transfers between devices, shards(): lax.ppermute(a, 'vert', [(i, i ^ bit) for i in range(parts)])  3.42 us
    all_to_all x1, starting transfers between devices, shards(): lax.all_to_all(picked.reshape(sources, most_rows, width), 'vert', split_a...  3.41 us
    ppermute x7, waiting for transfers between devices, shards(): lax.ppermute(a, 'tm', [(i, i ^ 1) for i in range(steps)])  3.3 us
    ppermute x2, starting transfers between devices, shards(): lax.ppermute(a, 'vert', [(i, i ^ bit) for i in range(parts)])  2.65 us
  transfers between devices with their start and end apart: 16, of which 7 were waited for; matrix products, arithmetic and copies ran while one was open for 4% of the time, Pallas kernels for 35%

profile of v4, /device:TPU:0, one launch (start us, length us, event | category | flops | bytes accessed | tf_op | source)
XLA Modules:
  0.0 64.0 jit_solution(15599917164070374837)
XLA Ops:
  0.1 0.1 stack.79.meta_ref
  0.2 0.7 %copy-done = bf16[128,1024]{1,0:T(8,128)(2,1)S(1)} copy-done((bf16[128,1024]{1,0:T(8,128)(2,1)S(1)}, bf16[128,1024]{1,0:T(8,128)(2,1)}, u32[]{:S(2)}) %copy-start) | copy-done | bytes 262168
  1.0 3.1 %collective-permute-start = (bf16[128,512]{1,0:T(8,128)(2,1)S(1)}, bf16[128,512]{1,0:T(8,128)(2,1)S(1)}, u32[]{:S(2)}, u32[]{:S(2)}) collective-permute-start(bf16[128,512]{1,0:T(8,128)(2,1)S(1)} %constant_dynamic-slice_fusion.1.refs_0_), channel_id=1, source_target_pairs={{0,2},{1,3},{2,4},{3,5},{4,6},{5,7},{6,0},{7,1},{8,10},{9,11},{10,... | collective-permute-start | bytes 393224 | tf_op jit(solution)/shard_map/ppermute | solution.py:214
  4.0 2.6 %collective-permute-start.1 = (bf16[128,512]{1,0:T(8,128)(2,1)S(1)}, bf16[128,512]{1,0:T(8,128)(2,1)S(1)}, u32[]{:S(2)}, u32[]{:S(2)}) collective-permute-start(bf16[128,512]{1,0:T(8,128)(2,1)S(1)} %constant_dynamic-slice_fusion.1.refs_0_), channel_id=1, source_target_pairs={{0,4},{1,5},{2,6},{3,7},{4,0},{5,1},{6,2},{7,3},{8,12},{9,13},{10,... | collective-permute-start | bytes 393224 | tf_op jit(solution)/shard_map/ppermute | solution.py:214
  6.6 1.3 %collective-permute-start.2 = (bf16[128,512]{1,0:T(8,128)(2,1)S(1)}, bf16[128,512]{1,0:T(8,128)(2,1)S(1)}, u32[]{:S(2)}, u32[]{:S(2)}) collective-permute-start(bf16[128,512]{1,0:T(8,128)(2,1)S(1)} %constant_dynamic-slice_fusion.1.refs_0_), channel_id=1, source_target_pairs={{0,6},{1,7},{2,0},{3,1},{4,2},{5,3},{6,4},{7,5},{8,14},{9,15},{10,... | collective-permute-start | bytes 393224 | tf_op jit(solution)/shard_map/ppermute | solution.py:214
  8.0 2.1 %constant_dynamic-slice_fusion = bf16[2,192,1024]{2,1,0:T(8,128)(2,1)} fusion(bf16[4,192,1024]{2,1,0:T(8,128)(2,1)} %refs_0_, s32[]{:T(128)S(6)} %select_n.62), kind=kLoop, calls=%fused_computation.1 | loop fusion | bytes 1572868 | tf_op jit(solution)/shard_map/dynamic_slice | solution.py:235
  10.1 1.5 %collective-permute-start.8 = (bf16[2,192,1024]{2,1,0:T(8,128)(2,1)}, bf16[2,192,1024]{2,1,0:T(8,128)(2,1)}, u32[]{:S(2)}, u32[]{:S(2)}) collective-permute-start(bf16[2,192,1024]{2,1,0:T(8,128)(2,1)} %constant_dynamic-slice_fusion), channel_id=1, source_target_pairs={{0,16},{8,24},{16,0},{24,8},{1,17},{9,25},{17,1},{25,9},{2,18},{10... | collective-permute-start | bytes 2359304 | tf_op jit(solution)/shard_map/ppermute | solution.py:214
  11.6 0.1 iota_compare_fusion
  11.7 0.1 lt.73
  11.7 0.1 squeeze.15
  11.8 1.0 %shard_map.74 = bf16[128,1024]{1,0:T(8,128)(2,1)} custom-call(s32[1,128]{1,0:T(1,128)S(1)} %broadcast_select_fusion.row_ref, bf16[512,1024]{1,0:T(8,128)(2,1)S(1)} %bitcast.29), custom_call_target="tpu_custom_call" | custom-call | tf_op jit(solution)/shard_map/pallas_call | solution.py:24
  12.9 3.4 %all-to-all-start = ((bf16[8,16,1024]{2,1,0:T(8,128)(2,1)}), bf16[8,16,1024]{2,1,0:T(8,128)(2,1)S(1)}, u32[]{:S(2)}, u32[]{:S(2)}) async-start(bf16[8,16,1024]{2,1,0:T(8,128)(2,1)} %bitcast.23), calls=%async_computation | async-start | bytes 524288 | tf_op jit(solution)/shard_map/all_to_all | solution.py:253
  16.3 0.1 copy.8
  16.4 1.5 %shard_map.73.refs_0_ = bf16[4,128,512]{2,1,0:T(8,128)(2,1)} custom-call(bf16[128,512]{1,0:T(8,128)(2,1)S(1)} %constant_dynamic-slice_fusion.1.refs_0_, bf16[128,512]{1,0:T(8,128)(2,1)S(1)} %collective-permute-done.refs_1_, bf16[128,512]{1,0:T(8,128)(2,1)S(1)} %collective-permute-done.1.refs_2_, bf16[128,512]{1,0:T(8,128)(2,1)S(1)} %collective-permute-done.2.refs_3_), custom_call_target="tpu_custom_call" | custom-call | flops 4000000000 | tf_op jit(solution)/shard_map/pallas_call | solution.py:24
  18.0 0.0 copy-start.2
  18.0 2.0 %collective-permute-start.4 = (bf16[4,128,512]{2,1,0:T(8,128)(2,1)}, bf16[4,128,512]{2,1,0:T(8,128)(2,1)}, u32[]{:S(2)}, u32[]{:S(2)}) collective-permute-start(bf16[4,128,512]{2,1,0:T(8,128)(2,1)} %shard_map.73.refs_0_), channel_id=1, source_target_pairs={{0,1},{1,0},{2,3},{3,2},{4,5},{5,4},{6,7},{7,6},{8,9},{9,8},{10,11... | collective-permute-start | bytes 1572872 | tf_op jit(solution)/shard_map/ppermute | solution.py:213
  20.0 4.6 %all-to-all-done = bf16[8,16,1024]{2,1,0:T(8,128)(2,1)S(1)} async-done(((bf16[8,16,1024]{2,1,0:T(8,128)(2,1)}), bf16[8,16,1024]{2,1,0:T(8,128)(2,1)S(1)}, u32[]{:S(2)}, u32[]{:S(2)}) %all-to-all-start) | async-done | bytes 262176 | tf_op jit(solution)/shard_map/all_to_all | solution.py:253
  24.6 1.6 %shard_map.75 = (bf16[384,1024]{1,0:T(8,128)(2,1)S(1)}, bf16[128,1024]{1,0:T(8,128)(2,1)S(1)}, bf16[512,1024]{1,0:T(8,128)(2,1)S(1)}) custom-call(s32[4,3]{1,0:T(4,128)S(1)} %bitcast.33, bf16[512,1024]{1,0:T(8,128)(2,1)S(1)} %bitcast.30, bf16[3,512,128]{2,1,0:T(8,128)(2,1)S(1)} %bitcast.32, bf16[128,1024]{1,0:T(8,128)(2,1)S(1)} %bitcast.31), custom_call_target="tpu_custom_call" | custom-call | tf_op jit(solution)/shard_map/pallas_call | solution.py:24
  26.2 0.1 collective-permute-start.6
  26.2 0.6 collective-permute-start.7
  26.9 2.0 %collective-permute-done.8.refs_0_ = bf16[2,192,1024]{2,1,0:T(8,128)(2,1)} collective-permute-done((bf16[2,192,1024]{2,1,0:T(8,128)(2,1)}, bf16[2,192,1024]{2,1,0:T(8,128)(2,1)}, u32[]{:S(2)}, u32[]{:S(2)}) %collective-permute-start.8) | collective-permute-done | bytes 786464 | tf_op jit(solution)/shard_map/ppermute | solution.py:214
  28.8 0.7 %collective-permute-start.9 = (bf16[2,192,1024]{2,1,0:T(8,128)(2,1)}, bf16[2,192,1024]{2,1,0:T(8,128)(2,1)S(1)}, u32[]{:S(2)}, u32[]{:S(2)}) collective-permute-start(bf16[2,192,1024]{2,1,0:T(8,128)(2,1)} %collective-permute-done.8.refs_0_), channel_id=1, source_target_pairs={{0,2},{1,3},{2,0},{3,1},{4,6},{5,7},{6,4},{7,5},{8,10},{9,11},{10,... | collective-permute-start | bytes 2359304 | tf_op jit(solution)/shard_map/ppermute | solution.py:213
  29.5 0.0 collective-permute-start.3
  29.5 0.1 shard_map.76
  29.6 3.4 %collective-permute-done.4.refs_2_ = bf16[4,128,512]{2,1,0:T(8,128)(2,1)} collective-permute-done((bf16[4,128,512]{2,1,0:T(8,128)(2,1)}, bf16[4,128,512]{2,1,0:T(8,128)(2,1)}, u32[]{:S(2)}, u32[]{:S(2)}) %collective-permute-start.4) | collective-permute-done | bytes 524320 | tf_op jit(solution)/shard_map/ppermute | solution.py:213
  33.0 0.0 collective-permute-start.5
  33.0 0.0 collective-permute-done.3.refs_1_
  33.0 0.9 %collective-permute-start.11 = (bf16[128,1024]{1,0:T(8,128)(2,1)S(1)}, bf16[128,1024]{1,0:T(8,128)(2,1)S(1)}, u32[]{:S(2)}, u32[]{:S(2)}) collective-permute-start(bf16[128,1024]{1,0:T(8,128)(2,1)S(1)} %get-tuple-element.70), channel_id=1, source_target_pairs={{0,16},{8,24},{16,0},{24,8},{1,17},{9,25},{17,1},{25,9},{2,18},{10... | collective-permute-start | bytes 786440 | tf_op jit(solution)/shard_map/ppermute | solution.py:214
  33.9 1.2 %collective-permute-done.5.refs_3_ = bf16[4,128,512]{2,1,0:T(8,128)(2,1)S(1)} collective-permute-done((bf16[4,128,512]{2,1,0:T(8,128)(2,1)}, bf16[4,128,512]{2,1,0:T(8,128)(2,1)S(1)}, u32[]{:S(2)}, u32[]{:S(2)}) %collective-permute-start.5) | collective-permute-done | bytes 524320 | tf_op jit(solution)/shard_map/ppermute | solution.py:212
  35.1 0.0 collective-permute-done.6.refs_5_
  35.1 3.7 %shard_map.77 = (bf16[1024,1024]{1,0:T(8,128)(2,1)S(1)}, bf16[512,1024]{1,0:T(8,128)(2,1)S(1)}, bf16[512,1024]{1,0:T(8,128)(2,1)S(1)}) custom-call(s32[18]{0:T(128)S(1)} %stack.79.meta_ref, bf16[4,128,512]{2,1,0:T(8,128)(2,1)} %shard_map.73.refs_0_, bf16[4,128,512]{2,1,0:T(8,128)(2,1)S(1)} %collective-permute-done.3.refs_1_, ...), custom_call_target="tpu_custom_call" | custom-call | tf_op jit(solution)/shard_map/pallas_call | solution.py:24
  38.8 2.4 %shard_map.78 = (bf16[2,1,512,256]{3,2,1,0:T(8,128)(2,1)S(1)}, bf16[2,1,512,512]{3,2,1,0:T(8,128)(2,1)S(1)}) custom-call(s32[18]{0:T(128)S(1)} %stack.79.meta_ref, bf16[512,1024]{1,0:T(8,128)(2,1)S(1)} %get-tuple-element.53.mine_ref.hidden_ref, bf16[512,1024]{1,0:T(8,128)(2,1)S(1)} %get-tuple-element.55.other_ref, ...), custom_call_target="tpu_custom_call" | custom-call | tf_op jit(solution)/shard_map/pallas_call | solution.py:24
  41.2 5.4 %collective-permute-done.7.refs_6_ = bf16[384,1024]{1,0:T(8,128)(2,1)S(1)} collective-permute-done((bf16[384,1024]{1,0:T(8,128)(2,1)S(1)}, bf16[384,1024]{1,0:T(8,128)(2,1)S(1)}, u32[]{:S(2)}, u32[]{:S(2)}) %collective-permute-start.7) | collective-permute-done | bytes 786464 | tf_op jit(solution)/shard_map/ppermute | solution.py:214
  46.6 0.0 collective-permute-done.9.refs_1_
  46.7 0.0 collective-permute-start.10
  46.7 1.2 %shard_map.79 = (bf16[1,256,1024]{2,1,0:T(8,128)(2,1)S(1)}, bf16[1,512,1024]{2,1,0:T(8,128)(2,1)S(1)}) custom-call(bf16[2,192,1024]{2,1,0:T(8,128)(2,1)} %collective-permute-done.8.refs_0_, bf16[2,192,1024]{2,1,0:T(8,128)(2,1)S(1)} %collective-permute-done.9.refs_1_), custom_call_target="tpu_custom_call" | custom-call | flops 12000000000 | tf_op jit(solution)/shard_map/pallas_call | solution.py:24
  47.9 2.4 %shard_map.80 = (bf16[2,1,512,256]{3,2,1,0:T(8,128)(2,1)S(1)}, bf16[2,1,512,512]{3,2,1,0:T(8,128)(2,1)S(1)}) custom-call(s32[18]{0:T(128)S(1)} %stack.79.meta_ref, bf16[512,1024]{1,0:T(8,128)(2,1)S(1)} %get-tuple-element.53.mine_ref.hidden_ref, bf16[512,1024]{1,0:T(8,128)(2,1)S(1)} %get-tuple-element.55.other_ref, ...), custom_call_target="tpu_custom_call" | custom-call | tf_op jit(solution)/shard_map/pallas_call | solution.py:24
  50.3 0.0 collective-permute-done.10.refs_7_
  50.3 6.0 %shard_map.81 = (bf16[384,512]{1,0:T(8,128)(2,1)S(1)}, bf16[384,512]{1,0:T(8,128)(2,1)S(1)}) custom-call(s32[18]{0:T(128)S(1)} %stack.79.meta_ref, bf16[1024,1024]{1,0:T(8,128)(2,1)S(1)} %get-tuple-element.54.weight_ref, bf16[1,512,1024]{2,1,0:T(8,128)(2,1)S(1)} %get-tuple-element.51.pair_ref.refs_0_, ...), custom_call_target="tpu_custom_call" | custom-call | tf_op jit(solution)/shard_map/pallas_call | solution.py:24
  56.3 0.0 collective-permute-done.11.refs_6_
  56.3 0.6 collective-permute-start.12
  56.9 0.1 collective-permute-start.13
  57.0 1.1 %collective-permute-done.12.refs_7_ = bf16[128,1024]{1,0:T(8,128)(2,1)S(1)} collective-permute-done((bf16[128,1024]{1,0:T(8,128)(2,1)S(1)}, bf16[128,1024]{1,0:T(8,128)(2,1)S(1)}, u32[]{:S(2)}, u32[]{:S(2)}) %collective-permute-start.12) | collective-permute-done | bytes 262176 | tf_op jit(solution)/shard_map/ppermute | solution.py:212
  58.1 2.6 %shard_map.82 = (bf16[128,512]{1,0:T(8,128)(2,1)S(1)}, bf16[128,512]{1,0:T(8,128)(2,1)S(1)}) custom-call(s32[18]{0:T(128)S(1)} %stack.79.meta_ref, bf16[1024,1024]{1,0:T(8,128)(2,1)S(1)} %get-tuple-element.54.weight_ref, bf16[1,512,1024]{2,1,0:T(8,128)(2,1)S(1)} %get-tuple-element.51.pair_ref.refs_0_, ...), custom_call_target="tpu_custom_call" | custom-call | tf_op jit(solution)/shard_map/pallas_call | solution.py:24
  60.7 0.4 collective-permute-start.14
  61.1 0.0 collective-permute-done.13.refs_2_
  61.1 1.0 %collective-permute-done.14.refs_3_ = bf16[128,512]{1,0:T(8,128)(2,1)S(1)} collective-permute-done((bf16[128,512]{1,0:T(8,128)(2,1)S(1)}, bf16[128,512]{1,0:T(8,128)(2,1)S(1)}, u32[]{:S(2)}, u32[]{:S(2)}) %collective-permute-start.14) | collective-permute-done | bytes 131104 | tf_op jit(solution)/shard_map/ppermute | solution.py:212
  62.1 1.9 %shard_map.83 = bf16[512,1024]{1,0:T(8,128)(2,1)} custom-call(s32[18]{0:T(128)S(1)} %stack.79.meta_ref, bf16[512,1024]{1,0:T(8,128)(2,1)S(1)} %get-tuple-element.53.mine_ref.hidden_ref, bf16[384,512]{1,0:T(8,128)(2,1)S(1)} %get-tuple-element.69.refs_0_, bf16[128,512]{1,0:T(8,128)(2,1)S(1)} %get-tuple-element.73.refs_1_, ...), custom_call_target="tpu_custom_call" | custom-call | tf_op jit(solution)/shard_map/pallas_call | solution.py:24
  (17 shorter events, 0.0 us)
Async XLA Ops:
  0.0 1.0 %copy-start = (bf16[128,1024]{1,0:T(8,128)(2,1)S(1)}, bf16[128,1024]{1,0:T(8,128)(2,1)}, u32[]{:S(2)}) copy-start(bf16[128,1024]{1,0:T(8,128)(2,1)} %param.8) | copy-start | bytes 786436
  0.0 11.8 %copy-start.1 = (bf16[1,512,1024]{2,1,0:T(8,128)(2,1)S(1)}, bf16[1,512,1024]{2,1,0:T(8,128)(2,1)}, u32[]{:S(2)}) copy-start(bf16[1,512,1024]{2,1,0:T(8,128)(2,1)} %param.7) | copy-start | bytes 3145732
  0.0 11.7 %copy-start.4 = (s32[1,1,8,16]{3,2,1,0:T(8,128)S(1)}, s32[1,1,8,16]{3,2,1,0:T(8,128)}, u32[]{:S(2)}) copy-start(s32[1,1,8,16]{3,2,1,0:T(8,128)} %param.10) | copy-start | bytes 1540
  0.0 11.6 %copy-start.6 = (s32[1,1,8]{2,1,0:T(1,128)S(1)}, s32[1,1,8]{2,1,0:T(1,128)}, u32[]{:S(2)}) copy-start(s32[1,1,8]{2,1,0:T(1,128)} %param.11) | copy-start | bytes 100
  1.0 15.4 %collective-permute-start = (bf16[128,512]{1,0:T(8,128)(2,1)S(1)}, bf16[128,512]{1,0:T(8,128)(2,1)S(1)}, u32[]{:S(2)}, u32[]{:S(2)}) collective-permute-start(bf16[128,512]{1,0:T(8,128)(2,1)S(1)} %constant_dynamic-slice_fusion.1.refs_0_), channel_id=1, source_target_pairs={{0,2},{1,3},{2,4},{3,5},{4,6},{5,7},{6,0},{7,1},{8,10},{9,11},{10,... | collective-permute-start | bytes 393224 | tf_op jit(solution)/shard_map/ppermute | solution.py:214
  4.0 12.4 %collective-permute-start.1 = (bf16[128,512]{1,0:T(8,128)(2,1)S(1)}, bf16[128,512]{1,0:T(8,128)(2,1)S(1)}, u32[]{:S(2)}, u32[]{:S(2)}) collective-permute-start(bf16[128,512]{1,0:T(8,128)(2,1)S(1)} %constant_dynamic-slice_fusion.1.refs_0_), channel_id=1, source_target_pairs={{0,4},{1,5},{2,6},{3,7},{4,0},{5,1},{6,2},{7,3},{8,12},{9,13},{10,... | collective-permute-start | bytes 393224 | tf_op jit(solution)/shard_map/ppermute | solution.py:214
  6.6 9.8 %collective-permute-start.2 = (bf16[128,512]{1,0:T(8,128)(2,1)S(1)}, bf16[128,512]{1,0:T(8,128)(2,1)S(1)}, u32[]{:S(2)}, u32[]{:S(2)}) collective-permute-start(bf16[128,512]{1,0:T(8,128)(2,1)S(1)} %constant_dynamic-slice_fusion.1.refs_0_), channel_id=1, source_target_pairs={{0,6},{1,7},{2,0},{3,1},{4,2},{5,3},{6,4},{7,5},{8,14},{9,15},{10,... | collective-permute-start | bytes 393224 | tf_op jit(solution)/shard_map/ppermute | solution.py:214
  8.0 8.3 %copy-start.5 = (s32[1,4,3]{1,0,2:T(1,128)S(1)}, s32[1,4,3]{1,0,2:T(1,128)}, u32[]{:S(2)}) copy-start(s32[1,4,3]{1,0,2:T(1,128)} %param.12) | copy-start | bytes 148
  10.1 18.8 %collective-permute-start.8 = (bf16[2,192,1024]{2,1,0:T(8,128)(2,1)}, bf16[2,192,1024]{2,1,0:T(8,128)(2,1)}, u32[]{:S(2)}, u32[]{:S(2)}) collective-permute-start(bf16[2,192,1024]{2,1,0:T(8,128)(2,1)} %constant_dynamic-slice_fusion), channel_id=1, source_target_pairs={{0,16},{8,24},{16,0},{24,8},{1,17},{9,25},{17,1},{25,9},{2,18},{10... | collective-permute-start | bytes 2359304 | tf_op jit(solution)/shard_map/ppermute | solution.py:214
  12.9 11.7 %all-to-all-start = ((bf16[8,16,1024]{2,1,0:T(8,128)(2,1)}), bf16[8,16,1024]{2,1,0:T(8,128)(2,1)S(1)}, u32[]{:S(2)}, u32[]{:S(2)}) async-start(bf16[8,16,1024]{2,1,0:T(8,128)(2,1)} %bitcast.23), calls=%async_computation | async-start | bytes 524288 | tf_op jit(solution)/shard_map/all_to_all | solution.py:253
  16.4 8.2 %copy-start.3 = (bf16[1,512,3,128]{3,1,2,0:T(8,128)(2,1)S(1)}, bf16[1,512,3,128]{3,1,2,0:T(8,128)(2,1)}, u32[]{:S(2)}) copy-start(bf16[1,512,3,128]{3,1,2,0:T(8,128)(2,1)} %param.13) | copy-start | bytes 1179652
  18.0 11.5 %copy-start.2 = (bf16[4,192,1024]{2,1,0:T(8,128)(2,1)S(1)}, bf16[4,192,1024]{2,1,0:T(8,128)(2,1)}, u32[]{:S(2)}) copy-start(bf16[4,192,1024]{2,1,0:T(8,128)(2,1)} %refs_0_) | copy-start | bytes 4718596
  18.0 15.0 %collective-permute-start.4 = (bf16[4,128,512]{2,1,0:T(8,128)(2,1)}, bf16[4,128,512]{2,1,0:T(8,128)(2,1)}, u32[]{:S(2)}, u32[]{:S(2)}) collective-permute-start(bf16[4,128,512]{2,1,0:T(8,128)(2,1)} %shard_map.73.refs_0_), channel_id=1, source_target_pairs={{0,1},{1,0},{2,3},{3,2},{4,5},{5,4},{6,7},{7,6},{8,9},{9,8},{10,11... | collective-permute-start | bytes 1572872 | tf_op jit(solution)/shard_map/ppermute | solution.py:213
  26.2 9.0 %collective-permute-start.6 = (bf16[512,1024]{1,0:T(8,128)(2,1)S(1)}, bf16[512,1024]{1,0:T(8,128)(2,1)S(1)}, u32[]{:S(2)}, u32[]{:S(2)}) collective-permute-start(bf16[512,1024]{1,0:T(8,128)(2,1)S(1)} %get-tuple-element.48.refs_4_), channel_id=1, source_target_pairs={{0,8},{8,0},{16,24},{24,16},{1,9},{9,1},{17,25},{25,17},{2,10},{10... | collective-permute-start | bytes 3145736 | tf_op jit(solution)/shard_map/ppermute | solution.py:212
  26.2 20.4 %collective-permute-start.7 = (bf16[384,1024]{1,0:T(8,128)(2,1)S(1)}, bf16[384,1024]{1,0:T(8,128)(2,1)S(1)}, u32[]{:S(2)}, u32[]{:S(2)}) collective-permute-start(bf16[384,1024]{1,0:T(8,128)(2,1)S(1)} %get-tuple-element.58), channel_id=1, source_target_pairs={{0,16},{8,24},{16,0},{24,8},{1,17},{9,25},{17,1},{25,9},{2,18},{10... | collective-permute-start | bytes 2359304 | tf_op jit(solution)/shard_map/ppermute | solution.py:214
  28.8 17.9 %collective-permute-start.9 = (bf16[2,192,1024]{2,1,0:T(8,128)(2,1)}, bf16[2,192,1024]{2,1,0:T(8,128)(2,1)S(1)}, u32[]{:S(2)}, u32[]{:S(2)}) collective-permute-start(bf16[2,192,1024]{2,1,0:T(8,128)(2,1)} %collective-permute-done.8.refs_0_), channel_id=1, source_target_pairs={{0,2},{1,3},{2,0},{3,1},{4,6},{5,7},{6,4},{7,5},{8,10},{9,11},{10,... | collective-permute-start | bytes 2359304 | tf_op jit(solution)/shard_map/ppermute | solution.py:213
  29.5 3.5 %collective-permute-start.3 = (bf16[4,128,512]{2,1,0:T(8,128)(2,1)}, bf16[4,128,512]{2,1,0:T(8,128)(2,1)S(1)}, u32[]{:S(2)}, u32[]{:S(2)}) collective-permute-start(bf16[4,128,512]{2,1,0:T(8,128)(2,1)} %shard_map.73.refs_0_), channel_id=1, source_target_pairs={{0,8},{8,0},{16,24},{24,16},{1,9},{9,1},{17,25},{25,17},{2,10},{10... | collective-permute-start | bytes 1572872 | tf_op jit(solution)/shard_map/ppermute | solution.py:212
  33.0 2.1 %collective-permute-start.5 = (bf16[4,128,512]{2,1,0:T(8,128)(2,1)}, bf16[4,128,512]{2,1,0:T(8,128)(2,1)S(1)}, u32[]{:S(2)}, u32[]{:S(2)}) collective-permute-start(bf16[4,128,512]{2,1,0:T(8,128)(2,1)} %collective-permute-done.4.refs_2_), channel_id=1, source_target_pairs={{0,8},{8,0},{16,24},{24,16},{1,9},{9,1},{17,25},{25,17},{2,10},{10... | collective-permute-start | bytes 1572872 | tf_op jit(solution)/shard_map/ppermute | solution.py:212
  33.0 23.3 %collective-permute-start.11 = (bf16[128,1024]{1,0:T(8,128)(2,1)S(1)}, bf16[128,1024]{1,0:T(8,128)(2,1)S(1)}, u32[]{:S(2)}, u32[]{:S(2)}) collective-permute-start(bf16[128,1024]{1,0:T(8,128)(2,1)S(1)} %get-tuple-element.70), channel_id=1, source_target_pairs={{0,16},{8,24},{16,0},{24,8},{1,17},{9,25},{17,1},{25,9},{2,18},{10... | collective-permute-start | bytes 786440 | tf_op jit(solution)/shard_map/ppermute | solution.py:214
  46.7 3.6 %collective-permute-start.10 = (bf16[384,1024]{1,0:T(8,128)(2,1)S(1)}, bf16[384,1024]{1,0:T(8,128)(2,1)S(1)}, u32[]{:S(2)}, u32[]{:S(2)}) collective-permute-start(bf16[384,1024]{1,0:T(8,128)(2,1)S(1)} %collective-permute-done.7.refs_6_), channel_id=1, source_target_pairs={{0,8},{8,0},{16,24},{24,16},{1,9},{9,1},{17,25},{25,17},{2,10},{10... | collective-permute-start | bytes 2359304 | tf_op jit(solution)/shard_map/ppermute | solution.py:212
  56.3 1.7 %collective-permute-start.12 = (bf16[128,1024]{1,0:T(8,128)(2,1)S(1)}, bf16[128,1024]{1,0:T(8,128)(2,1)S(1)}, u32[]{:S(2)}, u32[]{:S(2)}) collective-permute-start(bf16[128,1024]{1,0:T(8,128)(2,1)S(1)} %collective-permute-done.11.refs_6_), channel_id=1, source_target_pairs={{0,8},{8,0},{16,24},{24,16},{1,9},{9,1},{17,25},{25,17},{2,10},{10... | collective-permute-start | bytes 786440 | tf_op jit(solution)/shard_map/ppermute | solution.py:212
  56.9 4.2 %collective-permute-start.13 = (bf16[384,512]{1,0:T(8,128)(2,1)S(1)}, bf16[384,512]{1,0:T(8,128)(2,1)S(1)}, u32[]{:S(2)}, u32[]{:S(2)}) collective-permute-start(bf16[384,512]{1,0:T(8,128)(2,1)S(1)} %get-tuple-element.71), channel_id=1, source_target_pairs={{0,8},{8,0},{16,24},{24,16},{1,9},{9,1},{17,25},{25,17},{2,10},{10... | collective-permute-start | bytes 1179656 | tf_op jit(solution)/shard_map/ppermute | solution.py:212
  60.7 1.4 %collective-permute-start.14 = (bf16[128,512]{1,0:T(8,128)(2,1)S(1)}, bf16[128,512]{1,0:T(8,128)(2,1)S(1)}, u32[]{:S(2)}, u32[]{:S(2)}) collective-permute-start(bf16[128,512]{1,0:T(8,128)(2,1)S(1)} %get-tuple-element.74), channel_id=1, source_target_pairs={{0,8},{8,0},{16,24},{24,16},{1,9},{9,1},{17,25},{25,17},{2,10},{10... | collective-permute-start | bytes 393224 | tf_op jit(solution)/shard_map/ppermute | solution.py:212

commit v5 on v4

--- a/solution.py
+++ b/solution.py
@@ -105,103 +105,121 @@
     hidden_other_ref[...] = relu_dot(other_ref[...], weight_ref[...])
 
 
-def arrange_kernel(*refs):
-    *weight_refs, ask_ref, pair_ref = refs
-    width = ask_ref.shape[1]
-    head_size = weight_refs[0].shape[1] // 3
-    i = 0
-    for ref in weight_refs:
-        for j in range(ref.shape[0]):
-            piece, start = divmod(i * head_size, width)
-            here = slice(start, start + head_size)
-            ask_ref[piece, here, :] = ref[j, :head_size, :]
-            pair_ref[piece, here, :] = ref[j, head_size : 2 * head_size, :]
-            here = slice(width + start, width + start + head_size)
-            pair_ref[piece, here, :] = ref[j, 2 * head_size :, :]
-            i += 1
-
-
-def own_kernel(meta_ref, mine_ref, other_ref, ask_ref, pair_ref, query_ref, both_ref, stacked_ref):
+def arrange_kernel(heads_ref, rows_ref):
+    heads, head_rows, _ = heads_ref.shape
+    size = head_rows // 3
+    for h in range(heads):
+        for i in range(3):
+            start = (i * heads + h) * size
+            rows_ref[start : start + size, :] = heads_ref[h, i * size : (i + 1) * size, :]
+
+
+def own_kernel(meta_ref, mine_ref, other_ref, rows_ref, query_ref, both_ref, stacked_ref):
     rows = mine_ref.shape[0]
+    width = query_ref.shape[2]
     core = meta_ref[0]
     stacked_ref[:rows, :] = mine_ref[...]
     stacked_ref[rows:, :] = other_ref[...]
-    for p in range(ask_ref.shape[0]):
-        for weight_ref, out_ref in ((ask_ref, query_ref), (pair_ref, both_ref)):
-            packed = lax.dot_general(
-                stacked_ref[...], weight_ref[p], NT, preferred_element_type=jnp.float32
-            ).astype(jnp.bfloat16)
-            out_ref[core, p] = packed[:rows]
-            out_ref[1 - core, p] = packed[rows:]
-
-
-def attend_kernel(groups, head_size, start, meta_ref, weight_ref, *refs):
-    pair_refs, query_refs, both_refs = refs[:groups], refs[groups : 2 * groups], refs[2 * groups : 3 * groups]
-    *mixed_refs, mine_ref, other_ref, stacked_ref, attended_ref = refs[3 * groups :]
+    packed = lax.dot_general(
+        stacked_ref[...], rows_ref[...], NT, preferred_element_type=jnp.float32
+    ).astype(jnp.bfloat16)
+    for t, slot in enumerate((core, 1 - core)):
+        part = packed[t * rows : (t + 1) * rows]
+        query_ref[slot] = part[:, :width]
+        both_ref[slot] = part[:, width:]
+
+
+def arrange_own_kernel(meta_ref, mine_ref, other_ref, heads_ref, rows_ref, query_ref, both_ref, stacked_ref):
+    arrange_kernel(heads_ref, rows_ref)
+    own_kernel(meta_ref, mine_ref, other_ref, rows_ref, query_ref, both_ref, stacked_ref)
+
+
+def attend_kernel(lists, head_size, start, meta_ref, weight_ref, *refs):
+    total = sum(lists)
+    rows_refs, query_refs, both_refs = refs[:total], refs[total : 2 * total], refs[2 * total : 3 * total]
+    *mixed_refs, mine_ref, other_ref, stacked_ref, attended_ref = refs[3 * total :]
     rows = mine_ref.shape[0]
     here = slice(start, start + rows)
+    slot = lambda s: slice(s * rows, (s + 1) * rows)
     for s, ref in enumerate(mixed_refs):
-        stacked_ref[s * rows : (s + 1) * rows, :] = ref[...]
+        stacked_ref[slot(s), :] = ref[...]
     raised = relu_dot(stacked_ref[...], weight_ref[...])
     scale = head_size ** (-0.5)
     folded = math.frexp(scale)[0] == 0.5
     at = 0
-    for pair_ref, query_ref, both_ref in zip(pair_refs, query_refs, both_refs):
-        pieces, double, _ = pair_ref.shape
-        width = double // 2
-        group = lambda axis: lax.broadcasted_iota(jnp.int32, (width, width), axis) // head_size
+    for g, count in enumerate(lists):
+        members = range(sum(lists[:g]), sum(lists[: g + 1]))
+        packed = []
+        for m in members:
+            first = query_refs[m].shape[2]
+            packed.append(lax.dot_general(
+                raised, rows_refs[m][first:, :], NT, preferred_element_type=jnp.float32
+            ))
+        join = lambda parts: jnp.concatenate(parts, axis=1) if len(parts) > 1 else parts[0]
+        half = packed[0].shape[1] // 2
+        key = join([a[:, :half] for a in packed]).astype(jnp.bfloat16)
+        value = join([a[:, half:] for a in packed])
+        keys = [key[slot(s)] for s in range(len(mixed_refs))]
+        values = [value[slot(s)] for s in range(len(mixed_refs))]
+        keys += [join([both_refs[m][u, here, :half] for m in members]) for u in range(CORES)]
+        values += [
+            join([both_refs[m][u, here, half:] for m in members]).astype(jnp.float32) for u in range(CORES)
+        ]
+        size = key.shape[1]
+        group = lambda axis: lax.broadcasted_iota(jnp.int32, (size, size), axis) // head_size
         spread = jnp.where(group(0) == group(1), scale if folded else 1.0, 0.0).astype(jnp.bfloat16)
-        for p in range(pieces):
-            packed = lax.dot_general(raised, pair_ref[p], NT, preferred_element_type=jnp.float32)
-            lower = [packed[s * rows : (s + 1) * rows] for s in range(len(mixed_refs))]
-            keys = [a[:, :width].astype(jnp.bfloat16) for a in lower]
-            values = [a[:, width:] for a in lower]
-            keys += [both_ref[u, p, here, :width] for u in range(CORES)]
-            values += [both_ref[u, p, here, width:].astype(jnp.float32) for u in range(CORES)]
-            for t in range(CORES):
-                slots = len(lower) + t + 1
-                query = query_ref[t, p, here, :]
-                products = jnp.concatenate([query * key for key in keys[:slots]], axis=0)
-                scores = jnp.dot(products, spread, preferred_element_type=jnp.float32)
-                if not folded:
-                    scores *= scale
-                parts = [scores[u * rows : (u + 1) * rows] for u in range(slots)]
-                for u in range(len(lower)):
-                    parts[u] = jnp.where(meta_ref[1 + u // CORES] > 0, parts[u], MASKED)
-                top = functools.reduce(jnp.maximum, parts)
-                parts = [jnp.exp(part - top) for part in parts]
-                total = functools.reduce(jnp.add, [a * b for a, b in zip(parts, values)])
-                total *= 1.0 / functools.reduce(jnp.add, parts)
-                attended_ref[t, :, at : at + width] = total.astype(attended_ref.dtype)
-            at += width
+        for t in range(CORES):
+            slots = len(mixed_refs) + t + 1
+            query = join([query_refs[m][t, here, :] for m in members])
+            products = jnp.concatenate([query * k for k in keys[:slots]], axis=0)
+            scores = jnp.dot(products, spread, preferred_element_type=jnp.float32)
+            if not folded:
+                scores *= scale
+            parts = [scores[slot(u)] for u in range(slots)]
+            for u in range(len(mixed_refs)):
+                parts[u] = jnp.where(meta_ref[1 + u // CORES] > 0, parts[u], MASKED)
+            top = functools.reduce(jnp.maximum, parts)
+            parts = [jnp.exp(part - top) for part in parts]
+            result = functools.reduce(jnp.add, [a * b for a, b in zip(parts, values)])
+            result *= 1.0 / functools.reduce(jnp.add, parts)
+            attended_ref[t, :, at : at + size] = result.astype(attended_ref.dtype)
+        at += size
     mine_ref[...] = attended_ref[meta_ref[0]]
     other_ref[...] = attended_ref[1 - meta_ref[0]]
 
 
 def combine_kernel(blocks, pieces, base, meta_ref, hidden_ref, *refs):
-    out_ref = refs[-1]
+    *refs, out_ref, sum_ref, sems = refs
     width = refs[0].shape[1] // pieces
     lanes = width % LANES == 0
+    step = math.gcd(*[ref.shape[0] for ref in refs])
+    copies = []
     at = 0
     for r in range(blocks):
-        here = slice(at, at + refs[r].shape[0])
-        at = here.stop
-        whole = None if lanes else hidden_ref[here, :].astype(jnp.float32)
-        for half in range(CORES):
-            for p in range(pieces):
-                start = meta_ref[base + half * pieces + p] * width
-                attended = refs[half * blocks + r][:, p * width : (p + 1) * width]
-                if lanes:
-                    column = pl.ds(pl.multiple_of(start, width), width)
-                    total = hidden_ref[here, column].astype(jnp.float32) + attended.astype(jnp.float32)
-                    out_ref[here, column] = total.astype(out_ref.dtype)
-                else:
-                    shape = (width, out_ref.shape[1])
-                    spot = lax.broadcasted_iota(jnp.int32, shape, 0) + start
-                    spot = (spot == lax.broadcasted_iota(jnp.int32, shape, 1)).astype(jnp.bfloat16)
-                    whole += jnp.dot(attended, spot, preferred_element_type=jnp.float32)
-        if not lanes:
-            out_ref[here, :] = whole.astype(out_ref.dtype)
+        for first in range(0, refs[r].shape[0], step):
+            rows = slice(first, first + step)
+            here = slice(at, at + step)
+            whole = None if lanes else hidden_ref[here, :].astype(jnp.float32)
+            for half in range(CORES):
+                for p in range(pieces):
+                    start = meta_ref[base + half * pieces + p] * width
+                    attended = refs[half * blocks + r][rows, p * width : (p + 1) * width]
+                    if lanes:
+                        column = pl.ds(pl.multiple_of(start, width), width)
+                        total = hidden_ref[here, column].astype(jnp.float32) + attended.astype(jnp.float32)
+                        sum_ref[here, column] = total.astype(sum_ref.dtype)
+                    else:
+                        shape = (width, out_ref.shape[1])
+                        spot = lax.broadcasted_iota(jnp.int32, shape, 0) + start
+                        spot = (spot == lax.broadcasted_iota(jnp.int32, shape, 1)).astype(jnp.bfloat16)
+                        whole += jnp.dot(attended, spot, preferred_element_type=jnp.float32)
+            if not lanes:
+                sum_ref[here, :] = whole.astype(sum_ref.dtype)
+            copies.append(pltpu.make_async_copy(sum_ref.at[here], out_ref.at[here], sems.at[len(copies)]))
+            copies[-1].start()
+            at += step
+    for copy in copies:
+        copy.wait()
 
 
 def shards(sizes, features, graph_weight, head_weight, send_rows, send_count, block_index, block_values):
@@ -235,13 +253,6 @@
     sent = lax.dynamic_slice_in_dim(head_weight, share * (heads // shares), heads // shares, 0)
     fetched = [turn(sent, "tm", CORES * d, steps) for d in range(1, chips)]
 
-    size = heads * head_size
-    unit = min(size, PIECE)
-    count = size // unit
-    arrange = lambda group, seconds=0: call(
-        arrange_kernel, (shaped(count, unit, width), shaped(count, 2 * unit, width)), group, seconds=seconds
-    )
-
     rows_list = send_rows[0, 0]
     sources, most_rows = rows_list.shape
     live = jnp.arange(most_rows)[None, :] < send_count[0, 0][:, None]
@@ -281,11 +292,9 @@
         ]
         for chunk in chunks
     ]
-    arranged = arrange([after(head_weight, mixed)])
+    arranged = call(arrange_kernel, shaped(heads * head_rows, width), (after(head_weight, mixed),))
     across = after(across, arranged)
-    groups = []
-    for group in fetched:
-        groups.append([group, swap_part(group, 2)] if shared else [group])
+    groups = [[group, swap_part(group, 2)] if shared else [group] for group in fetched]
     weight, hidden, sibling = call(
         functools.partial(assemble_kernel, chips),
         (shaped(width, width), shaped(own, width), shaped(own, width)),
@@ -295,31 +304,40 @@
         flops=4 * own * width * width,
     )
 
-    owned, pairs = [], []
-    for g in range(chips):
-        if g == 1:
-            owned, lower[0], groups = lax.optimization_barrier((owned, lower[0], groups))
-        ask, pair = arranged if g == 0 else arrange(groups[g - 1], 12e-6)
-        pairs.append(pair)
-        owned.append(call(
-            own_kernel,
-            (shaped(CORES, count, own, unit), shaped(CORES, count, own, 2 * unit)),
-            (meta, hidden, sibling, ask, pair),
+    def place(weights, ready=None, seconds=0):
+        count = weights.shape[0] // 3 if ready else weights.shape[0] * head_size
+        outs = (shaped(CORES, own, count), shaped(CORES, own, 2 * count))
+        if not ready:
+            outs = (shaped(3 * count, width), *outs)
+        result = call(
+            own_kernel if ready else arrange_own_kernel,
+            outs,
+            (meta, hidden, sibling, weights),
+            seconds=seconds,
             scratch=[pltpu.VMEM((CORES * own, width), jnp.bfloat16)],
-        ))
-    queries, boths = zip(*owned)
-
-    total = sum(a.shape[1] * a.shape[3] for a in queries)
+        )
+        return (weights, *result) if ready else result
+
+    owned = [place(arranged, True)]
+    for group in groups:
+        group = list(group)
+        for i, weights in enumerate(group):
+            if i == len(group) - 1:
+                owned, lower[0], weights = lax.optimization_barrier((owned, lower[0], weights))
+            owned.append(place(weights, seconds=12e-6 if i == len(group) - 1 else 0))
+    lists = [1, *[len(group) for group in groups]]
+
+    total = chips * heads * head_size
     kept, got = [], []
-    token = owned[0]
+    token = owned[0][1]
     for r in range(blocks):
         rows = cuts[r + 1] - cuts[r]
         chunk = after(lower[r], token)
         mixed_rows = [a for b in chunk for a in (b, swap_core(b))]
         keep, send = token = call(
-            functools.partial(attend_kernel, chips, head_size, cuts[r]),
+            functools.partial(attend_kernel, lists, head_size, cuts[r]),
             (shaped(rows, total), shaped(rows, total)),
-            (meta, weight, *pairs, *queries, *boths, *mixed_rows),
+            (meta, weight, *[a[i] for i in range(3) for a in owned], *mixed_rows),
             limit=11 + len(mixed_rows) * rows * width // 2**17,
             flops=2 * len(mixed_rows) * rows * width * (2 * total + width),
             scratch=[
@@ -333,6 +351,11 @@
         functools.partial(combine_kernel, blocks, len(spots), meta.size - 2 * len(spots)),
         shaped(own, width),
         (meta, hidden, *kept, *got),
+        out_specs=ANY,
+        scratch=[
+            pltpu.VMEM((own, width), jnp.bfloat16),
+            pltpu.SemaphoreType.DMA((own // math.gcd(*[a.shape[0] for a in kept]),)),
+        ],
     )
     return combined[None]
 

time: 64.3 us -> 62.6 us (0.974)
  waiting for transfers between devices: 18.7 us -> 16.9 us
    ppermute x6, waiting for transfers between devices: 7.41 us -> 5 us  [shards(): lax.ppermute(a, axis, [(i, (i + by) % n) for i in range(n)])]
  transfers between devices with their start and end apart: 16 -> 16, of which waited for: 7 -> 8; matrix products, arithmetic and copies ran while one was open for 4% -> 4% of each run, Pallas kernels for 35% -> 37%
where the time goes in v5:
time: 62.6 us; the launch traced here: 62.3 us
  Pallas kernels  24.9 us (40%)
  starting transfers between devices  17 us (27%)
  waiting for transfers between devices  16.9 us (27%)
  local copies, waits for them, and re-layouts  3.19 us (5%)
    pallas_call x11, Pallas kernels, call(): pl.pallas_call(kernel, out_shape=outs, grid=(1,) if specs and grid is Non...  24.9 us
    ppermute x6, starting transfers between devices, shards(): lax.ppermute(a, axis, [(i, (i + by) % n) for i in range(n)])  10 us
    ppermute x6, waiting for transfers between devices, shards(): lax.ppermute(a, axis, [(i, (i + by) % n) for i in range(n)])  5 us
    all_to_all x1, waiting for transfers between devices, shards(): lax.all_to_all(picked.reshape(sources, most_rows, width), 'vert', split_a...  4.6 us
    ppermute x7, waiting for transfers between devices, shards(): lax.ppermute(a, 'tm', [(i, i ^ 1) for i in range(steps)])  3.93 us
    ppermute x2, waiting for transfers between devices, shards(): lax.ppermute(a, 'vert', [(i, i ^ bit) for i in range(parts)])  3.42 us
    all_to_all x1, starting transfers between devices, shards(): lax.all_to_all(picked.reshape(sources, most_rows, width), 'vert', split_a...  3.41 us
    ppermute x2, starting transfers between devices, shards(): lax.ppermute(a, 'vert', [(i, i ^ bit) for i in range(parts)])  2.65 us
  transfers between devices with their start and end apart: 16, of which 8 were waited for; matrix products, arithmetic and copies ran while one was open for 4% of the time, Pallas kernels for 37%

profile of v5, /device:TPU:0, one launch (start us, length us, event | category | flops | bytes accessed | tf_op | source)
XLA Modules:
  0.0 62.3 jit_solution(8982044698228138107)
XLA Ops:
  0.1 0.1 stack.79.meta_ref
  0.2 0.7 %copy-done = bf16[128,1024]{1,0:T(8,128)(2,1)S(1)} copy-done((bf16[128,1024]{1,0:T(8,128)(2,1)S(1)}, bf16[128,1024]{1,0:T(8,128)(2,1)}, u32[]{:S(2)}) %copy-start) | copy-done | bytes 262168
  1.0 3.1 %collective-permute-start = (bf16[128,512]{1,0:T(8,128)(2,1)S(1)}, bf16[128,512]{1,0:T(8,128)(2,1)S(1)}, u32[]{:S(2)}, u32[]{:S(2)}) collective-permute-start(bf16[128,512]{1,0:T(8,128)(2,1)S(1)} %constant_dynamic-slice_fusion.1.refs_0_), channel_id=1, source_target_pairs={{0,2},{1,3},{2,4},{3,5},{4,6},{5,7},{6,0},{7,1},{8,10},{9,11},{10,... | collective-permute-start | bytes 393224 | tf_op jit(solution)/shard_map/ppermute | solution.py:232
  4.0 2.6 %collective-permute-start.1 = (bf16[128,512]{1,0:T(8,128)(2,1)S(1)}, bf16[128,512]{1,0:T(8,128)(2,1)S(1)}, u32[]{:S(2)}, u32[]{:S(2)}) collective-permute-start(bf16[128,512]{1,0:T(8,128)(2,1)S(1)} %constant_dynamic-slice_fusion.1.refs_0_), channel_id=1, source_target_pairs={{0,4},{1,5},{2,6},{3,7},{4,0},{5,1},{6,2},{7,3},{8,12},{9,13},{10,... | collective-permute-start | bytes 393224 | tf_op jit(solution)/shard_map/ppermute | solution.py:232
  6.6 1.3 %collective-permute-start.2 = (bf16[128,512]{1,0:T(8,128)(2,1)S(1)}, bf16[128,512]{1,0:T(8,128)(2,1)S(1)}, u32[]{:S(2)}, u32[]{:S(2)}) collective-permute-start(bf16[128,512]{1,0:T(8,128)(2,1)S(1)} %constant_dynamic-slice_fusion.1.refs_0_), channel_id=1, source_target_pairs={{0,6},{1,7},{2,0},{3,1},{4,2},{5,3},{6,4},{7,5},{8,14},{9,15},{10,... | collective-permute-start | bytes 393224 | tf_op jit(solution)/shard_map/ppermute | solution.py:232
  8.0 2.1 %constant_dynamic-slice_fusion = bf16[2,192,1024]{2,1,0:T(8,128)(2,1)} fusion(bf16[4,192,1024]{2,1,0:T(8,128)(2,1)} %heads_ref, s32[]{:T(128)S(6)} %select_n.62), kind=kLoop, calls=%fused_computation.1 | loop fusion | bytes 1572868 | tf_op jit(solution)/shard_map/dynamic_slice | solution.py:253
  10.1 1.5 %collective-permute-start.7 = (bf16[2,192,1024]{2,1,0:T(8,128)(2,1)}, bf16[2,192,1024]{2,1,0:T(8,128)(2,1)}, u32[]{:S(2)}, u32[]{:S(2)}) collective-permute-start(bf16[2,192,1024]{2,1,0:T(8,128)(2,1)} %constant_dynamic-slice_fusion), channel_id=1, source_target_pairs={{0,16},{8,24},{16,0},{24,8},{1,17},{9,25},{17,1},{25,9},{2,18},{10... | collective-permute-start | bytes 2359304 | tf_op jit(solution)/shard_map/ppermute | solution.py:232
  11.6 0.1 iota_compare_fusion
  11.7 0.1 lt.73
  11.7 0.1 squeeze.15
  11.8 1.1 %shard_map.74 = bf16[128,1024]{1,0:T(8,128)(2,1)} custom-call(s32[1,128]{1,0:T(1,128)S(1)} %broadcast_select_fusion.row_ref, bf16[512,1024]{1,0:T(8,128)(2,1)S(1)} %bitcast.29), custom_call_target="tpu_custom_call" | custom-call | tf_op jit(solution)/shard_map/pallas_call | solution.py:24
  12.9 3.4 %all-to-all-start = ((bf16[8,16,1024]{2,1,0:T(8,128)(2,1)}), bf16[8,16,1024]{2,1,0:T(8,128)(2,1)S(1)}, u32[]{:S(2)}, u32[]{:S(2)}) async-start(bf16[8,16,1024]{2,1,0:T(8,128)(2,1)} %bitcast.23), calls=%async_computation | async-start | bytes 524288 | tf_op jit(solution)/shard_map/all_to_all | solution.py:264
  16.3 0.1 copy.8
  16.4 0.0 collective-permute-done.refs_1_
  16.4 0.0 collective-permute-done.1.refs_2_
  16.4 0.0 collective-permute-done.2.refs_3_
  16.4 1.6 %shard_map.73.refs_0_ = bf16[4,128,512]{2,1,0:T(8,128)(2,1)} custom-call(bf16[128,512]{1,0:T(8,128)(2,1)S(1)} %constant_dynamic-slice_fusion.1.refs_0_, bf16[128,512]{1,0:T(8,128)(2,1)S(1)} %collective-permute-done.refs_1_, bf16[128,512]{1,0:T(8,128)(2,1)S(1)} %collective-permute-done.1.refs_2_, bf16[128,512]{1,0:T(8,128)(2,1)S(1)} %collective-permute-done.2.refs_3_), custom_call_target="tpu_custom_call" | custom-call | flops 4000000000 | tf_op jit(solution)/shard_map/pallas_call | solution.py:24
  18.0 0.0 copy-start.2
  18.0 2.0 %collective-permute-start.4 = (bf16[4,128,512]{2,1,0:T(8,128)(2,1)}, bf16[4,128,512]{2,1,0:T(8,128)(2,1)}, u32[]{:S(2)}, u32[]{:S(2)}) collective-permute-start(bf16[4,128,512]{2,1,0:T(8,128)(2,1)} %shard_map.73.refs_0_), channel_id=1, source_target_pairs={{0,1},{1,0},{2,3},{3,2},{4,5},{5,4},{6,7},{7,6},{8,9},{9,8},{10,11... | collective-permute-start | bytes 1572872 | tf_op jit(solution)/shard_map/ppermute | solution.py:231
  20.0 4.6 %all-to-all-done = bf16[8,16,1024]{2,1,0:T(8,128)(2,1)S(1)} async-done(((bf16[8,16,1024]{2,1,0:T(8,128)(2,1)}), bf16[8,16,1024]{2,1,0:T(8,128)(2,1)S(1)}, u32[]{:S(2)}, u32[]{:S(2)}) %all-to-all-start) | async-done | bytes 262176 | tf_op jit(solution)/shard_map/all_to_all | solution.py:264
  24.6 1.6 %shard_map.75 = (bf16[384,1024]{1,0:T(8,128)(2,1)S(1)}, bf16[128,1024]{1,0:T(8,128)(2,1)S(1)}, bf16[512,1024]{1,0:T(8,128)(2,1)S(1)}) custom-call(s32[4,3]{1,0:T(4,128)S(1)} %bitcast.33, bf16[512,1024]{1,0:T(8,128)(2,1)S(1)} %bitcast.30, bf16[3,512,128]{2,1,0:T(8,128)(2,1)S(1)} %bitcast.32, bf16[128,1024]{1,0:T(8,128)(2,1)S(1)} %bitcast.31), custom_call_target="tpu_custom_call" | custom-call | tf_op jit(solution)/shard_map/pallas_call | solution.py:24
  26.2 0.1 collective-permute-start.6
  26.2 0.6 collective-permute-start.8
  26.9 2.0 %collective-permute-done.7.heads_ref = bf16[2,192,1024]{2,1,0:T(8,128)(2,1)} collective-permute-done((bf16[2,192,1024]{2,1,0:T(8,128)(2,1)}, bf16[2,192,1024]{2,1,0:T(8,128)(2,1)}, u32[]{:S(2)}, u32[]{:S(2)}) %collective-permute-start.7) | collective-permute-done | bytes 786464 | tf_op jit(solution)/shard_map/ppermute | solution.py:232
  28.8 0.7 %collective-permute-start.9 = (bf16[2,192,1024]{2,1,0:T(8,128)(2,1)}, bf16[2,192,1024]{2,1,0:T(8,128)(2,1)S(1)}, u32[]{:S(2)}, u32[]{:S(2)}) collective-permute-start(bf16[2,192,1024]{2,1,0:T(8,128)(2,1)} %collective-permute-done.7.heads_ref), channel_id=1, source_target_pairs={{0,2},{1,3},{2,0},{3,1},{4,6},{5,7},{6,4},{7,5},{8,10},{9,11},{10,... | collective-permute-start | bytes 2359304 | tf_op jit(solution)/shard_map/ppermute | solution.py:231
  29.5 0.0 collective-permute-start.3
  29.5 0.1 shard_map.76.rows_ref.refs_0_
  29.6 3.4 %collective-permute-done.4.refs_2_ = bf16[4,128,512]{2,1,0:T(8,128)(2,1)} collective-permute-done((bf16[4,128,512]{2,1,0:T(8,128)(2,1)}, bf16[4,128,512]{2,1,0:T(8,128)(2,1)}, u32[]{:S(2)}, u32[]{:S(2)}) %collective-permute-start.4) | collective-permute-done | bytes 524320 | tf_op jit(solution)/shard_map/ppermute | solution.py:231
  33.0 0.0 collective-permute-start.5
  33.0 0.0 collective-permute-done.3.refs_1_
  33.0 0.9 %collective-permute-start.11 = (bf16[128,1024]{1,0:T(8,128)(2,1)S(1)}, bf16[128,1024]{1,0:T(8,128)(2,1)S(1)}, u32[]{:S(2)}, u32[]{:S(2)}) collective-permute-start(bf16[128,1024]{1,0:T(8,128)(2,1)S(1)} %get-tuple-element.76), channel_id=1, source_target_pairs={{0,16},{8,24},{16,0},{24,8},{1,17},{9,25},{17,1},{25,9},{2,18},{10... | collective-permute-start | bytes 786440 | tf_op jit(solution)/shard_map/ppermute | solution.py:232
  33.9 1.2 %collective-permute-done.5.refs_3_ = bf16[4,128,512]{2,1,0:T(8,128)(2,1)S(1)} collective-permute-done((bf16[4,128,512]{2,1,0:T(8,128)(2,1)}, bf16[4,128,512]{2,1,0:T(8,128)(2,1)S(1)}, u32[]{:S(2)}, u32[]{:S(2)}) %collective-permute-start.5) | collective-permute-done | bytes 524320 | tf_op jit(solution)/shard_map/ppermute | solution.py:230
  35.1 3.7 %shard_map.77 = (bf16[1024,1024]{1,0:T(8,128)(2,1)S(1)}, bf16[512,1024]{1,0:T(8,128)(2,1)S(1)}, bf16[512,1024]{1,0:T(8,128)(2,1)S(1)}) custom-call(s32[18]{0:T(128)S(1)} %stack.79.meta_ref, bf16[4,128,512]{2,1,0:T(8,128)(2,1)} %shard_map.73.refs_0_, bf16[4,128,512]{2,1,0:T(8,128)(2,1)S(1)} %collective-permute-done.3.refs_1_, ...), custom_call_target="tpu_custom_call" | custom-call | tf_op jit(solution)/shard_map/pallas_call | solution.py:24
  38.8 2.4 %shard_map.78 = (bf16[2,512,256]{2,1,0:T(8,128)(2,1)S(1)}, bf16[2,512,512]{2,1,0:T(8,128)(2,1)S(1)}) custom-call(s32[18]{0:T(128)S(1)} %stack.79.meta_ref, bf16[512,1024]{1,0:T(8,128)(2,1)S(1)} %get-tuple-element.54.mine_ref.hidden_ref, bf16[512,1024]{1,0:T(8,128)(2,1)S(1)} %get-tuple-element.56.other_ref, bf16[768,1024]{1,0:T(8,128)(2,1)S(1)} %shard_map.76.rows_ref.refs_0_), custom_call_target="tpu_custom_call" | custom-call | tf_op jit(solution)/shard_map/pallas_call | solution.py:24
  41.2 2.4 %shard_map.79 = (bf16[384,1024]{1,0:T(8,128)(2,1)S(1)}, bf16[2,512,128]{2,1,0:T(8,128)(2,1)S(1)}, bf16[2,512,256]{2,1,0:T(8,128)(2,1)S(1)}) custom-call(s32[18]{0:T(128)S(1)} %stack.79.meta_ref, bf16[512,1024]{1,0:T(8,128)(2,1)S(1)} %get-tuple-element.54.mine_ref.hidden_ref, bf16[512,1024]{1,0:T(8,128)(2,1)S(1)} %get-tuple-element.56.other_ref, ...), custom_call_target="tpu_custom_call" | custom-call | tf_op jit(solution)/shard_map/pallas_call | solution.py:24
  43.6 3.0 %collective-permute-done.8.refs_9_ = bf16[384,1024]{1,0:T(8,128)(2,1)S(1)} collective-permute-done((bf16[384,1024]{1,0:T(8,128)(2,1)S(1)}, bf16[384,1024]{1,0:T(8,128)(2,1)S(1)}, u32[]{:S(2)}, u32[]{:S(2)}) %collective-permute-start.8) | collective-permute-done | bytes 786464 | tf_op jit(solution)/shard_map/ppermute | solution.py:232
  46.7 0.0 collective-permute-done.9.heads_ref
  46.7 0.0 collective-permute-start.10
  46.7 1.8 %shard_map.80 = (bf16[384,1024]{1,0:T(8,128)(2,1)S(1)}, bf16[2,512,128]{2,1,0:T(8,128)(2,1)S(1)}, bf16[2,512,256]{2,1,0:T(8,128)(2,1)S(1)}) custom-call(s32[18]{0:T(128)S(1)} %stack.79.meta_ref, bf16[512,1024]{1,0:T(8,128)(2,1)S(1)} %get-tuple-element.54.mine_ref.hidden_ref, bf16[512,1024]{1,0:T(8,128)(2,1)S(1)} %get-tuple-element.56.other_ref, ...), custom_call_target="tpu_custom_call" | custom-call | flops 12000000000 | tf_op jit(solution)/shard_map/pallas_call | solution.py:24
  48.5 0.5 collective-permute-done.10.refs_10_
  49.0 6.0 %shard_map.81 = (bf16[384,512]{1,0:T(8,128)(2,1)S(1)}, bf16[384,512]{1,0:T(8,128)(2,1)S(1)}) custom-call(s32[18]{0:T(128)S(1)} %stack.79.meta_ref, bf16[1024,1024]{1,0:T(8,128)(2,1)S(1)} %get-tuple-element.55.weight_ref, bf16[768,1024]{1,0:T(8,128)(2,1)S(1)} %shard_map.76.rows_ref.refs_0_, bf16[384,1024]{1,0:T(8,128)(2,1)S(1)} %get-tuple-element.64.refs_1_, ...), custom_call_target="tpu_custom_call" | custom-call | tf_op jit(solution)/shard_map/pallas_call | solution.py:24
  55.0 0.2 collective-permute-start.12
  55.2 0.4 collective-permute-start.13
  55.6 1.0 %collective-permute-done.12.refs_10_ = bf16[128,1024]{1,0:T(8,128)(2,1)S(1)} collective-permute-done((bf16[128,1024]{1,0:T(8,128)(2,1)S(1)}, bf16[128,1024]{1,0:T(8,128)(2,1)S(1)}, u32[]{:S(2)}, u32[]{:S(2)}) %collective-permute-start.12) | collective-permute-done | bytes 262176 | tf_op jit(solution)/shard_map/ppermute | solution.py:230
  56.6 2.6 %shard_map.82 = (bf16[128,512]{1,0:T(8,128)(2,1)S(1)}, bf16[128,512]{1,0:T(8,128)(2,1)S(1)}) custom-call(s32[18]{0:T(128)S(1)} %stack.79.meta_ref, bf16[1024,1024]{1,0:T(8,128)(2,1)S(1)} %get-tuple-element.55.weight_ref, bf16[768,1024]{1,0:T(8,128)(2,1)S(1)} %shard_map.76.rows_ref.refs_0_, bf16[384,1024]{1,0:T(8,128)(2,1)S(1)} %get-tuple-element.64.refs_1_, ...), custom_call_target="tpu_custom_call" | custom-call | tf_op jit(solution)/shard_map/pallas_call | solution.py:24
  59.2 0.2 collective-permute-start.14
  59.4 1.2 %collective-permute-done.14.refs_3_ = bf16[128,512]{1,0:T(8,128)(2,1)S(1)} collective-permute-done((bf16[128,512]{1,0:T(8,128)(2,1)S(1)}, bf16[128,512]{1,0:T(8,128)(2,1)S(1)}, u32[]{:S(2)}, u32[]{:S(2)}) %collective-permute-start.14) | collective-permute-done | bytes 131104 | tf_op jit(solution)/shard_map/ppermute | solution.py:230
  60.7 1.6 %shard_map.83 = bf16[512,1024]{1,0:T(8,128)(2,1)} custom-call(s32[18]{0:T(128)S(1)} %stack.79.meta_ref, bf16[512,1024]{1,0:T(8,128)(2,1)S(1)} %get-tuple-element.54.mine_ref.hidden_ref, bf16[384,512]{1,0:T(8,128)(2,1)S(1)} %get-tuple-element.75.refs_0_, bf16[128,512]{1,0:T(8,128)(2,1)S(1)} %get-tuple-element.79.refs_1_, ...), custom_call_target="tpu_custom_call" | custom-call | tf_op jit(solution)/shard_map/pallas_call | solution.py:24
  (17 shorter events, 0.0 us)
Async XLA Ops:
  0.0 1.0 %copy-start = (bf16[128,1024]{1,0:T(8,128)(2,1)S(1)}, bf16[128,1024]{1,0:T(8,128)(2,1)}, u32[]{:S(2)}) copy-start(bf16[128,1024]{1,0:T(8,128)(2,1)} %param.8) | copy-start | bytes 786436
  0.0 11.8 %copy-start.1 = (bf16[1,512,1024]{2,1,0:T(8,128)(2,1)S(1)}, bf16[1,512,1024]{2,1,0:T(8,128)(2,1)}, u32[]{:S(2)}) copy-start(bf16[1,512,1024]{2,1,0:T(8,128)(2,1)} %param.7) | copy-start | bytes 3145732
  0.0 11.7 %copy-start.4 = (s32[1,1,8,16]{3,2,1,0:T(8,128)S(1)}, s32[1,1,8,16]{3,2,1,0:T(8,128)}, u32[]{:S(2)}) copy-start(s32[1,1,8,16]{3,2,1,0:T(8,128)} %param.10) | copy-start | bytes 1540
  0.0 11.6 %copy-start.6 = (s32[1,1,8]{2,1,0:T(1,128)S(1)}, s32[1,1,8]{2,1,0:T(1,128)}, u32[]{:S(2)}) copy-start(s32[1,1,8]{2,1,0:T(1,128)} %param.11) | copy-start | bytes 100
  1.0 15.5 %collective-permute-start = (bf16[128,512]{1,0:T(8,128)(2,1)S(1)}, bf16[128,512]{1,0:T(8,128)(2,1)S(1)}, u32[]{:S(2)}, u32[]{:S(2)}) collective-permute-start(bf16[128,512]{1,0:T(8,128)(2,1)S(1)} %constant_dynamic-slice_fusion.1.refs_0_), channel_id=1, source_target_pairs={{0,2},{1,3},{2,4},{3,5},{4,6},{5,7},{6,0},{7,1},{8,10},{9,11},{10,... | collective-permute-start | bytes 393224 | tf_op jit(solution)/shard_map/ppermute | solution.py:232
  4.0 12.4 %collective-permute-start.1 = (bf16[128,512]{1,0:T(8,128)(2,1)S(1)}, bf16[128,512]{1,0:T(8,128)(2,1)S(1)}, u32[]{:S(2)}, u32[]{:S(2)}) collective-permute-start(bf16[128,512]{1,0:T(8,128)(2,1)S(1)} %constant_dynamic-slice_fusion.1.refs_0_), channel_id=1, source_target_pairs={{0,4},{1,5},{2,6},{3,7},{4,0},{5,1},{6,2},{7,3},{8,12},{9,13},{10,... | collective-permute-start | bytes 393224 | tf_op jit(solution)/shard_map/ppermute | solution.py:232
  6.6 9.8 %collective-permute-start.2 = (bf16[128,512]{1,0:T(8,128)(2,1)S(1)}, bf16[128,512]{1,0:T(8,128)(2,1)S(1)}, u32[]{:S(2)}, u32[]{:S(2)}) collective-permute-start(bf16[128,512]{1,0:T(8,128)(2,1)S(1)} %constant_dynamic-slice_fusion.1.refs_0_), channel_id=1, source_target_pairs={{0,6},{1,7},{2,0},{3,1},{4,2},{5,3},{6,4},{7,5},{8,14},{9,15},{10,... | collective-permute-start | bytes 393224 | tf_op jit(solution)/shard_map/ppermute | solution.py:232
  8.0 8.3 %copy-start.5 = (s32[1,4,3]{1,0,2:T(1,128)S(1)}, s32[1,4,3]{1,0,2:T(1,128)}, u32[]{:S(2)}) copy-start(s32[1,4,3]{1,0,2:T(1,128)} %param.12) | copy-start | bytes 148
  10.1 18.8 %collective-permute-start.7 = (bf16[2,192,1024]{2,1,0:T(8,128)(2,1)}, bf16[2,192,1024]{2,1,0:T(8,128)(2,1)}, u32[]{:S(2)}, u32[]{:S(2)}) collective-permute-start(bf16[2,192,1024]{2,1,0:T(8,128)(2,1)} %constant_dynamic-slice_fusion), channel_id=1, source_target_pairs={{0,16},{8,24},{16,0},{24,8},{1,17},{9,25},{17,1},{25,9},{2,18},{10... | collective-permute-start | bytes 2359304 | tf_op jit(solution)/shard_map/ppermute | solution.py:232
  12.9 11.7 %all-to-all-start = ((bf16[8,16,1024]{2,1,0:T(8,128)(2,1)}), bf16[8,16,1024]{2,1,0:T(8,128)(2,1)S(1)}, u32[]{:S(2)}, u32[]{:S(2)}) async-start(bf16[8,16,1024]{2,1,0:T(8,128)(2,1)} %bitcast.23), calls=%async_computation | async-start | bytes 524288 | tf_op jit(solution)/shard_map/all_to_all | solution.py:264
  16.4 8.2 %copy-start.3 = (bf16[1,512,3,128]{3,1,2,0:T(8,128)(2,1)S(1)}, bf16[1,512,3,128]{3,1,2,0:T(8,128)(2,1)}, u32[]{:S(2)}) copy-start(bf16[1,512,3,128]{3,1,2,0:T(8,128)(2,1)} %param.13) | copy-start | bytes 1179652
  18.0 11.5 %copy-start.2 = (bf16[4,192,1024]{2,1,0:T(8,128)(2,1)S(1)}, bf16[4,192,1024]{2,1,0:T(8,128)(2,1)}, u32[]{:S(2)}) copy-start(bf16[4,192,1024]{2,1,0:T(8,128)(2,1)} %heads_ref) | copy-start | bytes 4718596
  18.0 15.0 %collective-permute-start.4 = (bf16[4,128,512]{2,1,0:T(8,128)(2,1)}, bf16[4,128,512]{2,1,0:T(8,128)(2,1)}, u32[]{:S(2)}, u32[]{:S(2)}) collective-permute-start(bf16[4,128,512]{2,1,0:T(8,128)(2,1)} %shard_map.73.refs_0_), channel_id=1, source_target_pairs={{0,1},{1,0},{2,3},{3,2},{4,5},{5,4},{6,7},{7,6},{8,9},{9,8},{10,11... | collective-permute-start | bytes 1572872 | tf_op jit(solution)/shard_map/ppermute | solution.py:231
  26.2 9.0 %collective-permute-start.6 = (bf16[512,1024]{1,0:T(8,128)(2,1)S(1)}, bf16[512,1024]{1,0:T(8,128)(2,1)S(1)}, u32[]{:S(2)}, u32[]{:S(2)}) collective-permute-start(bf16[512,1024]{1,0:T(8,128)(2,1)S(1)} %get-tuple-element.51.refs_4_), channel_id=1, source_target_pairs={{0,8},{8,0},{16,24},{24,16},{1,9},{9,1},{17,25},{25,17},{2,10},{10... | collective-permute-start | bytes 3145736 | tf_op jit(solution)/shard_map/ppermute | solution.py:230
  26.2 20.4 %collective-permute-start.8 = (bf16[384,1024]{1,0:T(8,128)(2,1)S(1)}, bf16[384,1024]{1,0:T(8,128)(2,1)S(1)}, u32[]{:S(2)}, u32[]{:S(2)}) collective-permute-start(bf16[384,1024]{1,0:T(8,128)(2,1)S(1)} %get-tuple-element.62), channel_id=1, source_target_pairs={{0,16},{8,24},{16,0},{24,8},{1,17},{9,25},{17,1},{25,9},{2,18},{10... | collective-permute-start | bytes 2359304 | tf_op jit(solution)/shard_map/ppermute | solution.py:232
  28.8 17.9 %collective-permute-start.9 = (bf16[2,192,1024]{2,1,0:T(8,128)(2,1)}, bf16[2,192,1024]{2,1,0:T(8,128)(2,1)S(1)}, u32[]{:S(2)}, u32[]{:S(2)}) collective-permute-start(bf16[2,192,1024]{2,1,0:T(8,128)(2,1)} %collective-permute-done.7.heads_ref), channel_id=1, source_target_pairs={{0,2},{1,3},{2,0},{3,1},{4,6},{5,7},{6,4},{7,5},{8,10},{9,11},{10,... | collective-permute-start | bytes 2359304 | tf_op jit(solution)/shard_map/ppermute | solution.py:231
  29.5 3.5 %collective-permute-start.3 = (bf16[4,128,512]{2,1,0:T(8,128)(2,1)}, bf16[4,128,512]{2,1,0:T(8,128)(2,1)S(1)}, u32[]{:S(2)}, u32[]{:S(2)}) collective-permute-start(bf16[4,128,512]{2,1,0:T(8,128)(2,1)} %shard_map.73.refs_0_), channel_id=1, source_target_pairs={{0,8},{8,0},{16,24},{24,16},{1,9},{9,1},{17,25},{25,17},{2,10},{10... | collective-permute-start | bytes 1572872 | tf_op jit(solution)/shard_map/ppermute | solution.py:230
  33.0 2.1 %collective-permute-start.5 = (bf16[4,128,512]{2,1,0:T(8,128)(2,1)}, bf16[4,128,512]{2,1,0:T(8,128)(2,1)S(1)}, u32[]{:S(2)}, u32[]{:S(2)}) collective-permute-start(bf16[4,128,512]{2,1,0:T(8,128)(2,1)} %collective-permute-done.4.refs_2_), channel_id=1, source_target_pairs={{0,8},{8,0},{16,24},{24,16},{1,9},{9,1},{17,25},{25,17},{2,10},{10... | collective-permute-start | bytes 1572872 | tf_op jit(solution)/shard_map/ppermute | solution.py:230
  33.0 22.0 %collective-permute-start.11 = (bf16[128,1024]{1,0:T(8,128)(2,1)S(1)}, bf16[128,1024]{1,0:T(8,128)(2,1)S(1)}, u32[]{:S(2)}, u32[]{:S(2)}) collective-permute-start(bf16[128,1024]{1,0:T(8,128)(2,1)S(1)} %get-tuple-element.76), channel_id=1, source_target_pairs={{0,16},{8,24},{16,0},{24,8},{1,17},{9,25},{17,1},{25,9},{2,18},{10... | collective-permute-start | bytes 786440 | tf_op jit(solution)/shard_map/ppermute | solution.py:232
  46.7 2.3 %collective-permute-start.10 = (bf16[384,1024]{1,0:T(8,128)(2,1)S(1)}, bf16[384,1024]{1,0:T(8,128)(2,1)S(1)}, u32[]{:S(2)}, u32[]{:S(2)}) collective-permute-start(bf16[384,1024]{1,0:T(8,128)(2,1)S(1)} %collective-permute-done.8.refs_9_), channel_id=1, source_target_pairs={{0,8},{8,0},{16,24},{24,16},{1,9},{9,1},{17,25},{25,17},{2,10},{10... | collective-permute-start | bytes 2359304 | tf_op jit(solution)/shard_map/ppermute | solution.py:230
  55.0 1.6 %collective-permute-start.12 = (bf16[128,1024]{1,0:T(8,128)(2,1)S(1)}, bf16[128,1024]{1,0:T(8,128)(2,1)S(1)}, u32[]{:S(2)}, u32[]{:S(2)}) collective-permute-start(bf16[128,1024]{1,0:T(8,128)(2,1)S(1)} %collective-permute-done.11.refs_9_), channel_id=1, source_target_pairs={{0,8},{8,0},{16,24},{24,16},{1,9},{9,1},{17,25},{25,17},{2,10},{10... | collective-permute-start | bytes 786440 | tf_op jit(solution)/shard_map/ppermute | solution.py:230
  55.2 4.3 %collective-permute-start.13 = (bf16[384,512]{1,0:T(8,128)(2,1)S(1)}, bf16[384,512]{1,0:T(8,128)(2,1)S(1)}, u32[]{:S(2)}, u32[]{:S(2)}) collective-permute-start(bf16[384,512]{1,0:T(8,128)(2,1)S(1)} %get-tuple-element.77), channel_id=1, source_target_pairs={{0,8},{8,0},{16,24},{24,16},{1,9},{9,1},{17,25},{25,17},{2,10},{10... | collective-permute-start | bytes 1179656 | tf_op jit(solution)/shard_map/ppermute | solution.py:230
  59.2 1.4 %collective-permute-start.14 = (bf16[128,512]{1,0:T(8,128)(2,1)S(1)}, bf16[128,512]{1,0:T(8,128)(2,1)S(1)}, u32[]{:S(2)}, u32[]{:S(2)}) collective-permute-start(bf16[128,512]{1,0:T(8,128)(2,1)S(1)} %get-tuple-element.80), channel_id=1, source_target_pairs={{0,8},{8,0},{16,24},{24,16},{1,9},{9,1},{17,25},{25,17},{2,10},{10... | collective-permute-start | bytes 393224 | tf_op jit(solution)/shard_map/ppermute | solution.py:230

commit v6 on v5

--- a/solution.py
+++ b/solution.py
@@ -61,7 +61,8 @@
         for j in range(block_rows + outer_ref.shape[1] // size):
             dense = jnp.zeros_like(blocks[0])
             for k in range(chosen):
-                dense = jnp.where(index_ref[b, k] == j, blocks[k], dense)
+                here = (index_ref[b : b + 1, k : k + 1] == j).astype(jnp.float32).astype(dense.dtype)
+                dense += here * blocks[k]
             if j < block_rows:
                 dense_ref[rows, j * size : (j + 1) * size] = dense
             else:
@@ -91,15 +92,19 @@
     return jnp.maximum(total, 0.0).astype(jnp.bfloat16)
 
 
-def assemble_kernel(base, meta_ref, *refs):
+def assemble_kernel(parts, *refs):
     *piece_refs, mine_ref, other_ref, weight_ref, hidden_ref, hidden_other_ref = refs
     _, depth, half = piece_refs[0].shape
-    at = base
+    core = lax.rem(lax.axis_index("tm"), CORES)
+    part = lax.axis_index("vert")
+    around = [lax.rem(part + (parts - 2 * d), parts) for d in range(parts // 2)]
+    origin = around + [i ^ 1 for i in around]
+    at = 0
     for first, second in zip(piece_refs[::2], piece_refs[1::2]):
         for i in range(first.shape[0]):
-            row = pl.ds(pl.multiple_of(meta_ref[at] * depth, depth), depth)
-            for ref, core in ((first, meta_ref[0]), (second, 1 - meta_ref[0])):
-                weight_ref[row, pl.ds(pl.multiple_of(core * half, half), half)] = ref[i]
+            row = pl.ds(pl.multiple_of(origin[at] * depth, depth), depth)
+            for ref, side in ((first, core), (second, 1 - core)):
+                weight_ref[row, pl.ds(pl.multiple_of(side * half, half), half)] = ref[i]
             at += 1
     hidden_ref[...] = relu_dot(mine_ref[...], weight_ref[...])
     hidden_other_ref[...] = relu_dot(other_ref[...], weight_ref[...])
@@ -114,10 +119,10 @@
             rows_ref[start : start + size, :] = heads_ref[h, i * size : (i + 1) * size, :]
 
 
-def own_kernel(meta_ref, mine_ref, other_ref, rows_ref, query_ref, both_ref, stacked_ref):
+def own_kernel(mine_ref, other_ref, rows_ref, query_ref, both_ref, stacked_ref):
     rows = mine_ref.shape[0]
     width = query_ref.shape[2]
-    core = meta_ref[0]
+    core = lax.rem(lax.axis_index("tm"), CORES)
     stacked_ref[:rows, :] = mine_ref[...]
     stacked_ref[rows:, :] = other_ref[...]
     packed = lax.dot_general(
@@ -129,15 +134,17 @@
         both_ref[slot] = part[:, width:]
 
 
-def arrange_own_kernel(meta_ref, mine_ref, other_ref, heads_ref, rows_ref, query_ref, both_ref, stacked_ref):
+def arrange_own_kernel(mine_ref, other_ref, heads_ref, rows_ref, query_ref, both_ref, stacked_ref):
     arrange_kernel(heads_ref, rows_ref)
-    own_kernel(meta_ref, mine_ref, other_ref, rows_ref, query_ref, both_ref, stacked_ref)
-
-
-def attend_kernel(lists, head_size, start, meta_ref, weight_ref, *refs):
+    own_kernel(mine_ref, other_ref, rows_ref, query_ref, both_ref, stacked_ref)
+
+
+def attend_kernel(lists, head_size, start, weight_ref, *refs):
     total = sum(lists)
     rows_refs, query_refs, both_refs = refs[:total], refs[total : 2 * total], refs[2 * total : 3 * total]
     *mixed_refs, mine_ref, other_ref, stacked_ref, attended_ref = refs[3 * total :]
+    core = lax.rem(lax.axis_index("tm"), CORES)
+    chip = lax.div(lax.axis_index("tm"), CORES)
     rows = mine_ref.shape[0]
     here = slice(start, start + rows)
     slot = lambda s: slice(s * rows, (s + 1) * rows)
@@ -177,19 +184,21 @@
                 scores *= scale
             parts = [scores[slot(u)] for u in range(slots)]
             for u in range(len(mixed_refs)):
-                parts[u] = jnp.where(meta_ref[1 + u // CORES] > 0, parts[u], MASKED)
+                parts[u] = jnp.where(chip >= 1 + u // CORES, parts[u], MASKED)
             top = functools.reduce(jnp.maximum, parts)
             parts = [jnp.exp(part - top) for part in parts]
             result = functools.reduce(jnp.add, [a * b for a, b in zip(parts, values)])
             result *= 1.0 / functools.reduce(jnp.add, parts)
             attended_ref[t, :, at : at + size] = result.astype(attended_ref.dtype)
         at += size
-    mine_ref[...] = attended_ref[meta_ref[0]]
-    other_ref[...] = attended_ref[1 - meta_ref[0]]
-
-
-def combine_kernel(blocks, pieces, base, meta_ref, hidden_ref, *refs):
+    mine_ref[...] = attended_ref[core]
+    other_ref[...] = attended_ref[1 - core]
+
+
+def combine_kernel(blocks, spots, hidden_ref, *refs):
     *refs, out_ref, sum_ref, sems = refs
+    spots = spots(lax.axis_index("tm"), lax.axis_index("vert"))
+    pieces = len(spots) // CORES
     width = refs[0].shape[1] // pieces
     lanes = width % LANES == 0
     step = math.gcd(*[ref.shape[0] for ref in refs])
@@ -202,7 +211,7 @@
             whole = None if lanes else hidden_ref[here, :].astype(jnp.float32)
             for half in range(CORES):
                 for p in range(pieces):
-                    start = meta_ref[base + half * pieces + p] * width
+                    start = spots[half * pieces + p] * width
                     attended = refs[half * blocks + r][rows, p * width : (p + 1) * width]
                     if lanes:
                         column = pl.ds(pl.multiple_of(start, width), width)
@@ -235,17 +244,14 @@
     shares = 2 if shared else 1
     share = (part >> 1) % shares
 
-    around = [(part - 2 * d) % parts for d in range(parts // 2)]
-    spots = [step * shares + i for i in range(shares)]
-    for d in range(1, chips):
-        block = (step - CORES * d) % steps * shares
-        spots += [block + share, block + 1 - share] if shared else [block]
-    meta = [core, *[chip >= d for d in range(1, chips)], *around, *[i ^ 1 for i in around]]
-    meta = jnp.stack([jnp.asarray(i, jnp.int32) for i in meta + spots + [i ^ shares for i in spots]])
-    arrays = (features, graph_weight, head_weight, send_rows, send_count, block_index, block_values)
-    (features, graph_weight, head_weight, send_rows, send_count, block_index, block_values), meta = (
-        lax.optimization_barrier((arrays, meta))
-    )
+    def spots(step, part):
+        share = lax.rem(lax.div(part, 2), shares)
+        places = [step * shares + i for i in range(shares)]
+        for d in range(1, chips):
+            block = lax.rem(step + (steps - CORES * d), steps) * shares
+            places += [block + share, block + 1 - share] if shared else [block]
+        return places + [i ^ shares for i in places]
+
     inputs = features[0]
     own, width = inputs.shape
 
@@ -259,7 +265,7 @@
     slots = jnp.where(live, rows_list, -1).reshape(1, -1)
     picked = call(
         pick_kernel, shaped(sources * most_rows, width), (slots, inputs),
-        specs=[VMEM, VMEM], flops=2 * own * width * sources * most_rows,
+        specs=[VMEM, VMEM], grid=(), flops=2 * own * width * sources * most_rows,
     )
     arrived = lax.all_to_all(
         picked.reshape(sources, most_rows, width), "vert", split_axis=0, concat_axis=0, tiled=True
@@ -283,6 +289,7 @@
         mix_kernel,
         (*[shaped(b - a, width) for a, b in zip(cuts, cuts[1:])], shaped(own, width)),
         (block_index[0], inputs, block_values[0].transpose(1, 0, 2), arrived),
+        specs=[VMEM] * 4, grid=(),
         scratch=[pltpu.VMEM((own, own), jnp.bfloat16), pltpu.VMEM((own, outer_size), jnp.bfloat16)],
     )
     lower = [
@@ -296,10 +303,10 @@
     across = after(across, arranged)
     groups = [[group, swap_part(group, 2)] if shared else [group] for group in fetched]
     weight, hidden, sibling = call(
-        functools.partial(assemble_kernel, chips),
+        functools.partial(assemble_kernel, parts),
         (shaped(width, width), shaped(own, width), shaped(own, width)),
         (
-            meta, around, swap_core(around), across, swap_core(across), mixed, swap_core(mixed),
+            around, swap_core(around), across, swap_core(across), mixed, swap_core(mixed),
         ),
         flops=4 * own * width * width,
     )
@@ -312,7 +319,7 @@
         result = call(
             own_kernel if ready else arrange_own_kernel,
             outs,
-            (meta, hidden, sibling, weights),
+            (hidden, sibling, weights),
             seconds=seconds,
             scratch=[pltpu.VMEM((CORES * own, width), jnp.bfloat16)],
         )
@@ -337,7 +344,7 @@
         keep, send = token = call(
             functools.partial(attend_kernel, lists, head_size, cuts[r]),
             (shaped(rows, total), shaped(rows, total)),
-            (meta, weight, *[a[i] for i in range(3) for a in owned], *mixed_rows),
+            (weight, *[a[i] for i in range(3) for a in owned], *mixed_rows),
             limit=11 + len(mixed_rows) * rows * width // 2**17,
             flops=2 * len(mixed_rows) * rows * width * (2 * total + width),
             scratch=[
@@ -348,9 +355,9 @@
         kept.append(keep)
         got.append(swap_core(send))
     combined = call(
-        functools.partial(combine_kernel, blocks, len(spots), meta.size - 2 * len(spots)),
+        functools.partial(combine_kernel, blocks, spots),
         shaped(own, width),
-        (meta, hidden, *kept, *got),
+        (hidden, *kept, *got),
         out_specs=ANY,
         scratch=[
             pltpu.VMEM((own, width), jnp.bfloat16),

time: 62.6 us -> 60.9 us (0.973)
  Pallas kernels: 24.9 us -> 21.7 us
  waiting for transfers between devices: 16.9 us -> 18.4 us
    pallas_call x11, Pallas kernels: 24.9 us -> 21.7 us  [call(): pl.pallas_call(kernel, out_shape=outs, grid=(1,) if specs and grid is Non...]
  transfers between devices with their start and end apart: 16 -> 16, of which waited for: 8 -> 9; matrix products, arithmetic and copies ran while one was open for 4% -> 4% of each run, Pallas kernels for 37% -> 34%
where the time goes in v6:
time: 60.9 us; the launch traced here: 60.5 us
  Pallas kernels  21.7 us (36%)
  waiting for transfers between devices  18.4 us (30%)
  starting transfers between devices  17 us (28%)
  local copies, waits for them, and re-layouts  3.3 us (5%)
    pallas_call x11, Pallas kernels, call(): pl.pallas_call(kernel, out_shape=outs, grid=(1,) if specs and grid is Non...  21.7 us
    ppermute x6, starting transfers between devices, shards(): lax.ppermute(a, axis, [(i, (i + by) % n) for i in range(n)])  10 us
    ppermute x6, waiting for transfers between devices, shards(): lax.ppermute(a, axis, [(i, (i + by) % n) for i in range(n)])  5.57 us
    all_to_all x1, waiting for transfers between devices, shards(): lax.all_to_all(picked.reshape(sources, most_rows, width), 'vert', split_a...  4.6 us
    ppermute x7, waiting for transfers between devices, shards(): lax.ppermute(a, 'tm', [(i, i ^ 1) for i in range(steps)])  4.46 us
    ppermute x2, waiting for transfers between devices, shards(): lax.ppermute(a, 'vert', [(i, i ^ bit) for i in range(parts)])  3.75 us
    all_to_all x1, starting transfers between devices, shards(): lax.all_to_all(picked.reshape(sources, most_rows, width), 'vert', split_a...  3.41 us
    ppermute x2, starting transfers between devices, shards(): lax.ppermute(a, 'vert', [(i, i ^ bit) for i in range(parts)])  2.65 us
  transfers between devices with their start and end apart: 16, of which 9 were waited for; matrix products, arithmetic and copies ran while one was open for 4% of the time, Pallas kernels for 34%

profile of v6, /device:TPU:0, one launch (start us, length us, event | category | flops | bytes accessed | tf_op | source)
XLA Modules:
  0.0 60.5 jit_solution(1284639506868242585)
XLA Ops:
  0.0 0.9 %copy-done = bf16[128,1024]{1,0:T(8,128)(2,1)S(1)} copy-done((bf16[128,1024]{1,0:T(8,128)(2,1)S(1)}, bf16[128,1024]{1,0:T(8,128)(2,1)}, u32[]{:S(2)}) %copy-start) | copy-done | bytes 262168
  1.0 3.1 %collective-permute-start = (bf16[128,512]{1,0:T(8,128)(2,1)S(1)}, bf16[128,512]{1,0:T(8,128)(2,1)S(1)}, u32[]{:S(2)}, u32[]{:S(2)}) collective-permute-start(bf16[128,512]{1,0:T(8,128)(2,1)S(1)} %constant_dynamic-slice_fusion.1.refs_0_), channel_id=1, source_target_pairs={{0,2},{1,3},{2,4},{3,5},{4,6},{5,7},{6,0},{7,1},{8,10},{9,11},{10,... | collective-permute-start | bytes 393224 | tf_op jit(solution)/shard_map/ppermute | solution.py:241
  4.0 2.6 %collective-permute-start.1 = (bf16[128,512]{1,0:T(8,128)(2,1)S(1)}, bf16[128,512]{1,0:T(8,128)(2,1)S(1)}, u32[]{:S(2)}, u32[]{:S(2)}) collective-permute-start(bf16[128,512]{1,0:T(8,128)(2,1)S(1)} %constant_dynamic-slice_fusion.1.refs_0_), channel_id=1, source_target_pairs={{0,4},{1,5},{2,6},{3,7},{4,0},{5,1},{6,2},{7,3},{8,12},{9,13},{10,... | collective-permute-start | bytes 393224 | tf_op jit(solution)/shard_map/ppermute | solution.py:241
  6.6 1.3 %collective-permute-start.2 = (bf16[128,512]{1,0:T(8,128)(2,1)S(1)}, bf16[128,512]{1,0:T(8,128)(2,1)S(1)}, u32[]{:S(2)}, u32[]{:S(2)}) collective-permute-start(bf16[128,512]{1,0:T(8,128)(2,1)S(1)} %constant_dynamic-slice_fusion.1.refs_0_), channel_id=1, source_target_pairs={{0,6},{1,7},{2,0},{3,1},{4,2},{5,3},{6,4},{7,5},{8,14},{9,15},{10,... | collective-permute-start | bytes 393224 | tf_op jit(solution)/shard_map/ppermute | solution.py:241
  8.0 2.1 %constant_dynamic-slice_fusion = bf16[2,192,1024]{2,1,0:T(8,128)(2,1)} fusion(bf16[4,192,1024]{2,1,0:T(8,128)(2,1)} %heads_ref, s32[]{:T(128)S(6)} %select_n.32), kind=kLoop, calls=%fused_computation.1 | loop fusion | bytes 1572868 | tf_op jit(solution)/shard_map/dynamic_slice | solution.py:259
  10.1 1.5 %collective-permute-start.7 = (bf16[2,192,1024]{2,1,0:T(8,128)(2,1)}, bf16[2,192,1024]{2,1,0:T(8,128)(2,1)}, u32[]{:S(2)}, u32[]{:S(2)}) collective-permute-start(bf16[2,192,1024]{2,1,0:T(8,128)(2,1)} %constant_dynamic-slice_fusion), channel_id=1, source_target_pairs={{0,16},{8,24},{16,0},{24,8},{1,17},{9,25},{17,1},{25,9},{2,18},{10... | collective-permute-start | bytes 2359304 | tf_op jit(solution)/shard_map/ppermute | solution.py:241
  11.6 0.1 iota_compare_fusion
  11.7 0.1 lt.47
  11.7 0.1 squeeze.15
  11.8 1.1 %shard_map.74 = bf16[128,1024]{1,0:T(8,128)(2,1)} custom-call(s32[1,128]{1,0:T(1,128)S(1)} %broadcast_select_fusion.row_ref, bf16[512,1024]{1,0:T(8,128)(2,1)S(1)} %bitcast.11), custom_call_target="tpu_custom_call" | custom-call | tf_op jit(solution)/shard_map/pallas_call | solution.py:24
  12.9 3.4 %all-to-all-start = ((bf16[8,16,1024]{2,1,0:T(8,128)(2,1)}), bf16[8,16,1024]{2,1,0:T(8,128)(2,1)S(1)}, u32[]{:S(2)}, u32[]{:S(2)}) async-start(bf16[8,16,1024]{2,1,0:T(8,128)(2,1)} %bitcast.5), calls=%async_computation | async-start | bytes 524288 | tf_op jit(solution)/shard_map/all_to_all | solution.py:270
  16.3 0.1 copy.8
  16.4 0.0 collective-permute-done.refs_1_
  16.4 0.0 collective-permute-done.1.refs_2_
  16.4 0.0 collective-permute-done.2.refs_3_
  16.4 1.6 %shard_map.73.refs_0_ = bf16[4,128,512]{2,1,0:T(8,128)(2,1)} custom-call(bf16[128,512]{1,0:T(8,128)(2,1)S(1)} %constant_dynamic-slice_fusion.1.refs_0_, bf16[128,512]{1,0:T(8,128)(2,1)S(1)} %collective-permute-done.refs_1_, bf16[128,512]{1,0:T(8,128)(2,1)S(1)} %collective-permute-done.1.refs_2_, bf16[128,512]{1,0:T(8,128)(2,1)S(1)} %collective-permute-done.2.refs_3_), custom_call_target="tpu_custom_call" | custom-call | flops 4000000000 | tf_op jit(solution)/shard_map/pallas_call | solution.py:24
  18.0 0.0 copy-start.2
  18.0 2.0 %collective-permute-start.4 = (bf16[4,128,512]{2,1,0:T(8,128)(2,1)}, bf16[4,128,512]{2,1,0:T(8,128)(2,1)}, u32[]{:S(2)}, u32[]{:S(2)}) collective-permute-start(bf16[4,128,512]{2,1,0:T(8,128)(2,1)} %shard_map.73.refs_0_), channel_id=1, source_target_pairs={{0,1},{1,0},{2,3},{3,2},{4,5},{5,4},{6,7},{7,6},{8,9},{9,8},{10,11... | collective-permute-start | bytes 1572872 | tf_op jit(solution)/shard_map/ppermute | solution.py:240
  20.0 4.6 %all-to-all-done = bf16[8,16,1024]{2,1,0:T(8,128)(2,1)S(1)} async-done(((bf16[8,16,1024]{2,1,0:T(8,128)(2,1)}), bf16[8,16,1024]{2,1,0:T(8,128)(2,1)S(1)}, u32[]{:S(2)}, u32[]{:S(2)}) %all-to-all-start) | async-done | bytes 262176 | tf_op jit(solution)/shard_map/all_to_all | solution.py:270
  24.6 1.1 %shard_map.75 = (bf16[384,1024]{1,0:T(8,128)(2,1)S(1)}, bf16[128,1024]{1,0:T(8,128)(2,1)S(1)}, bf16[512,1024]{1,0:T(8,128)(2,1)S(1)}) custom-call(s32[4,3]{1,0:T(4,128)S(1)} %bitcast.15, bf16[512,1024]{1,0:T(8,128)(2,1)S(1)} %bitcast.12, bf16[3,512,128]{2,1,0:T(8,128)(2,1)S(1)} %bitcast.14, bf16[128,1024]{1,0:T(8,128)(2,1)S(1)} %bitcast.13), custom_call_target="tpu_custom_call" | custom-call | tf_op jit(solution)/shard_map/pallas_call | solution.py:24
  25.7 0.1 collective-permute-start.6
  25.8 0.6 %collective-permute-start.8 = (bf16[384,1024]{1,0:T(8,128)(2,1)S(1)}, bf16[384,1024]{1,0:T(8,128)(2,1)S(1)}, u32[]{:S(2)}, u32[]{:S(2)}) collective-permute-start(bf16[384,1024]{1,0:T(8,128)(2,1)S(1)} %get-tuple-element.46), channel_id=1, source_target_pairs={{0,16},{8,24},{16,0},{24,8},{1,17},{9,25},{17,1},{25,9},{2,18},{10... | collective-permute-start | bytes 2359304 | tf_op jit(solution)/shard_map/ppermute | solution.py:241
  26.4 2.4 %collective-permute-done.7.heads_ref = bf16[2,192,1024]{2,1,0:T(8,128)(2,1)} collective-permute-done((bf16[2,192,1024]{2,1,0:T(8,128)(2,1)}, bf16[2,192,1024]{2,1,0:T(8,128)(2,1)}, u32[]{:S(2)}, u32[]{:S(2)}) %collective-permute-start.7) | collective-permute-done | bytes 786464 | tf_op jit(solution)/shard_map/ppermute | solution.py:241
  28.8 0.7 %collective-permute-start.9 = (bf16[2,192,1024]{2,1,0:T(8,128)(2,1)}, bf16[2,192,1024]{2,1,0:T(8,128)(2,1)S(1)}, u32[]{:S(2)}, u32[]{:S(2)}) collective-permute-start(bf16[2,192,1024]{2,1,0:T(8,128)(2,1)} %collective-permute-done.7.heads_ref), channel_id=1, source_target_pairs={{0,2},{1,3},{2,0},{3,1},{4,6},{5,7},{6,4},{7,5},{8,10},{9,11},{10,... | collective-permute-start | bytes 2359304 | tf_op jit(solution)/shard_map/ppermute | solution.py:240
  29.5 0.0 collective-permute-start.3
  29.5 0.1 shard_map.76.rows_ref.refs_0_
  29.6 3.4 %collective-permute-done.4.refs_2_ = bf16[4,128,512]{2,1,0:T(8,128)(2,1)} collective-permute-done((bf16[4,128,512]{2,1,0:T(8,128)(2,1)}, bf16[4,128,512]{2,1,0:T(8,128)(2,1)}, u32[]{:S(2)}, u32[]{:S(2)}) %collective-permute-start.4) | collective-permute-done | bytes 524320 | tf_op jit(solution)/shard_map/ppermute | solution.py:240
  33.0 0.0 collective-permute-done.3.refs_1_
  33.0 0.9 %collective-permute-start.11 = (bf16[128,1024]{1,0:T(8,128)(2,1)S(1)}, bf16[128,1024]{1,0:T(8,128)(2,1)S(1)}, u32[]{:S(2)}, u32[]{:S(2)}) collective-permute-start(bf16[128,1024]{1,0:T(8,128)(2,1)S(1)} %get-tuple-element.60), channel_id=1, source_target_pairs={{0,16},{8,24},{16,0},{24,8},{1,17},{9,25},{17,1},{25,9},{2,18},{10... | collective-permute-start | bytes 786440 | tf_op jit(solution)/shard_map/ppermute | solution.py:241
  33.9 1.2 %collective-permute-done.5.refs_3_ = bf16[4,128,512]{2,1,0:T(8,128)(2,1)S(1)} collective-permute-done((bf16[4,128,512]{2,1,0:T(8,128)(2,1)}, bf16[4,128,512]{2,1,0:T(8,128)(2,1)S(1)}, u32[]{:S(2)}, u32[]{:S(2)}) %collective-permute-start.5) | collective-permute-done | bytes 524320 | tf_op jit(solution)/shard_map/ppermute | solution.py:239
  35.1 0.0 collective-permute-done.6.refs_5_
  35.1 3.7 %shard_map.77 = (bf16[1024,1024]{1,0:T(8,128)(2,1)S(1)}, bf16[512,1024]{1,0:T(8,128)(2,1)S(1)}, bf16[512,1024]{1,0:T(8,128)(2,1)S(1)}) custom-call(bf16[4,128,512]{2,1,0:T(8,128)(2,1)} %shard_map.73.refs_0_, bf16[4,128,512]{2,1,0:T(8,128)(2,1)S(1)} %collective-permute-done.3.refs_1_, bf16[4,128,512]{2,1,0:T(8,128)(2,1)} %collective-permute-done.4.refs_2_, ...), custom_call_target="tpu_custom_call" | custom-call | tf_op jit(solution)/shard_map/pallas_call | solution.py:24
  38.8 1.8 %shard_map.78 = (bf16[2,512,256]{2,1,0:T(8,128)(2,1)S(1)}, bf16[2,512,512]{2,1,0:T(8,128)(2,1)S(1)}) custom-call(bf16[512,1024]{1,0:T(8,128)(2,1)S(1)} %get-tuple-element.38.mine_ref.hidden_ref, bf16[512,1024]{1,0:T(8,128)(2,1)S(1)} %get-tuple-element.40.other_ref, bf16[768,1024]{1,0:T(8,128)(2,1)S(1)} %shard_map.76.rows_ref.refs_0_), custom_call_target="tpu_custom_call" | custom-call | tf_op jit(solution)/shard_map/pallas_call | solution.py:24
  40.6 2.4 %shard_map.79 = (bf16[384,1024]{1,0:T(8,128)(2,1)S(1)}, bf16[2,512,128]{2,1,0:T(8,128)(2,1)S(1)}, bf16[2,512,256]{2,1,0:T(8,128)(2,1)S(1)}) custom-call(bf16[512,1024]{1,0:T(8,128)(2,1)S(1)} %get-tuple-element.38.mine_ref.hidden_ref, bf16[512,1024]{1,0:T(8,128)(2,1)S(1)} %get-tuple-element.40.other_ref, bf16[2,192,1024]{2,1,0:T(8,128)(2,1)} %collective-permute-done.7.heads_ref), custom_call_target="tpu_custom_call" | custom-call | tf_op jit(solution)/shard_map/pallas_call | solution.py:24
  43.1 3.1 %collective-permute-done.8.refs_9_ = bf16[384,1024]{1,0:T(8,128)(2,1)S(1)} collective-permute-done((bf16[384,1024]{1,0:T(8,128)(2,1)S(1)}, bf16[384,1024]{1,0:T(8,128)(2,1)S(1)}, u32[]{:S(2)}, u32[]{:S(2)}) %collective-permute-start.8) | collective-permute-done | bytes 786464 | tf_op jit(solution)/shard_map/ppermute | solution.py:241
  46.2 0.4 collective-permute-done.9.heads_ref
  46.5 0.0 collective-permute-start.10
  46.5 1.3 %shard_map.80 = (bf16[384,1024]{1,0:T(8,128)(2,1)S(1)}, bf16[2,512,128]{2,1,0:T(8,128)(2,1)S(1)}, bf16[2,512,256]{2,1,0:T(8,128)(2,1)S(1)}) custom-call(bf16[512,1024]{1,0:T(8,128)(2,1)S(1)} %get-tuple-element.38.mine_ref.hidden_ref, bf16[512,1024]{1,0:T(8,128)(2,1)S(1)} %get-tuple-element.40.other_ref, ...), custom_call_target="tpu_custom_call" | custom-call | flops 12000000000 | tf_op jit(solution)/shard_map/pallas_call | solution.py:24
  47.8 1.0 %collective-permute-done.10.refs_10_ = bf16[384,1024]{1,0:T(8,128)(2,1)S(1)} collective-permute-done((bf16[384,1024]{1,0:T(8,128)(2,1)S(1)}, bf16[384,1024]{1,0:T(8,128)(2,1)S(1)}, u32[]{:S(2)}, u32[]{:S(2)}) %collective-permute-start.10) | collective-permute-done | bytes 786464 | tf_op jit(solution)/shard_map/ppermute | solution.py:239
  48.8 5.5 %shard_map.81 = (bf16[384,512]{1,0:T(8,128)(2,1)S(1)}, bf16[384,512]{1,0:T(8,128)(2,1)S(1)}) custom-call(bf16[1024,1024]{1,0:T(8,128)(2,1)S(1)} %get-tuple-element.39.weight_ref, bf16[768,1024]{1,0:T(8,128)(2,1)S(1)} %shard_map.76.rows_ref.refs_0_, bf16[384,1024]{1,0:T(8,128)(2,1)S(1)} %get-tuple-element.48.refs_1_, ...), custom_call_target="tpu_custom_call" | custom-call | tf_op jit(solution)/shard_map/pallas_call | solution.py:24
  54.3 0.0 collective-permute-done.11.refs_9_
  54.3 0.2 collective-permute-start.12
  54.5 0.4 collective-permute-start.13
  54.9 1.0 %collective-permute-done.12.refs_10_ = bf16[128,1024]{1,0:T(8,128)(2,1)S(1)} collective-permute-done((bf16[128,1024]{1,0:T(8,128)(2,1)S(1)}, bf16[128,1024]{1,0:T(8,128)(2,1)S(1)}, u32[]{:S(2)}, u32[]{:S(2)}) %collective-permute-start.12) | collective-permute-done | bytes 262176 | tf_op jit(solution)/shard_map/ppermute | solution.py:239
  55.9 2.1 %shard_map.82 = (bf16[128,512]{1,0:T(8,128)(2,1)S(1)}, bf16[128,512]{1,0:T(8,128)(2,1)S(1)}) custom-call(bf16[1024,1024]{1,0:T(8,128)(2,1)S(1)} %get-tuple-element.39.weight_ref, bf16[768,1024]{1,0:T(8,128)(2,1)S(1)} %shard_map.76.rows_ref.refs_0_, bf16[384,1024]{1,0:T(8,128)(2,1)S(1)} %get-tuple-element.48.refs_1_, ...), custom_call_target="tpu_custom_call" | custom-call | tf_op jit(solution)/shard_map/pallas_call | solution.py:24
  58.0 0.2 collective-permute-start.14
  58.3 1.2 %collective-permute-done.14.refs_3_ = bf16[128,512]{1,0:T(8,128)(2,1)S(1)} collective-permute-done((bf16[128,512]{1,0:T(8,128)(2,1)S(1)}, bf16[128,512]{1,0:T(8,128)(2,1)S(1)}, u32[]{:S(2)}, u32[]{:S(2)}) %collective-permute-start.14) | collective-permute-done | bytes 131104 | tf_op jit(solution)/shard_map/ppermute | solution.py:239
  59.5 1.1 %shard_map.83 = bf16[512,1024]{1,0:T(8,128)(2,1)} custom-call(bf16[512,1024]{1,0:T(8,128)(2,1)S(1)} %get-tuple-element.38.mine_ref.hidden_ref, bf16[384,512]{1,0:T(8,128)(2,1)S(1)} %get-tuple-element.59.refs_0_, bf16[128,512]{1,0:T(8,128)(2,1)S(1)} %get-tuple-element.63.refs_1_, bf16[384,512]{1,0:T(8,128)(2,1)S(1)} %collective-permute-done.13.refs_2_, ...), custom_call_target="tpu_custom_call" | custom-call | tf_op jit(solution)/shard_map/pallas_call | solution.py:24
  (16 shorter events, 0.0 us)
Async XLA Ops:
  0.0 1.0 %copy-start = (bf16[128,1024]{1,0:T(8,128)(2,1)S(1)}, bf16[128,1024]{1,0:T(8,128)(2,1)}, u32[]{:S(2)}) copy-start(bf16[128,1024]{1,0:T(8,128)(2,1)} %param.8) | copy-start | bytes 786436
  0.0 11.6 %copy-start.6 = (s32[1,1,8]{2,1,0:T(1,128)S(1)}, s32[1,1,8]{2,1,0:T(1,128)}, u32[]{:S(2)}) copy-start(s32[1,1,8]{2,1,0:T(1,128)} %param.11) | copy-start | bytes 100
  0.0 11.7 %copy-start.4 = (s32[1,1,8,16]{3,2,1,0:T(8,128)S(1)}, s32[1,1,8,16]{3,2,1,0:T(8,128)}, u32[]{:S(2)}) copy-start(s32[1,1,8,16]{3,2,1,0:T(8,128)} %param.10) | copy-start | bytes 1540
  0.0 11.8 %copy-start.1 = (bf16[1,512,1024]{2,1,0:T(8,128)(2,1)S(1)}, bf16[1,512,1024]{2,1,0:T(8,128)(2,1)}, u32[]{:S(2)}) copy-start(bf16[1,512,1024]{2,1,0:T(8,128)(2,1)} %param.7) | copy-start | bytes 3145732
  1.0 15.5 %collective-permute-start = (bf16[128,512]{1,0:T(8,128)(2,1)S(1)}, bf16[128,512]{1,0:T(8,128)(2,1)S(1)}, u32[]{:S(2)}, u32[]{:S(2)}) collective-permute-start(bf16[128,512]{1,0:T(8,128)(2,1)S(1)} %constant_dynamic-slice_fusion.1.refs_0_), channel_id=1, source_target_pairs={{0,2},{1,3},{2,4},{3,5},{4,6},{5,7},{6,0},{7,1},{8,10},{9,11},{10,... | collective-permute-start | bytes 393224 | tf_op jit(solution)/shard_map/ppermute | solution.py:241
  4.0 12.4 %collective-permute-start.1 = (bf16[128,512]{1,0:T(8,128)(2,1)S(1)}, bf16[128,512]{1,0:T(8,128)(2,1)S(1)}, u32[]{:S(2)}, u32[]{:S(2)}) collective-permute-start(bf16[128,512]{1,0:T(8,128)(2,1)S(1)} %constant_dynamic-slice_fusion.1.refs_0_), channel_id=1, source_target_pairs={{0,4},{1,5},{2,6},{3,7},{4,0},{5,1},{6,2},{7,3},{8,12},{9,13},{10,... | collective-permute-start | bytes 393224 | tf_op jit(solution)/shard_map/ppermute | solution.py:241
  6.6 9.8 %collective-permute-start.2 = (bf16[128,512]{1,0:T(8,128)(2,1)S(1)}, bf16[128,512]{1,0:T(8,128)(2,1)S(1)}, u32[]{:S(2)}, u32[]{:S(2)}) collective-permute-start(bf16[128,512]{1,0:T(8,128)(2,1)S(1)} %constant_dynamic-slice_fusion.1.refs_0_), channel_id=1, source_target_pairs={{0,6},{1,7},{2,0},{3,1},{4,2},{5,3},{6,4},{7,5},{8,14},{9,15},{10,... | collective-permute-start | bytes 393224 | tf_op jit(solution)/shard_map/ppermute | solution.py:241
  8.0 8.3 %copy-start.5 = (s32[1,4,3]{1,0,2:T(1,128)S(1)}, s32[1,4,3]{1,0,2:T(1,128)}, u32[]{:S(2)}) copy-start(s32[1,4,3]{1,0,2:T(1,128)} %param.12) | copy-start | bytes 148
  10.1 18.8 %collective-permute-start.7 = (bf16[2,192,1024]{2,1,0:T(8,128)(2,1)}, bf16[2,192,1024]{2,1,0:T(8,128)(2,1)}, u32[]{:S(2)}, u32[]{:S(2)}) collective-permute-start(bf16[2,192,1024]{2,1,0:T(8,128)(2,1)} %constant_dynamic-slice_fusion), channel_id=1, source_target_pairs={{0,16},{8,24},{16,0},{24,8},{1,17},{9,25},{17,1},{25,9},{2,18},{10... | collective-permute-start | bytes 2359304 | tf_op jit(solution)/shard_map/ppermute | solution.py:241
  12.9 11.7 %all-to-all-start = ((bf16[8,16,1024]{2,1,0:T(8,128)(2,1)}), bf16[8,16,1024]{2,1,0:T(8,128)(2,1)S(1)}, u32[]{:S(2)}, u32[]{:S(2)}) async-start(bf16[8,16,1024]{2,1,0:T(8,128)(2,1)} %bitcast.5), calls=%async_computation | async-start | bytes 524288 | tf_op jit(solution)/shard_map/all_to_all | solution.py:270
  16.4 8.2 %copy-start.3 = (bf16[1,512,3,128]{3,1,2,0:T(8,128)(2,1)S(1)}, bf16[1,512,3,128]{3,1,2,0:T(8,128)(2,1)}, u32[]{:S(2)}) copy-start(bf16[1,512,3,128]{3,1,2,0:T(8,128)(2,1)} %param.13) | copy-start | bytes 1179652
  18.0 11.5 %copy-start.2 = (bf16[4,192,1024]{2,1,0:T(8,128)(2,1)S(1)}, bf16[4,192,1024]{2,1,0:T(8,128)(2,1)}, u32[]{:S(2)}) copy-start(bf16[4,192,1024]{2,1,0:T(8,128)(2,1)} %heads_ref) | copy-start | bytes 4718596
  18.0 15.0 %collective-permute-start.4 = (bf16[4,128,512]{2,1,0:T(8,128)(2,1)}, bf16[4,128,512]{2,1,0:T(8,128)(2,1)}, u32[]{:S(2)}, u32[]{:S(2)}) collective-permute-start(bf16[4,128,512]{2,1,0:T(8,128)(2,1)} %shard_map.73.refs_0_), channel_id=1, source_target_pairs={{0,1},{1,0},{2,3},{3,2},{4,5},{5,4},{6,7},{7,6},{8,9},{9,8},{10,11... | collective-permute-start | bytes 1572872 | tf_op jit(solution)/shard_map/ppermute | solution.py:240
  25.7 9.4 %collective-permute-start.6 = (bf16[512,1024]{1,0:T(8,128)(2,1)S(1)}, bf16[512,1024]{1,0:T(8,128)(2,1)S(1)}, u32[]{:S(2)}, u32[]{:S(2)}) collective-permute-start(bf16[512,1024]{1,0:T(8,128)(2,1)S(1)} %get-tuple-element.35.refs_4_), channel_id=1, source_target_pairs={{0,8},{8,0},{16,24},{24,16},{1,9},{9,1},{17,25},{25,17},{2,10},{10... | collective-permute-start | bytes 3145736 | tf_op jit(solution)/shard_map/ppermute | solution.py:239
  25.8 20.4 %collective-permute-start.8 = (bf16[384,1024]{1,0:T(8,128)(2,1)S(1)}, bf16[384,1024]{1,0:T(8,128)(2,1)S(1)}, u32[]{:S(2)}, u32[]{:S(2)}) collective-permute-start(bf16[384,1024]{1,0:T(8,128)(2,1)S(1)} %get-tuple-element.46), channel_id=1, source_target_pairs={{0,16},{8,24},{16,0},{24,8},{1,17},{9,25},{17,1},{25,9},{2,18},{10... | collective-permute-start | bytes 2359304 | tf_op jit(solution)/shard_map/ppermute | solution.py:241
  28.8 17.7 %collective-permute-start.9 = (bf16[2,192,1024]{2,1,0:T(8,128)(2,1)}, bf16[2,192,1024]{2,1,0:T(8,128)(2,1)S(1)}, u32[]{:S(2)}, u32[]{:S(2)}) collective-permute-start(bf16[2,192,1024]{2,1,0:T(8,128)(2,1)} %collective-permute-done.7.heads_ref), channel_id=1, source_target_pairs={{0,2},{1,3},{2,0},{3,1},{4,6},{5,7},{6,4},{7,5},{8,10},{9,11},{10,... | collective-permute-start | bytes 2359304 | tf_op jit(solution)/shard_map/ppermute | solution.py:240
  29.5 3.5 %collective-permute-start.3 = (bf16[4,128,512]{2,1,0:T(8,128)(2,1)}, bf16[4,128,512]{2,1,0:T(8,128)(2,1)S(1)}, u32[]{:S(2)}, u32[]{:S(2)}) collective-permute-start(bf16[4,128,512]{2,1,0:T(8,128)(2,1)} %shard_map.73.refs_0_), channel_id=1, source_target_pairs={{0,8},{8,0},{16,24},{24,16},{1,9},{9,1},{17,25},{25,17},{2,10},{10... | collective-permute-start | bytes 1572872 | tf_op jit(solution)/shard_map/ppermute | solution.py:239
  33.0 2.1 %collective-permute-start.5 = (bf16[4,128,512]{2,1,0:T(8,128)(2,1)}, bf16[4,128,512]{2,1,0:T(8,128)(2,1)S(1)}, u32[]{:S(2)}, u32[]{:S(2)}) collective-permute-start(bf16[4,128,512]{2,1,0:T(8,128)(2,1)} %collective-permute-done.4.refs_2_), channel_id=1, source_target_pairs={{0,8},{8,0},{16,24},{24,16},{1,9},{9,1},{17,25},{25,17},{2,10},{10... | collective-permute-start | bytes 1572872 | tf_op jit(solution)/shard_map/ppermute | solution.py:239
  33.0 21.3 %collective-permute-start.11 = (bf16[128,1024]{1,0:T(8,128)(2,1)S(1)}, bf16[128,1024]{1,0:T(8,128)(2,1)S(1)}, u32[]{:S(2)}, u32[]{:S(2)}) collective-permute-start(bf16[128,1024]{1,0:T(8,128)(2,1)S(1)} %get-tuple-element.60), channel_id=1, source_target_pairs={{0,16},{8,24},{16,0},{24,8},{1,17},{9,25},{17,1},{25,9},{2,18},{10... | collective-permute-start | bytes 786440 | tf_op jit(solution)/shard_map/ppermute | solution.py:241
  46.5 2.3 %collective-permute-start.10 = (bf16[384,1024]{1,0:T(8,128)(2,1)S(1)}, bf16[384,1024]{1,0:T(8,128)(2,1)S(1)}, u32[]{:S(2)}, u32[]{:S(2)}) collective-permute-start(bf16[384,1024]{1,0:T(8,128)(2,1)S(1)} %collective-permute-done.8.refs_9_), channel_id=1, source_target_pairs={{0,8},{8,0},{16,24},{24,16},{1,9},{9,1},{17,25},{25,17},{2,10},{10... | collective-permute-start | bytes 2359304 | tf_op jit(solution)/shard_map/ppermute | solution.py:239
  54.3 1.6 %collective-permute-start.12 = (bf16[128,1024]{1,0:T(8,128)(2,1)S(1)}, bf16[128,1024]{1,0:T(8,128)(2,1)S(1)}, u32[]{:S(2)}, u32[]{:S(2)}) collective-permute-start(bf16[128,1024]{1,0:T(8,128)(2,1)S(1)} %collective-permute-done.11.refs_9_), channel_id=1, source_target_pairs={{0,8},{8,0},{16,24},{24,16},{1,9},{9,1},{17,25},{25,17},{2,10},{10... | collective-permute-start | bytes 786440 | tf_op jit(solution)/shard_map/ppermute | solution.py:239
  54.5 3.7 %collective-permute-start.13 = (bf16[384,512]{1,0:T(8,128)(2,1)S(1)}, bf16[384,512]{1,0:T(8,128)(2,1)S(1)}, u32[]{:S(2)}, u32[]{:S(2)}) collective-permute-start(bf16[384,512]{1,0:T(8,128)(2,1)S(1)} %get-tuple-element.61), channel_id=1, source_target_pairs={{0,8},{8,0},{16,24},{24,16},{1,9},{9,1},{17,25},{25,17},{2,10},{10... | collective-permute-start | bytes 1179656 | tf_op jit(solution)/shard_map/ppermute | solution.py:239
  58.0 1.4 %collective-permute-start.14 = (bf16[128,512]{1,0:T(8,128)(2,1)S(1)}, bf16[128,512]{1,0:T(8,128)(2,1)S(1)}, u32[]{:S(2)}, u32[]{:S(2)}) collective-permute-start(bf16[128,512]{1,0:T(8,128)(2,1)S(1)} %get-tuple-element.64), channel_id=1, source_target_pairs={{0,8},{8,0},{16,24},{24,16},{1,9},{9,1},{17,25},{25,17},{2,10},{10... | collective-permute-start | bytes 393224 | tf_op jit(solution)/shard_map/ppermute | solution.py:239
